TPU v7x, 256 devices: a whole 4x4x8 slice. The times are simulated.
256 devices in a mesh: dp: 64 (over x, z_lo, y, core), mp: 4 (over z_hi).
Axes of the slice: x: 4, y: 4, z: 8 (z_hi: 4, z_lo: 2; z = z_hi * 2 + z_lo), core: 2. Of those that a mesh axis runs over, the one named last changes fastest.
Arguments:
- train_acts: bfloat16 [32768, 2560], P('dp'), may hold values from -6 to 6
- train_grads: bfloat16 [32768, 2560], P('dp'), may hold values from -6 to 6
- lengths: int32 [256], P('dp'), may hold values from 1 to 256, as said below
- query_acts: bfloat16 [128, 2560], replicated, may hold values from -6 to 6
- query_grads: bfloat16 [128, 2560], replicated, may hold values from -0.0059814453 to 0.0059814453
- basis_in: bfloat16 [2560, 2560], P(None, 'mp'), may hold values from -0.125 to 0.125
- basis_out: bfloat16 [2560, 2560], P(None, 'mp'), may hold values from -0.125 to 0.125
Outputs:
- scores: float32 [1, 256], P(None, 'dp')
Inputs may be any that keep to these rules, and one draw needn't show every extreme that they name: The 4 lengths of one index of dp sum to at most 512; in every draw some index's sequences fill all 512 rows and one of them has exactly 256 tokens.
All inputs are finite; a program needn't handle non-finite values.
Results may differ from a plain program's by a relative error of at most 0.0045.
Values may be sent and summed in bfloat16 or wider, within the bound.
No kernel may reach another device: no remote copies, remote signals or barrier semaphores. Data moves between devices by JAX's collectives and lax.ppermute only.
A program may use at most 128 MiB of HBM per device.

v0:
```python
import jax
import jax.numpy as jnp
from jax import lax
from jax.sharding import PartitionSpec as P

QUERIES = 1
QLEN = 128


damping_ratio = 0.1


def sent_to_all(array, axis):
    count = lax.axis_size(axis)
    return lax.all_to_all(
        jnp.broadcast_to(array[None], (count, *array.shape)), axis, 0, 0, tiled=True
    )


def of_everyone(array, axis):
    return sent_to_all(array, axis).sum(axis=0)


def rotate(values, basis):
    return jnp.dot(values, basis, preferred_element_type=jnp.float32).astype(jnp.bfloat16)


def shards(train_acts, train_grads, lengths, query_acts, query_grads, basis_in, basis_out):
    capacity = train_acts.shape[0]
    window = capacity // 2
    slot_count = lengths.shape[0]
    acts_block = rotate(train_acts, basis_in)
    query_block = rotate(query_acts, basis_in)
    acts_rot, query_rot = (
        lax.all_gather(acts_block, "mp", axis=1, tiled=True),
        lax.all_gather(query_block, "mp", axis=1, tiled=True),
    )
    grads_rot = rotate(train_grads, basis_out)
    query_grot = rotate(query_grads, basis_out).reshape(QUERIES, QLEN, -1)
    finish = jnp.cumsum(lengths)
    starts = finish - lengths
    position = jnp.arange(window, dtype=jnp.int32)
    curvature_local = jnp.zeros((grads_rot.shape[1], acts_rot.shape[1]), jnp.float32)
    stored_list = []
    for slot in range(slot_count):
        begin = jnp.minimum(starts[slot], capacity - window)
        grads_win = lax.dynamic_slice_in_dim(grads_rot, begin, window, 0)
        acts_win = lax.dynamic_slice_in_dim(acts_rot, begin, window, 0)
        inside = (position + begin >= starts[slot]) & (position + begin < finish[slot])
        grads_win = jnp.where(inside[:, None], grads_win, jnp.zeros_like(grads_win))
        product = lax.dot_general(
            grads_win, acts_win, (((0,), (0,)), ((), ())), preferred_element_type=jnp.float32
        )
        curvature_local = curvature_local + product * product
        stored_list.append(product.astype(jnp.bfloat16))
    stored = jnp.stack(stored_list)
    inverse_count = 1.0 / (slot_count * lax.axis_size("dp"))
    query_full = query_rot.reshape(QUERIES, QLEN, -1)
    curvature = lax.psum(curvature_local, "dp") * inverse_count
    grand_total = of_everyone(jnp.sum(curvature), "mp")
    damping = damping_ratio * grand_total / (curvature.size * lax.axis_size("mp"))
    local_grad = jnp.einsum(
        "qti,qtj->qij", query_grot, query_full, preferred_element_type=jnp.float32
    )
    precond = (local_grad / (curvature + damping)).astype(jnp.bfloat16)
    partial_value = jnp.einsum("qik,sik->qs", precond, stored, preferred_element_type=jnp.float32)
    return lax.psum(partial_value, "mp")


def solution(mesh):
    return jax.shard_map(
        shards,
        mesh=mesh,
        in_specs=(P("dp", None), P("dp", None), P("dp"), P(), P(), P(None, "mp"), P(None, "mp")),
        out_specs=P(None, "dp"),
        check_vma=False,
    )
```

profile of v0, /device:TPU:1, one launch (start us, length us, event | category | flops | bytes accessed | tf_op | source)
XLA Modules:
  0.0 735.1 jit_solution(1750475405128751214)
XLA Ops:
  6.5 0.0 copy-start
  6.5 0.0 copy-start.4
  6.5 0.0 all-gather.2.cloned.1.call-start
  6.5 5.9 convolution_convert_fusion
  12.5 0.0 all-gather.2.cloned.1.call-update
  12.5 0.0 all-reduce.2.cloned.1.call-start
  12.5 0.0 copy-done.4
  12.5 0.2 reduce-window.4
  12.7 0.6 fusion.42
  15.9 0.6 fusion.41
  16.5 1.3 compare_and_fusion.1
  17.8 1.3 compare_and_fusion.2
  19.1 1.2 compare_and_fusion
  20.3 1.2 compare_and_fusion.3
  21.5 0.0 copy-done
  21.5 4.8 convolution_convert_fusion.1
  26.3 45.8 %all-gather.2.cloned.1.call-done = bf16[512,2560]{1,0:T(8,128)(2,1)} async-done(((bf16[512,640]{1,0:T(8,128)(2,1)}), bf16[512,2560]{1,0:T(8,128)(2,1)}) %all-gather.2.cloned.1.call-update) | async-done | bytes 2621456 | tf_op jit(solution)/shard_map/all_gather | solution.py:35
  72.1 0.0 copy-start.2
  72.1 0.0 copy-start.3
  72.1 2.7 fusion.6
  74.8 0.0 copy-done.2
  74.8 0.0 copy-done.3
  74.8 3.9 fusion.8
  78.7 3.9 fusion.4
  82.7 17.3 %multiply_add_fusion = (f32[640,2560]{1,0:T(8,128)}, bf16[1,640,2560]{2,1,0:T(8,128)(2,1)}, bf16[1,640,2560]{2,1,0:T(8,128)(2,1)}, bf16[1,640,2560]{2,1,0:T(8,128)(2,1)}, bf16[1,640,2560]{2,1,0:T(8,128)(2,1)}) fusion(f32[640,2560]{1,0:T(8,128)} %fusion.4, f32[640,2560]{1,0:T(8,128)S(1)} %fusion.6, f32[640,2560]{1,0:T(8,128)} %fusion.8, ...), kind=kOutput, calls=%fused_computation.4 | convolution fusion | flops 857047040 | bytes 40961536 | tf_op jit(solution)/shard_map/dot_general | solution.py:51
  99.9 0.0 all-reduce.2.cloned.1.call-update
  99.9 0.0 copy-start.1
  99.9 3.0 convolution_convert_fusion.2
  102.9 24.0 %all_gather.6 = bf16[128,2560]{1,0:T(8,128)(2,1)} all-gather(bf16[128,640]{1,0:T(8,128)(2,1)S(1)} %convolution_convert_fusion.2), channel_id=1, replica_groups=mesh['dp'=64,'mp'=4] {'mp'}, dimensions={1}, use_global_device_ids=true | all-gather | bytes 819200 | tf_op jit(solution)/shard_map/all_gather | solution.py:36
  126.9 0.0 copy-done.1
  126.9 9.9 %pad_maximum_fusion = bf16[4,640,2560]{2,1,0:T(8,128)(2,1)} fusion(bf16[1,640,2560]{2,1,0:T(8,128)(2,1)} %get-tuple-element.9, bf16[1,640,2560]{2,1,0:T(8,128)(2,1)} %get-tuple-element.8, bf16[1,640,2560]{2,1,0:T(8,128)(2,1)} %get-tuple-element.7, bf16[1,640,2560]{2,1,0:T(8,128)(2,1)S(1)} %copy-done.1), kind=kLoop, calls=%fused_computation | loop fusion | flops 19660800 | bytes 26214400 | tf_op jit(solution)/shard_map/stack | solution.py:56
  136.8 534.0 %all-reduce.2.cloned.1.call-done = f32[640,2560]{1,0:T(8,128)} async-done(((f32[640,2560]{1,0:T(8,128)}), f32[640,2560]{1,0:T(8,128)}) %all-reduce.2.cloned.1.call-update) | async-done | bytes 6553616 | tf_op jit(solution)/shard_map/psum | solution.py:59
  670.8 5.1 multiply_reduce_fusion
  675.9 0.6 broadcast_in_dim.38
  676.6 12.3 %all_to_all.6 = f32[4,1,1]{2,1,0:T(1,128)S(1)} all-to-all(f32[4,1,1]{2,1,0:T(1,128)S(1)} %broadcast_in_dim.38), channel_id=1, replica_groups=mesh['dp'=64,'mp'=4] {'mp'}, dimensions={0} | all-to-all | bytes 32 | tf_op jit(solution)/shard_map/all_to_all | solution.py:15
  688.9 0.6 reduce_sum.19
  690.2 6.7 fusion.3
  696.8 23.8 %fusion.12 = f32[1,4]{1,0:T(1,128)S(1)} fusion(bf16[4,640,2560]{2,1,0:T(8,128)(2,1)} %pad_maximum_fusion, bf16[640,2560,1]{1,0,2:T(8,128)(2,1)} %fusion.3), kind=kOutput, calls=%fused_computation.24 | convolution fusion | flops 13107200 | bytes 16384016 | tf_op jit(solution)/shard_map/qik,sik->qs/dot_general | solution.py:66
  720.6 7.7 %psum.15 = f32[1,4]{1,0:T(1,128)} all-reduce(f32[1,4]{1,0:T(1,128)S(1)} %fusion.12), channel_id=1, replica_groups=mesh['dp'=64,'mp'=4] {'mp'}, use_global_device_ids=true, to_apply=%region_4.5 | all-reduce | flops 4 | bytes 32 | tf_op jit(solution)/shard_map/psum | solution.py:67
  (1 shorter events, 0.0 us)
Async XLA Ops:
  6.5 14.9 %copy-start = (bf16[2560,640]{1,0:T(8,128)(2,1)S(1)}, bf16[2560,640]{1,0:T(8,128)(2,1)}, u32[]{:S(2)}) copy-start(bf16[2560,640]{1,0:T(8,128)(2,1)} %param.13) | copy-start | bytes 9830404
  6.5 6.0 copy-start.4
  6.5 65.5 %all-gather.2.cloned.1.call-start = ((), (), s32[]{:S(2)}) async-start(), calls=%async_computation.1 | async-start | bytes 3276800 | tf_op jit(solution)/shard_map/all_gather | solution.py:35
  12.5 658.3 %all-reduce.2.cloned.1.call-start = ((), (), s32[]{:S(2)}) async-start(), calls=%async_computation.2 | async-start | bytes 13107200 | tf_op jit(solution)/shard_map/psum | solution.py:59
  72.1 2.8 copy-start.2
  72.1 2.8 copy-start.3
  99.9 27.0 %copy-start.1 = (bf16[1,640,2560]{2,1,0:T(8,128)(2,1)S(1)}, bf16[1,640,2560]{2,1,0:T(8,128)(2,1)}, u32[]{:S(2)}) copy-start(bf16[1,640,2560]{2,1,0:T(8,128)(2,1)} %get-tuple-element.6) | copy-start | bytes 9830404
Sparse Core Ops, SparseCore 0:
  12.6 59.4 all-gather.1
  100.0 570.7 all-reduce.1
where the time goes:
time: 743 us; the launch traced here: 735 us
  waiting for transfers between devices  580 us (78%)
  matrix products  71.9 us (10%)
  blocking collectives  44 us (6%)
  other arithmetic  20.8 us (3%)
  between operations  16.6 us (2%)
    psum x1, waiting for transfers between devices, shards(): curvature = lax.psum(curvature_local, 'dp') * inverse_count  534 us
    all_gather x1, waiting for transfers between devices, shards(): lax.all_gather(acts_block, 'mp', axis=1, tiled=True)  45.8 us
    dot_general x4, matrix products, shards(): lax.dot_general(grads_win, acts_win, (((0,), (0,)), ((), ())), preferred_...  27.8 us
    all_gather x1, blocking collectives, shards(): lax.all_gather(query_block, 'mp', axis=1, tiled=True)  24 us
    dot_general x1, matrix products, shards(): jnp.einsum('qik,sik->qs', precond, stored, preferred_element_type=jnp.flo...  23.8 us
  transfers between devices with their start and end apart: 2, of which 2 were waited for; matrix products, arithmetic and copies ran while one was open for 3% of the time, Pallas kernels for 0%

commit v1 on v0

v1 whole, which is shorter than its diff:
```python
import functools

import jax
import jax.numpy as jnp
import numpy as np
from jax import lax
from jax.experimental import pallas as pl
from jax.experimental.pallas import tpu as pltpu
from jax.sharding import Mesh
from jax.sharding import PartitionSpec as P

DAMPING_RATIO = 0.1
DP = ("x", "zl", "y", "c")
RING = ("x", "zl", "y")
BLOCKS = ("c", "m")
HALF = 256
VMEM = 60 * 1024 * 1024
f32 = jnp.float32
bf16 = jnp.bfloat16


def params():
    return pltpu.CompilerParams(vmem_limit_bytes=VMEM)


def dot(a, b, contract):
    return lax.dot_general(a, b, (contract, ((), ())), preferred_element_type=f32)


def rotate_kernel(transposed, tokens_ref, query_ref, basis_ref, *rest):
    outs, acc = rest[:-1], rest[-1]
    k = pl.program_id(0)
    rows = tokens_ref.shape[0]

    @pl.when(k == 0)
    def _():
        acc[...] = jnp.zeros_like(acc)

    basis = basis_ref[...]
    acc[:rows] += dot(tokens_ref[...], basis, ((1,), (0,)))
    acc[rows:] += dot(query_ref[...], basis, ((1,), (0,)))

    @pl.when(k == pl.num_programs(0) - 1)
    def _():
        if transposed:
            outs[0][...] = acc[:rows].T.astype(bf16)
            outs[1][...] = acc[rows:].T.astype(bf16)
        else:
            outs[0][...] = acc[...].astype(bf16)


def rotate(tokens, query, basis, transposed):
    rows, depth = tokens.shape
    qrows, width = query.shape[0], basis.shape[1]
    step = 512
    if transposed:
        shapes = [(width, rows), (width, qrows)]
    else:
        shapes = [(rows + qrows, width)]
    return pl.pallas_call(
        functools.partial(rotate_kernel, transposed),
        grid=(depth // step,),
        in_specs=[
            pl.BlockSpec((rows, step), lambda k: (0, k)),
            pl.BlockSpec((qrows, step), lambda k: (0, k)),
            pl.BlockSpec((step, width), lambda k: (k, 0)),
        ],
        out_specs=[pl.BlockSpec(s, lambda k: (0, 0)) for s in shapes],
        out_shape=[jax.ShapeDtypeStruct(s, bf16) for s in shapes],
        scratch_shapes=[pltpu.VMEM((rows + qrows, width), f32)],
        compiler_params=params(),
    )(tokens, query, basis)


def bounds_of(lengths_ref, which):
    result, at = [], jnp.int32(0)
    for j in range(lengths_ref.shape[1]):
        end = at + lengths_ref[which, j]
        result.append((at, end))
        at = end
    return result


def curvature_kernel(
    lengths_ref, g00, g01, g10, g11, a0_ref, a1_ref, out_ref, total_ref, masked, wide, g_ref, acc
):
    i = pl.program_id(0)
    first_member = i < pl.num_programs(0) // 2
    acts = (a0_ref, a1_ref)
    tokens = a0_ref.shape[0]
    count = lengths_ref.shape[1]

    @pl.when(i == 0)
    def _():
        total_ref[...] = jnp.zeros_like(total_ref)
        row = lax.broadcasted_iota(jnp.int32, (HALF, 1), 0)
        rows = lax.broadcasted_iota(jnp.int32, (tokens, 1), 0)
        for b in range(2):
            for j, (start, finish) in enumerate(bounds_of(lengths_ref, b)):
                base = jnp.where(start >= HALF, HALF, 0)
                at = pl.multiple_of(base, HALF)
                inside = (row + base >= start) & (row + base < finish)
                window = acts[b][pl.ds(at, HALF), :]
                masked[b * count + j] = jnp.where(inside, window, jnp.zeros_like(window))

                @pl.when((start < HALF) & (finish > HALF))
                def _(b=b, start=start, finish=finish):
                    inside = (rows >= start) & (rows < finish)
                    window = acts[b][0:tokens, :]
                    wide[b] = jnp.where(inside, window, jnp.zeros_like(window))

    g_ref[0] = jnp.where(first_member, g00[...], g10[...])
    g_ref[1] = jnp.where(first_member, g01[...], g11[...])
    for b in range(2):
        for j, (start, finish) in enumerate(bounds_of(lengths_ref, b)):
            at = pl.multiple_of(jnp.where(start >= HALF, HALF, 0), HALF)
            across = (start < HALF) & (finish > HALF)
            opening = b == 0 and j == 0

            def add(product, opening=opening):
                if opening:
                    acc[...] = product * product
                else:
                    acc[...] += product * product

            @pl.when(jnp.logical_not(across))
            def _(b=b, j=j, at=at, add=add):
                add(dot(g_ref[b, :, pl.ds(at, HALF)], masked[b * count + j], ((1,), (0,))))

            @pl.when(across)
            def _(b=b, add=add):
                add(dot(g_ref[b], wide[b], ((1,), (0,))))

    total = acc[...]
    out_ref[...] = total.astype(bf16)
    total_ref[...] += jnp.sum(total, axis=0, keepdims=True)


def curvature_of(lengths, g00, g01, g10, g11, a0, a1):
    width, tokens = g00.shape
    cols = a0.shape[1]
    tile = width // 2
    count = lengths.shape[1]
    near = pl.BlockSpec((tile, tokens), lambda i, *_: (jnp.minimum(i, 1), 0))
    far = pl.BlockSpec((tile, tokens), lambda i, *_: (jnp.maximum(i - 2, 0), 0))
    acts = pl.BlockSpec((tokens, cols), lambda i, *_: (0, 0))
    return pl.pallas_call(
        curvature_kernel,
        grid_spec=pltpu.PrefetchScalarGridSpec(
            num_scalar_prefetch=1,
            grid=(4,),
            in_specs=[near, near, far, far, acts, acts],
            out_specs=[
                pl.BlockSpec((tile, cols), lambda i, *_: (i, 0)),
                pl.BlockSpec((1, cols), lambda i, *_: (0, 0)),
            ],
            scratch_shapes=[
                pltpu.VMEM((2 * count, HALF, cols), bf16),
                pltpu.VMEM((2, tokens, cols), bf16),
                pltpu.VMEM((2, tile, tokens), bf16),
                pltpu.VMEM((tile, cols), f32),
            ],
        ),
        out_shape=[
            jax.ShapeDtypeStruct((2 * width, cols), bf16),
            jax.ShapeDtypeStruct((1, cols), f32),
        ],
        compiler_params=params(),
    )(lengths, g00, g01, g10, g11, a0, a1)


def precond_kernel(scale, damping_ref, parts_ref, qg_ref, qa_ref, out_ref):
    total = parts_ref[0].astype(f32)
    for j in range(1, parts_ref.shape[0]):
        total = total + parts_ref[j].astype(f32)
    query = dot(qg_ref[...], qa_ref[...], ((1,), (0,)))
    value = (query / (total * scale + damping_ref[0, 0])).astype(bf16)
    for j in range(out_ref.shape[0]):
        out_ref[j] = value


def precond_of(scale, damping, parts, qg, qa):
    return pl.pallas_call(
        functools.partial(precond_kernel, scale),
        in_specs=[pl.BlockSpec(memory_space=pltpu.SMEM)] + [pl.BlockSpec(memory_space=pltpu.VMEM)] * 3,
        out_specs=pl.BlockSpec(memory_space=pltpu.VMEM),
        out_shape=jax.ShapeDtypeStruct(parts.shape, bf16),
        compiler_params=params(),
    )(damping, parts, qg, qa)


def score_kernel(lengths_ref, p_ref, g00, g01, g10, g11, a0_ref, a1_ref, out_ref, sums):
    i = pl.program_id(0)
    first_member = i < pl.num_programs(0) // 2
    tokens = g00.shape[1]

    @pl.when(i == 0)
    def _():
        sums[...] = jnp.zeros_like(sums)

    precond = p_ref[...]
    for b, (near, far, acts) in enumerate(((g00, g10, a0_ref), (g01, g11, a1_ref))):
        grads = jnp.where(first_member, near[...], far[...]).astype(f32)
        moved = dot(precond, acts[0:tokens, :], ((1,), (1,)))
        sums[b : b + 1] += jnp.sum(grads * moved, axis=0, keepdims=True)

    @pl.when(i == pl.num_programs(0) - 1)
    def _():
        lane = lax.broadcasted_iota(jnp.int32, (1, tokens), 1)
        for b in range(2):
            for j, (start, finish) in enumerate(bounds_of(lengths_ref, b)):
                inside = (lane >= start) & (lane < finish)
                value = jnp.sum(jnp.where(inside, sums[b : b + 1], 0.0), axis=1, keepdims=True)
                out_ref[b, j : j + 1, :] = jnp.broadcast_to(value, (1, out_ref.shape[2]))


def scores_of(lengths, precond, g00, g01, g10, g11, a0, a1):
    width, tokens = g00.shape
    cols = a0.shape[1]
    tile = width // 2
    count = lengths.shape[1]
    near = pl.BlockSpec((tile, tokens), lambda i, *_: (jnp.minimum(i, 1), 0))
    far = pl.BlockSpec((tile, tokens), lambda i, *_: (jnp.maximum(i - 2, 0), 0))
    acts = pl.BlockSpec((tokens, cols), lambda i, *_: (0, 0))
    return pl.pallas_call(
        score_kernel,
        grid_spec=pltpu.PrefetchScalarGridSpec(
            num_scalar_prefetch=1,
            grid=(4,),
            in_specs=[
                pl.BlockSpec((tile, cols), lambda i, *_: (i, 0)),
                near, near, far, far, acts, acts,
            ],
            out_specs=pl.BlockSpec((2, count, 128), lambda i, *_: (0, 0, 0)),
            scratch_shapes=[pltpu.VMEM((2, tokens), f32)],
        ),
        out_shape=jax.ShapeDtypeStruct((2, count, 128), f32),
        compiler_params=params(),
    )(lengths, precond, g00, g01, g10, g11, a0, a1)


def routes(f):
    return [(c * 4 + m, f(c, m)[0] * 4 + f(c, m)[1]) for c in range(2) for m in range(4)]


OTHER_CORE = routes(lambda c, m: (1 - c, m))
GRADS_PARTNER = routes(lambda c, m: (c, m ^ 1))
ACTS_SAME = routes(lambda c, m: (0, m) if c == 0 else (1, 3 - m))
ACTS_OTHER = routes(lambda c, m: (0, m) if c == 1 else (1, 3 - m))


def sent_to_all(array, axes, count):
    return lax.all_to_all(jnp.broadcast_to(array[None], (count, *array.shape)), axes, 0, 0, tiled=True)


def shards(train_acts, train_grads, lengths, query_acts, query_grads, basis_in, basis_out):
    core = lax.axis_index("c")
    ring = lax.axis_index(RING)
    ring_size = lax.axis_size(RING)
    tokens = train_acts.shape[0]
    count = lengths.shape[0]

    g00, qg_own = rotate(train_grads, query_grads, basis_out, True)
    both = jnp.stack([lengths, lax.ppermute(lengths, BLOCKS, OTHER_CORE)])
    g10 = lax.ppermute(g00, BLOCKS, GRADS_PARTNER)
    g01 = lax.ppermute(g00, BLOCKS, OTHER_CORE)
    (acts,) = rotate(train_acts, query_acts, basis_in, False)
    a1 = lax.ppermute(acts, BLOCKS, ACTS_OTHER)
    a0 = lax.ppermute(acts[:tokens], BLOCKS, ACTS_SAME)
    g11 = lax.ppermute(g10, BLOCKS, OTHER_CORE)
    qa = a1[tokens:]
    a1 = a1[:tokens]

    width, cols = g00.shape[0], a0.shape[1]
    chunk = 2 * width // ring_size
    inner = ring_size // 2
    qg_mine = lax.dynamic_slice_in_dim(qg_own, lax.rem(ring, inner) * chunk, chunk, 0)
    qg_far = lax.ppermute(qg_mine, BLOCKS, GRADS_PARTNER)
    qg = jnp.where(ring < inner, qg_mine, qg_far)

    curvature, totals = curvature_of(both, g00, g01, g10, g11, a0, a1)
    parts = lax.all_to_all(curvature.reshape(ring_size, chunk, cols), RING, 0, 0, tiled=True)
    total = jnp.sum(totals).reshape(1, 1)
    total = jnp.sum(sent_to_all(total, RING, ring_size), axis=0)
    total = jnp.sum(sent_to_all(total, BLOCKS, 8), axis=0)
    scale = 1.0 / (count * lax.axis_size(DP))
    entries = 2 * width * cols * 8
    damping = total * (DAMPING_RATIO * scale / entries)

    mine = precond_of(scale, damping, parts, qg, qa)
    precond = lax.all_to_all(mine, RING, 0, 0, tiled=True).reshape(2 * width, cols)
    found = scores_of(both, precond, g00, g01, g10, g11, a0, a1)[:, :, 0]
    by_core = jnp.where(core == 0, found, found[::-1])
    sent = jnp.broadcast_to(by_core[:, None], (2, 4, count)).reshape(8, 1, count)
    return jnp.sum(lax.all_to_all(sent, BLOCKS, 0, 0, tiled=True), axis=0)


def solution(mesh):
    cut = Mesh(np.asarray(mesh.devices).reshape(4, 2, 4, 2, 4), ("x", "zl", "y", "c", "m"))
    return jax.shard_map(
        shards,
        mesh=cut,
        in_specs=(P(DP, None), P(DP, None), P(DP), P(), P(), P(None, "m"), P(None, "m")),
        out_specs=P(None, DP),
        check_vma=False,
    )
```

time: 743 us -> 186 us (0.25)
  waiting for transfers between devices: 580 us -> 64.7 us
  matrix products: 71.9 us -> 0 us
  Pallas kernels: 0 us -> 38.6 us
  starting transfers between devices: 0.04 us -> 23.3 us
  other arithmetic: 20.8 us -> 4.95 us
  between operations: 16.6 us -> 0.76 us
  local copies, waits for them, and re-layouts: 1.96 us -> 9.8 us
    psum x1 -> x0, waiting for transfers between devices: 534 us -> none  [shards(): curvature = lax.psum(curvature_local, 'dp') * inverse_count]
    dot_general x9 -> x0, matrix products: 71.9 us -> none  [the longest x4 27.8 us: shards(): lax.dot_general(grads_win, acts_win, (((0,), (0,)), ((), ())), preferred_...]
    all_gather x1 -> x0, waiting for transfers between devices: 45.8 us -> none  [shards(): lax.all_gather(acts_block, 'mp', axis=1, tiled=True)]
    ppermute x0 -> x7, waiting for transfers between devices: none -> 41 us  [the longest x1 16.4 us: shards(): qg_far = lax.ppermute(qg_mine, BLOCKS, GRADS_PARTNER)]
    pallas_call x0 -> x5, Pallas kernels: none -> 38.6 us  [the longest x1 14.5 us: curvature_of(): pl.pallas_call(curvature_kernel, grid_spec=pltpu.PrefetchScalarGridSpec(n...]
    all_to_all x1 -> x3, blocking collectives: 12.3 us -> 42.6 us  [the longest x2 29.7 us: sent_to_all(): lax.all_to_all(jnp.broadcast_to(array[None], (count, *array.shape)), axes...]
    all_gather x1 -> x0, blocking collectives: 24 us -> none  [shards(): lax.all_gather(query_block, 'mp', axis=1, tiled=True)]
    all_to_all x0 -> x2, waiting for transfers between devices: none -> 23.7 us  [the longest x1 21 us: shards(): lax.all_to_all(mine, RING, 0, 0, tiled=True).reshape(2 * width, cols)]
  transfers between devices with their start and end apart: 2 -> 9, of which waited for: 2 -> 7; matrix products, arithmetic and copies ran while one was open for 3% -> 3% of each run, Pallas kernels for 0% -> 4%
where the time goes in v1:
time: 186 us; the launch traced here: 185 us
  waiting for transfers between devices  64.7 us (35%)
  blocking collectives  42.6 us (23%)
  Pallas kernels  38.6 us (21%)
  starting transfers between devices  23.3 us (13%)
  local copies, waits for them, and re-layouts  9.8 us (5%)
  other arithmetic  4.95 us (3%)
    all_to_all x2, blocking collectives, sent_to_all(): lax.all_to_all(jnp.broadcast_to(array[None], (count, *array.shape)), axes...  29.7 us
    all_to_all x1, waiting for transfers between devices, shards(): lax.all_to_all(mine, RING, 0, 0, tiled=True).reshape(2 * width, cols)  21 us
    ppermute x1, waiting for transfers between devices, shards(): qg_far = lax.ppermute(qg_mine, BLOCKS, GRADS_PARTNER)  16.4 us
    pallas_call x1, Pallas kernels, curvature_of(): pl.pallas_call(curvature_kernel, grid_spec=pltpu.PrefetchScalarGridSpec(n...  14.5 us
    pallas_call x2, Pallas kernels, rotate(): pl.pallas_call(functools.partial(rotate_kernel, transposed), grid=(depth...  14.4 us
    all_to_all x1, blocking collectives, shards(): return jnp.sum(lax.all_to_all(sent, BLOCKS, 0, 0, tiled=True), axis=0)  12.9 us
    ppermute x1, waiting for transfers between devices, shards(): g10 = lax.ppermute(g00, BLOCKS, GRADS_PARTNER)  12.7 us
    ppermute x1, waiting for transfers between devices, shards(): a1 = lax.ppermute(acts, BLOCKS, ACTS_OTHER)  7.7 us
  transfers between devices with their start and end apart: 9, of which 7 were waited for; matrix products, arithmetic and copies ran while one was open for 3% of the time, Pallas kernels for 4%

profile of v1, /device:TPU:1, one launch (start us, length us, event | category | flops | bytes accessed | tf_op | source)
XLA Modules:
  0.0 184.7 jit_solution(11291215411105172100)
XLA Ops:
  0.0 7.3 %shard_map.73 = (bf16[640,512]{1,0:T(8,128)(2,1)}, bf16[640,128]{1,0:T(8,128)(2,1)}) custom-call(bf16[512,2560]{1,0:T(8,128)(2,1)} %tokens_ref.2, bf16[128,2560]{1,0:T(8,128)(2,1)} %query_ref.2, bf16[2560,640]{1,0:T(8,128)(2,1)} %basis_ref.2), custom_call_target="tpu_custom_call" | custom-call | tf_op jit(solution)/shard_map/pallas_call | solution.py:60
  7.3 0.0 copy-start.2
  7.3 0.0 copy-start.7
  7.3 3.9 %collective-permute-start.2 = (bf16[640,512]{1,0:T(8,128)(2,1)}, bf16[640,512]{1,0:T(8,128)(2,1)S(1)}, u32[]{:S(2)}, u32[]{:S(2)}) collective-permute-start(bf16[640,512]{1,0:T(8,128)(2,1)} %get-tuple-element.9.g00), channel_id=1, source_target_pairs={{0,1},{1,0},{2,3},{3,2},{4,5},{5,4},{6,7},{7,6},{8,9},{9,8},{10,11... | collective-permute-start | bytes 1966088 | tf_op jit(solution)/shard_map/ppermute | solution.py:265
  11.2 7.1 %shard_map.74 = bf16[640,640]{1,0:T(8,128)(2,1)} custom-call(bf16[512,2560]{1,0:T(8,128)(2,1)} %tokens_ref.3, bf16[128,2560]{1,0:T(8,128)(2,1)} %query_ref.3, bf16[2560,640]{1,0:T(8,128)(2,1)} %basis_ref.3), custom_call_target="tpu_custom_call" | custom-call | tf_op jit(solution)/shard_map/pallas_call | solution.py:60
  18.3 1.0 collective-permute-start.5
  19.3 0.0 copy-done.2
  19.3 3.6 %collective-permute-start.1 = (bf16[640,512]{1,0:T(8,128)(2,1)S(1)}, bf16[640,512]{1,0:T(8,128)(2,1)S(1)}, u32[]{:S(2)}, u32[]{:S(2)}) collective-permute-start(bf16[640,512]{1,0:T(8,128)(2,1)S(1)} %copy-done.2), channel_id=1, source_target_pairs={{0,4},{1,5},{2,6},{3,7},{4,0},{5,1},{6,2},{7,3},{8,12},{9,13},{10,... | collective-permute-start | bytes 1966088 | tf_op jit(solution)/shard_map/ppermute | solution.py:266
  22.9 1.1 slice.16
  24.1 2.6 %collective-permute-start.4 = (bf16[512,640]{1,0:T(8,128)(2,1)S(1)}, bf16[512,640]{1,0:T(8,128)(2,1)S(1)}, u32[]{:S(2)}, u32[]{:S(2)}) collective-permute-start(bf16[512,640]{1,0:T(8,128)(2,1)S(1)} %slice.16), channel_id=1, source_target_pairs={{0,0},{1,1},{2,2},{3,3},{4,7},{5,6},{6,5},{7,4},{8,8},{9,9},{10,10... | collective-permute-start | bytes 1966088 | tf_op jit(solution)/shard_map/ppermute | solution.py:269
  26.6 12.7 %collective-permute-done.2.g10 = bf16[640,512]{1,0:T(8,128)(2,1)S(1)} collective-permute-done((bf16[640,512]{1,0:T(8,128)(2,1)}, bf16[640,512]{1,0:T(8,128)(2,1)S(1)}, u32[]{:S(2)}, u32[]{:S(2)}) %collective-permute-start.2) | collective-permute-done | bytes 655392 | tf_op jit(solution)/shard_map/ppermute | solution.py:265
  39.3 0.0 copy-start.3
  39.3 2.0 %collective-permute-start.3 = (bf16[640,512]{1,0:T(8,128)(2,1)S(1)}, bf16[640,512]{1,0:T(8,128)(2,1)S(1)}, u32[]{:S(2)}, u32[]{:S(2)}) collective-permute-start(bf16[640,512]{1,0:T(8,128)(2,1)S(1)} %collective-permute-done.2.g10), channel_id=1, source_target_pairs={{0,4},{1,5},{2,6},{3,7},{4,0},{5,1},{6,2},{7,3},{8,12},{9,13},{10,... | collective-permute-start | bytes 1966088 | tf_op jit(solution)/shard_map/ppermute | solution.py:270
  41.3 0.0 copy-done.7
  41.3 0.1 collective-permute-start
  41.4 1.6 collective-permute-done
  43.0 0.6 pad_add_fusion.lengths_ref
  43.6 7.7 %collective-permute-done.5 = bf16[640,640]{1,0:T(8,128)(2,1)S(1)} collective-permute-done((bf16[640,640]{1,0:T(8,128)(2,1)}, bf16[640,640]{1,0:T(8,128)(2,1)S(1)}, u32[]{:S(2)}, u32[]{:S(2)}) %collective-permute-start.5) | collective-permute-done | bytes 819232 | tf_op jit(solution)/shard_map/ppermute | solution.py:268
  51.3 0.9 slice.17.a1_ref
  52.2 2.6 %collective-permute-done.4.a0_ref = bf16[512,640]{1,0:T(8,128)(2,1)S(1)} collective-permute-done((bf16[512,640]{1,0:T(8,128)(2,1)S(1)}, bf16[512,640]{1,0:T(8,128)(2,1)S(1)}, u32[]{:S(2)}, u32[]{:S(2)}) %collective-permute-start.4) | collective-permute-done | bytes 655392 | tf_op jit(solution)/shard_map/ppermute | solution.py:269
  54.8 0.0 copy-start.5
  54.8 0.0 collective-permute-done.1.g01
  54.8 0.0 copy-start.4
  54.8 0.0 collective-permute-done.3.g11
  54.8 0.0 copy-done.3
  54.8 0.8 copy-done.5
  55.6 0.2 copy-done.4
  55.8 0.0 copy-start.6
  55.8 0.9 copy-done.6
  56.7 14.5 %shard_map.75 = (bf16[1280,640]{1,0:T(8,128)(2,1)}, f32[1,640]{1,0:T(1,128)}) custom-call(s32[2,4]{1,0:T(2,128)} %pad_add_fusion.lengths_ref, bf16[640,512]{1,0:T(8,128)(2,1)} %get-tuple-element.9.g00, bf16[640,512]{1,0:T(8,128)(2,1)} %copy-done.4, bf16[640,512]{1,0:T(8,128)(2,1)} %copy-done.3, bf16[640,512]{1,0:T(8,128)(2,1)} %copy-done.6, ...), custom_call_target="tpu_custom_call" | custom-call | tf_op jit(solution)/shard_map/pallas_call | solution.py:147
  71.2 1.3 reduce_sum.38
  72.4 0.7 broadcast_in_dim.6
  73.1 17.3 %all_to_all.25 = f32[32,1,1]{2,1,0:T(1,128)S(1)} all-to-all(f32[32,1,1]{2,1,0:T(1,128)S(1)} %broadcast_in_dim.6), channel_id=1, replica_groups=mesh['x'=4,'zl'=2,'y'=4,'c'=2,'m'=4] {'x','zl','y'}, dimensions={0} | all-to-all | bytes 256 | tf_op jit(solution)/shard_map/all_to_all | solution.py:253
  90.4 0.6 reduce_sum.39
  91.1 0.6 broadcast_in_dim.7
  91.7 12.4 %all_to_all.26 = f32[8,1,1]{2,1,0:T(1,128)S(1)} all-to-all(f32[8,1,1]{2,1,0:T(1,128)S(1)} %broadcast_in_dim.7), channel_id=1, replica_groups=mesh['x'=4,'zl'=2,'y'=4,'c'=2,'m'=4] {'c','m'}, dimensions={0} | all-to-all | bytes 64 | tf_op jit(solution)/shard_map/all_to_all | solution.py:253
  104.1 4.0 %all-to-all-start.2 = ((bf16[32,40,640]{2,1,0:T(8,128)(2,1)}), bf16[32,40,640]{2,1,0:T(8,128)(2,1)S(1)}, u32[]{:S(2)}, u32[]{:S(2)}) async-start(bf16[32,40,640]{2,1,0:T(8,128)(2,1)} %bitcast.8), calls=%async_computation.2 | async-start | bytes 3276800 | tf_op jit(solution)/shard_map/all_to_all | solution.py:282
  108.1 0.7 constant_dynamic-slice_fusion
  108.8 0.3 collective-permute-start.6
  109.1 16.4 %collective-permute-done.6 = bf16[40,128]{1,0:T(8,128)(2,1)S(1)} collective-permute-done((bf16[40,128]{1,0:T(8,128)(2,1)S(1)}, bf16[40,128]{1,0:T(8,128)(2,1)S(1)}, u32[]{:S(2)}, u32[]{:S(2)}) %collective-permute-start.6) | collective-permute-done | bytes 10272 | tf_op jit(solution)/shard_map/ppermute | solution.py:278
  125.5 1.3 broadcast_select_fusion.qg_ref
  126.8 0.7 slice.18.qa_ref
  127.5 0.6 reduce_sum.40
  128.7 2.7 %all-to-all-done.2.parts_ref = bf16[32,40,640]{2,1,0:T(8,128)(2,1)S(1)} async-done(((bf16[32,40,640]{2,1,0:T(8,128)(2,1)}), bf16[32,40,640]{2,1,0:T(8,128)(2,1)S(1)}, u32[]{:S(2)}, u32[]{:S(2)}) %all-to-all-start.2) | async-done | bytes 1638432 | tf_op jit(solution)/shard_map/all_to_all | solution.py:282
  131.4 0.0 copy-start
  131.4 1.2 copy-done
  132.6 2.9 %shard_map.76 = bf16[32,40,640]{2,1,0:T(8,128)(2,1)} custom-call(f32[1,1]{1,0:T(1,128)} %bitcast.2.damping_ref, bf16[32,40,640]{2,1,0:T(8,128)(2,1)} %copy-done, bf16[40,128]{1,0:T(8,128)(2,1)} %broadcast_select_fusion.qg_ref, bf16[128,640]{1,0:T(8,128)(2,1)} %slice.18.qa_ref), custom_call_target="tpu_custom_call" | custom-call | tf_op jit(solution)/shard_map/pallas_call | solution.py:183
  135.5 5.9 %all-to-all-start.3 = ((bf16[32,40,640]{2,1,0:T(8,128)(2,1)}), bf16[32,40,640]{2,1,0:T(8,128)(2,1)S(1)}, u32[]{:S(2)}, u32[]{:S(2)}) async-start(bf16[32,40,640]{2,1,0:T(8,128)(2,1)} %shard_map.76), calls=%async_computation.3 | async-start | bytes 3276800 | tf_op jit(solution)/shard_map/all_to_all | solution.py:291
  141.5 21.0 %all-to-all-done.3 = bf16[32,40,640]{2,1,0:T(8,128)(2,1)S(1)} async-done(((bf16[32,40,640]{2,1,0:T(8,128)(2,1)}), bf16[32,40,640]{2,1,0:T(8,128)(2,1)S(1)}, u32[]{:S(2)}, u32[]{:S(2)}) %all-to-all-start.3) | async-done | bytes 1638432 | tf_op jit(solution)/shard_map/all_to_all | solution.py:291
  162.5 0.0 copy-start.1
  162.5 1.2 copy-done.1
  163.7 6.8 %shard_map.77 = f32[2,4,128]{2,1,0:T(4,128)} custom-call(s32[2,4]{1,0:T(2,128)} %pad_add_fusion.lengths_ref, bf16[1280,640]{1,0:T(8,128)(2,1)} %bitcast.7, bf16[640,512]{1,0:T(8,128)(2,1)} %get-tuple-element.9.g00, bf16[640,512]{1,0:T(8,128)(2,1)} %copy-done.4, bf16[640,512]{1,0:T(8,128)(2,1)} %copy-done.3, bf16[640,512]{1,0:T(8,128)(2,1)} %copy-done.6, ...), custom_call_target="tpu_custom_call" | custom-call | tf_op jit(solution)/shard_map/pallas_call | solution.py:225
  170.4 0.8 slice_reduce_fusion
  171.2 12.9 %all_to_all.27 = f32[8,1,4]{2,1,0:T(1,128)S(1)} all-to-all(f32[8,1,4]{2,1,0:T(1,128)S(1)} %bitcast.9), channel_id=1, replica_groups=mesh['x'=4,'zl'=2,'y'=4,'c'=2,'m'=4] {'c','m'}, dimensions={0} | all-to-all | bytes 256 | tf_op jit(solution)/shard_map/all_to_all | solution.py:295
  184.1 0.5 reduce_sum.41
  (3 shorter events, 0.0 us)
Async XLA Ops:
  7.3 11.9 %copy-start.2 = (bf16[640,512]{1,0:T(8,128)(2,1)S(1)}, bf16[640,512]{1,0:T(8,128)(2,1)}, u32[]{:S(2)}) copy-start(bf16[640,512]{1,0:T(8,128)(2,1)} %get-tuple-element.9.g00) | copy-start | bytes 1966084
  7.3 33.9 %copy-start.7 = (s32[4]{0:T(128)S(1)}, s32[4]{0:T(128)}, u32[]{:S(2)}) copy-start(s32[4]{0:T(128)} %param.9) | copy-start | bytes 52
  7.3 32.0 %collective-permute-start.2 = (bf16[640,512]{1,0:T(8,128)(2,1)}, bf16[640,512]{1,0:T(8,128)(2,1)S(1)}, u32[]{:S(2)}, u32[]{:S(2)}) collective-permute-start(bf16[640,512]{1,0:T(8,128)(2,1)} %get-tuple-element.9.g00), channel_id=1, source_target_pairs={{0,1},{1,0},{2,3},{3,2},{4,5},{5,4},{6,7},{7,6},{8,9},{9,8},{10,11... | collective-permute-start | bytes 1966088 | tf_op jit(solution)/shard_map/ppermute | solution.py:265
  18.3 33.0 %collective-permute-start.5 = (bf16[640,640]{1,0:T(8,128)(2,1)}, bf16[640,640]{1,0:T(8,128)(2,1)S(1)}, u32[]{:S(2)}, u32[]{:S(2)}) collective-permute-start(bf16[640,640]{1,0:T(8,128)(2,1)} %shard_map.74), channel_id=1, source_target_pairs={{0,7},{1,6},{2,5},{3,4},{4,0},{5,1},{6,2},{7,3},{8,15},{9,14},{10,... | collective-permute-start | bytes 2457608 | tf_op jit(solution)/shard_map/ppermute | solution.py:268
  19.3 35.5 %collective-permute-start.1 = (bf16[640,512]{1,0:T(8,128)(2,1)S(1)}, bf16[640,512]{1,0:T(8,128)(2,1)S(1)}, u32[]{:S(2)}, u32[]{:S(2)}) collective-permute-start(bf16[640,512]{1,0:T(8,128)(2,1)S(1)} %copy-done.2), channel_id=1, source_target_pairs={{0,4},{1,5},{2,6},{3,7},{4,0},{5,1},{6,2},{7,3},{8,12},{9,13},{10,... | collective-permute-start | bytes 1966088 | tf_op jit(solution)/shard_map/ppermute | solution.py:266
  24.1 30.7 %collective-permute-start.4 = (bf16[512,640]{1,0:T(8,128)(2,1)S(1)}, bf16[512,640]{1,0:T(8,128)(2,1)S(1)}, u32[]{:S(2)}, u32[]{:S(2)}) collective-permute-start(bf16[512,640]{1,0:T(8,128)(2,1)S(1)} %slice.16), channel_id=1, source_target_pairs={{0,0},{1,1},{2,2},{3,3},{4,7},{5,6},{6,5},{7,4},{8,8},{9,9},{10,10... | collective-permute-start | bytes 1966088 | tf_op jit(solution)/shard_map/ppermute | solution.py:269
  39.3 15.5 %copy-start.3 = (bf16[640,512]{1,0:T(8,128)(2,1)}, bf16[640,512]{1,0:T(8,128)(2,1)S(1)}, u32[]{:S(2)}) copy-start(bf16[640,512]{1,0:T(8,128)(2,1)S(1)} %collective-permute-done.2.g10) | copy-start | bytes 1966084
  39.3 15.5 %collective-permute-start.3 = (bf16[640,512]{1,0:T(8,128)(2,1)S(1)}, bf16[640,512]{1,0:T(8,128)(2,1)S(1)}, u32[]{:S(2)}, u32[]{:S(2)}) collective-permute-start(bf16[640,512]{1,0:T(8,128)(2,1)S(1)} %collective-permute-done.2.g10), channel_id=1, source_target_pairs={{0,4},{1,5},{2,6},{3,7},{4,0},{5,1},{6,2},{7,3},{8,12},{9,13},{10,... | collective-permute-start | bytes 1966088 | tf_op jit(solution)/shard_map/ppermute | solution.py:270
  41.3 1.7 collective-permute-start
  54.8 0.8 copy-start.5
  54.8 1.1 copy-start.4
  55.8 0.9 copy-start.6
  104.1 27.3 %all-to-all-start.2 = ((bf16[32,40,640]{2,1,0:T(8,128)(2,1)}), bf16[32,40,640]{2,1,0:T(8,128)(2,1)S(1)}, u32[]{:S(2)}, u32[]{:S(2)}) async-start(bf16[32,40,640]{2,1,0:T(8,128)(2,1)} %bitcast.8), calls=%async_computation.2 | async-start | bytes 3276800 | tf_op jit(solution)/shard_map/all_to_all | solution.py:282
  108.8 16.7 %collective-permute-start.6 = (bf16[40,128]{1,0:T(8,128)(2,1)S(1)}, bf16[40,128]{1,0:T(8,128)(2,1)S(1)}, u32[]{:S(2)}, u32[]{:S(2)}) collective-permute-start(bf16[40,128]{1,0:T(8,128)(2,1)S(1)} %constant_dynamic-slice_fusion), channel_id=1, source_target_pairs={{0,1},{1,0},{2,3},{3,2},{4,5},{5,4},{6,7},{7,6},{8,9},{9,8},{10,11... | collective-permute-start | bytes 30728 | tf_op jit(solution)/shard_map/ppermute | solution.py:278
  131.4 1.2 copy-start
  135.5 27.0 %all-to-all-start.3 = ((bf16[32,40,640]{2,1,0:T(8,128)(2,1)}), bf16[32,40,640]{2,1,0:T(8,128)(2,1)S(1)}, u32[]{:S(2)}, u32[]{:S(2)}) async-start(bf16[32,40,640]{2,1,0:T(8,128)(2,1)} %shard_map.76), calls=%async_computation.3 | async-start | bytes 3276800 | tf_op jit(solution)/shard_map/all_to_all | solution.py:291
  162.5 1.2 copy-start.1

commit v2 on v0

v2 whole, which is shorter than its diff:
```python
import functools

import jax
import jax.numpy as jnp
import numpy as np
from jax import lax
from jax.experimental import pallas as pl
from jax.experimental.pallas import tpu as pltpu
from jax.sharding import Mesh
from jax.sharding import PartitionSpec as P

DAMPING_RATIO = 0.1
DP = ("x", "zl", "y", "c")
RING = ("x", "zl", "y")
BLOCKS = ("c", "m")
HALF = 256
VMEM = 24 * 1024 * 1024
f32 = jnp.float32
bf16 = jnp.bfloat16


def params():
    return pltpu.CompilerParams(vmem_limit_bytes=VMEM)


def dot(a, b, contract):
    return lax.dot_general(a, b, (contract, ((), ())), preferred_element_type=f32)


def rotate(values, basis):
    return dot(values, basis, ((1,), (0,))).astype(bf16)


def rotate_transposed(values, basis):
    return dot(basis, values, ((0,), (1,))).astype(bf16)


def in_vmem(*arrays):
    return [pltpu.with_memory_space_constraint(a, pltpu.VMEM) for a in arrays]


def local_call(kernel, shapes, scratch=(), scalars=1):
    def call(*operands):
        here = pl.BlockSpec(memory_space=pltpu.VMEM)
        there = pl.BlockSpec(memory_space=pltpu.SMEM)
        return pl.pallas_call(
            kernel,
            in_specs=[there] * scalars + [here] * (len(operands) - scalars),
            out_specs=[here] * len(shapes),
            out_shape=list(shapes),
            scratch_shapes=list(scratch),
            compiler_params=params(),
        )(*operands[:scalars], *in_vmem(*operands[scalars:]))

    return call


def bounds_of(lengths_ref, which):
    result, at = [], jnp.int32(0)
    for j in range(lengths_ref.shape[1]):
        end = at + lengths_ref[which, j]
        result.append((at, end))
        at = end
    return result


def pick(index, values):
    chosen = values[0]
    for j in range(1, len(values)):
        chosen = jnp.where(index == j, values[j], chosen)
    return chosen


def curvature_kernel(rt, lengths_ref, g00, g01, g10, g11, a0_ref, a1_ref, out_ref, masked, wide):
    acts = (a0_ref, a1_ref)
    tokens, cols = a0_ref.shape
    width = g00.shape[0]
    count = lengths_ref.shape[1]
    row = lax.broadcasted_iota(jnp.int32, (HALF, 1), 0)
    rows = lax.broadcasted_iota(jnp.int32, (tokens, 1), 0)
    places = []
    for b in range(2):
        bounds = bounds_of(lengths_ref, b)
        starts, ends = [v[0] for v in bounds], [v[1] for v in bounds]
        across = jnp.int32(count - 1)
        for j, (start, finish) in enumerate(bounds):
            across = jnp.where((start < HALF) & (finish > HALF), j, across)
        inside = (rows >= pick(across, starts)) & (rows < pick(across, ends))
        wide[b] = jnp.where(inside, acts[b][...], jnp.zeros((tokens, cols), bf16))
        for k in range(count - 1):
            which = k + (k >= across).astype(jnp.int32)
            start, finish = pick(which, starts), pick(which, ends)
            base = jnp.where(start >= HALF, HALF, 0)
            at = pl.multiple_of(base, HALF)
            inside = (row + base >= start) & (row + base < finish)
            window = acts[b][pl.ds(at, HALF), :]
            masked[b * (count - 1) + k] = jnp.where(inside, window, jnp.zeros_like(window))
            places.append((b, b * (count - 1) + k, at))

    sums = jnp.zeros((1, cols), f32)
    for member, grads in enumerate(((g00, g01), (g10, g11))):

        def body(i, sums, member=member, grads=grads):
            r = pl.multiple_of(i * rt, rt)
            total = None
            for b in range(2):
                product = dot(grads[b][pl.ds(r, rt), :], wide[b], ((1,), (0,)))
                total = product * product if total is None else total + product * product
            for b, slot, at in places:
                product = dot(grads[b][pl.ds(r, rt), pl.ds(at, HALF)], masked[slot], ((1,), (0,)))
                total = total + product * product
            out_ref[pl.ds(member * width + r, rt), 0:cols] = total.astype(bf16)
            return sums + jnp.sum(total, axis=0, keepdims=True)

        sums = lax.fori_loop(0, width // rt, body, sums)
    total = jnp.sum(sums, axis=1, keepdims=True)
    high = total.astype(bf16)
    rest = total - high.astype(f32)
    middle = rest.astype(bf16)
    low = (rest - middle.astype(f32)).astype(bf16)
    lane = lax.broadcasted_iota(jnp.int32, (1, 128), 1)
    terms = jnp.where(lane == 0, high.astype(f32), jnp.where(lane == 1, middle.astype(f32), low.astype(f32)))
    terms = jnp.where(lane < 3, terms, 0.0)
    out_ref[:, cols:] = jnp.broadcast_to(terms, (out_ref.shape[0], 128)).astype(bf16)


def curvature_of(lengths, g00, g01, g10, g11, a0, a1):
    width = g00.shape[0]
    tokens, cols = a0.shape
    count = lengths.shape[1]
    return local_call(
        functools.partial(curvature_kernel, width),
        [jax.ShapeDtypeStruct((2 * width, cols + 128), bf16)],
        [pltpu.VMEM((2 * (count - 1), HALF, cols), bf16), pltpu.VMEM((2, tokens, cols), bf16)],
    )(lengths, g00, g01, g10, g11, a0, a1)[0]


def precond_kernel(scale, damping_ref, parts_ref, qg_ref, qa_ref, out_ref):
    cols = qa_ref.shape[1]
    total = parts_ref[0, :, 0:cols].astype(f32)
    for j in range(1, parts_ref.shape[0]):
        total = total + parts_ref[j, :, 0:cols].astype(f32)
    query = dot(qg_ref[...], qa_ref[...], ((1,), (0,)))
    value = (query / (total * scale + damping_ref[0, 0])).astype(bf16)
    for j in range(out_ref.shape[0]):
        out_ref[j] = value


def precond_of(scale, damping, parts, qg, qa):
    shape = (parts.shape[0], parts.shape[1], qa.shape[1])
    return local_call(
        functools.partial(precond_kernel, scale), [jax.ShapeDtypeStruct(shape, bf16)]
    )(damping, parts, qg, qa)[0]


def score_kernel(lengths_ref, p_ref, g00, g01, g10, g11, a0_ref, a1_ref, out_ref):
    width, tokens = g00.shape
    lane = lax.broadcasted_iota(jnp.int32, (1, tokens), 1)
    for b, (near, far, acts) in enumerate(((g00, g10, a0_ref), (g01, g11, a1_ref))):
        sums = jnp.zeros((1, tokens), f32)
        for member, grads in enumerate((near, far)):
            moved = dot(p_ref[member * width : (member + 1) * width, :], acts[...], ((1,), (1,)))
            sums = sums + jnp.sum(grads[...].astype(f32) * moved, axis=0, keepdims=True)
        for j, (start, finish) in enumerate(bounds_of(lengths_ref, b)):
            inside = (lane >= start) & (lane < finish)
            value = jnp.sum(jnp.where(inside, sums, 0.0), axis=1, keepdims=True)
            out_ref[b, j : j + 1, :] = jnp.broadcast_to(value, (1, out_ref.shape[2]))


def scores_of(lengths, precond, g00, g01, g10, g11, a0, a1):
    return local_call(
        score_kernel, [jax.ShapeDtypeStruct((2, lengths.shape[1], 128), f32)]
    )(lengths, precond, g00, g01, g10, g11, a0, a1)[0]


def routes(f):
    return [(c * 4 + m, f(c, m)[0] * 4 + f(c, m)[1]) for c in range(2) for m in range(4)]


OTHER_CORE = routes(lambda c, m: (1 - c, m))
GRADS_PARTNER = routes(lambda c, m: (c, m ^ 1))
ACTS_PARTNER = routes(lambda c, m: (c, 3 - m))
ACTS_SAME = routes(lambda c, m: (0, m) if c == 0 else (1, 3 - m))
ACTS_OTHER = routes(lambda c, m: (0, m) if c == 1 else (1, 3 - m))


def moved(array, pairs):
    return lax.ppermute(array, BLOCKS, pairs)


def over_partners(value):
    value = value + moved(value, GRADS_PARTNER)
    return value + moved(value, ACTS_PARTNER)


def shards(train_acts, train_grads, lengths, query_acts, query_grads, basis_in, basis_out):
    ring = lax.axis_index(RING)
    ring_size = lax.axis_size(RING)
    count = lengths.shape[0]

    acts = rotate(train_acts, basis_in)
    acts, train_grads = lax.optimization_barrier((acts, train_grads))
    a1 = moved(acts, ACTS_OTHER)
    a0 = moved(acts, ACTS_SAME)
    g00 = rotate_transposed(train_grads, basis_out)
    g00, query_acts, query_grads = lax.optimization_barrier((g00, query_acts, query_grads))
    g10 = moved(g00, GRADS_PARTNER)
    g01 = moved(g00, OTHER_CORE)
    g11 = moved(g10, OTHER_CORE)
    both = jnp.stack([lengths, moved(lengths, OTHER_CORE)])

    width, cols = g00.shape[0], a0.shape[1]
    chunk = 2 * width // ring_size
    inner = ring_size // 2
    qa = rotate(query_acts, basis_in)
    qg_own = rotate_transposed(query_grads, basis_out)
    qg_mine = lax.dynamic_slice_in_dim(qg_own, lax.rem(ring, inner) * chunk, chunk, 0)
    a1, qa, qg_mine = lax.optimization_barrier((a1, qa, qg_mine))
    qa = moved(qa, ACTS_OTHER)
    qg_far = moved(qg_mine, GRADS_PARTNER)
    qg = jnp.where(ring < inner, qg_mine, qg_far)

    curvature = curvature_of(both, g00, g01, g10, g11, a0, a1)
    parts = lax.all_to_all(curvature.reshape(ring_size, chunk, cols + 128), RING, 0, 0, tiled=True)
    total = jnp.sum(parts[:, 0, cols : cols + 3].astype(f32)).reshape(1, 1)
    total = over_partners(total + moved(total, OTHER_CORE))
    scale = 1.0 / (count * lax.axis_size(DP))
    entries = 2 * width * cols * 8
    damping = total * (DAMPING_RATIO * scale / entries)

    mine = precond_of(scale, damping, parts, qg, qa)
    precond = lax.all_to_all(mine, RING, 0, 0, tiled=True).reshape(2 * width, cols)
    found = scores_of(both, precond, g00, g01, g10, g11, a0, a1)
    found = over_partners(found[0] + moved(found[1], OTHER_CORE))
    return found[:, 0].reshape(1, count)


def solution(mesh):
    cut = Mesh(np.asarray(mesh.devices).reshape(4, 2, 4, 2, 4), ("x", "zl", "y", "c", "m"))
    return jax.shard_map(
        shards,
        mesh=cut,
        in_specs=(P(DP, None), P(DP, None), P(DP), P(), P(), P(None, "m"), P(None, "m")),
        out_specs=P(None, DP),
        check_vma=False,
    )
```

time: 743 us -> 155 us (0.21)
  waiting for transfers between devices: 580 us -> 49.3 us
  matrix products: 71.9 us -> 13.6 us
  starting transfers between devices: 0.04 us -> 46 us
  blocking collectives: 44 us -> 24.6 us
  other arithmetic: 20.8 us -> 1.5 us
  Pallas kernels: 0 us -> 14 us
  between operations: 16.6 us -> 2.85 us
    psum x1 -> x0, waiting for transfers between devices: 534 us -> none  [shards(): curvature = lax.psum(curvature_local, 'dp') * inverse_count]
    dot_general x9 -> x4, matrix products: 71.9 us -> 13.6 us  [dot(): lax.dot_general(a, b, (contract, ((), ())), preferred_element_type=f32)]
    all_gather x1 -> x0, waiting for transfers between devices: 45.8 us -> none  [shards(): lax.all_gather(acts_block, 'mp', axis=1, tiled=True)]
    ppermute x0 -> x14, waiting for transfers between devices: none -> 45.2 us  [moved(): return lax.ppermute(array, BLOCKS, pairs)]
    ppermute x0 -> x14, starting transfers between devices: none -> 38.5 us  [moved(): return lax.ppermute(array, BLOCKS, pairs)]
    all_gather x1 -> x0, blocking collectives: 24 us -> none  [shards(): lax.all_gather(query_block, 'mp', axis=1, tiled=True)]
    pallas_call x0 -> x3, Pallas kernels: none -> 14 us  [call(): pl.pallas_call(kernel, in_specs=[there] * scalars + [here] * (len(operand...]
    all_to_all x1, blocking collectives: 12.3 us -> 24.6 us  [shards(): lax.all_to_all(mine, RING, 0, 0, tiled=True).reshape(2 * width, cols)]
  transfers between devices with their start and end apart: 2 -> 15, of which waited for: 2 -> 9; matrix products, arithmetic and copies ran while one was open for 3% -> 4% of each run, Pallas kernels for 0% -> 0%
where the time goes in v2:
time: 155 us; the launch traced here: 154 us
  waiting for transfers between devices  49.3 us (32%)
  starting transfers between devices  46 us (30%)
  blocking collectives  24.6 us (16%)
  Pallas kernels  14 us (9%)
  matrix products  13.6 us (9%)
  between operations  2.85 us (2%)
  local copies, waits for them, and re-layouts  1.91 us (1%)
    ppermute x14, waiting for transfers between devices, moved(): return lax.ppermute(array, BLOCKS, pairs)  45.2 us
    ppermute x14, starting transfers between devices, moved(): return lax.ppermute(array, BLOCKS, pairs)  38.5 us
    all_to_all x1, blocking collectives, shards(): lax.all_to_all(mine, RING, 0, 0, tiled=True).reshape(2 * width, cols)  24.6 us
    pallas_call x3, Pallas kernels, call(): pl.pallas_call(kernel, in_specs=[there] * scalars + [here] * (len(operand...  14 us
    dot_general x4, matrix products, dot(): lax.dot_general(a, b, (contract, ((), ())), preferred_element_type=f32)  13.6 us
    all_to_all x1, starting transfers between devices, shards(): lax.all_to_all(curvature.reshape(ring_size, chunk, cols + 128), RING, 0,...  7.57 us
    all_to_all x1, waiting for transfers between devices, shards(): lax.all_to_all(curvature.reshape(ring_size, chunk, cols + 128), RING, 0,...  4.1 us
  transfers between devices with their start and end apart: 15, of which 9 were waited for; matrix products, arithmetic and copies ran while one was open for 4% of the time, Pallas kernels for 0%

profile of v2, /device:TPU:1, one launch (start us, length us, event | category | flops | bytes accessed | tf_op | source)
XLA Modules:
  0.0 153.8 jit_solution(3451321091529065036)
XLA Ops:
  0.0 0.0 copy-start
  0.0 0.0 copy-start.4
  0.0 5.9 %convolution_convert_fusion.1 = bf16[512,640]{1,0:T(8,128)(2,1)} fusion(bf16[512,2560]{1,0:T(8,128)(2,1)} %param.7, bf16[2560,640]{1,0:T(8,128)(2,1)} %param.12), kind=kOutput, calls=%fused_computation.1 | convolution fusion | flops 1678049280 | bytes 6553600 | tf_op jit(solution)/shard_map/dot_general | solution.py:27
  5.9 0.0 copy-done
  5.9 0.0 copy-done.4
  5.9 0.0 copy-start.3
  5.9 0.0 copy-start.2
  5.9 2.8 %fusion.g00 = bf16[640,512]{1,0:T(8,128)(2,1)} fusion(bf16[512,2560]{1,0:T(8,128)(2,1)S(1)} %copy-done.4, bf16[2560,640]{1,0:T(8,128)(2,1)S(1)} %copy-done), kind=kOutput, calls=%fused_computation.2 | convolution fusion | flops 1678049280 | bytes 6553600 | tf_op jit(solution)/shard_map/dot_general | solution.py:27
  8.7 3.8 %collective-permute-start.2 = (bf16[640,512]{1,0:T(8,128)(2,1)}, bf16[640,512]{1,0:T(8,128)(2,1)}, u32[]{:S(2)}, u32[]{:S(2)}) collective-permute-start(bf16[640,512]{1,0:T(8,128)(2,1)} %fusion.g00), channel_id=1, source_target_pairs={{0,1},{1,0},{2,3},{3,2},{4,5},{5,4},{6,7},{7,6},{8,9},{9,8},{10,11... | collective-permute-start | bytes 1966088 | tf_op jit(solution)/shard_map/ppermute | solution.py:188
  12.5 1.0 collective-permute-start.1
  13.5 0.0 collective-permute-start.5
  13.5 6.1 %collective-permute-start.4 = (bf16[512,640]{1,0:T(8,128)(2,1)}, bf16[512,640]{1,0:T(8,128)(2,1)}, u32[]{:S(2)}, u32[]{:S(2)}) collective-permute-start(bf16[512,640]{1,0:T(8,128)(2,1)} %convolution_convert_fusion.1), channel_id=1, source_target_pairs={{0,0},{1,1},{2,2},{3,3},{4,7},{5,6},{6,5},{7,4},{8,8},{9,9},{10,10... | collective-permute-start | bytes 1966088 | tf_op jit(solution)/shard_map/ppermute | solution.py:188
  19.6 0.0 copy-done.3
  19.6 5.0 %collective-permute-start = (s32[4]{0:T(128)S(1)}, s32[4]{0:T(128)S(1)}, u32[]{:S(2)}, u32[]{:S(2)}) collective-permute-start(s32[4]{0:T(128)S(1)} %copy-done.3), channel_id=1, source_target_pairs={{0,4},{1,5},{2,6},{3,7},{4,0},{5,1},{6,2},{7,3},{8,12},{9,13},{10,... | collective-permute-start | bytes 56 | tf_op jit(solution)/shard_map/ppermute | solution.py:188
  24.6 16.2 %collective-permute-done.2.g10 = bf16[640,512]{1,0:T(8,128)(2,1)} collective-permute-done((bf16[640,512]{1,0:T(8,128)(2,1)}, bf16[640,512]{1,0:T(8,128)(2,1)}, u32[]{:S(2)}, u32[]{:S(2)}) %collective-permute-start.2) | collective-permute-done | bytes 655392 | tf_op jit(solution)/shard_map/ppermute | solution.py:188
  40.7 2.0 %collective-permute-start.3 = (bf16[640,512]{1,0:T(8,128)(2,1)}, bf16[640,512]{1,0:T(8,128)(2,1)}, u32[]{:S(2)}, u32[]{:S(2)}) collective-permute-start(bf16[640,512]{1,0:T(8,128)(2,1)} %collective-permute-done.2.g10), channel_id=1, source_target_pairs={{0,4},{1,5},{2,6},{3,7},{4,0},{5,1},{6,2},{7,3},{8,12},{9,13},{10,... | collective-permute-start | bytes 1966088 | tf_op jit(solution)/shard_map/ppermute | solution.py:188
  42.7 0.0 copy-done.2
  42.7 1.4 fusion.4
  44.2 3.5 %convolution_convert_fusion.2 = bf16[128,640]{1,0:T(8,128)(2,1)} fusion(bf16[128,2560]{1,0:T(8,128)(2,1)} %param.10, bf16[2560,640]{1,0:T(8,128)(2,1)} %param.12), kind=kOutput, calls=%fused_computation.3 | convolution fusion | flops 419512320 | bytes 4096000 | tf_op jit(solution)/shard_map/dot_general | solution.py:27
  47.7 0.0 collective-permute-done
  47.7 0.0 collective-permute-done.5.a1_ref
  47.7 0.0 collective-permute-done.1.g01
  47.7 0.0 collective-permute-done.4.a0_ref
  47.7 0.0 collective-permute-done.3.g11
  47.7 7.7 %shard_map.73 = bf16[1280,768]{1,0:T(8,128)(2,1)S(1)} custom-call(s32[2,4]{1,0:T(2,128)S(1)} %pad_add_fusion.lengths_ref, bf16[640,512]{1,0:T(8,128)(2,1)} %fusion.g00, bf16[640,512]{1,0:T(8,128)(2,1)} %collective-permute-done.1.g01, bf16[640,512]{1,0:T(8,128)(2,1)} %collective-permute-done.2.g10, bf16[640,512]{1,0:T(8,128)(2,1)} %collective-permute-done.3.g11, ...), custom_call_target="tpu_custom_call" | custom-call | tf_op jit(solution)/shard_map/pallas_call | solution.py:46
  55.4 0.0 copy-start.1
  55.4 1.2 copy-done.1
  56.7 7.6 %all-to-all-start = ((bf16[32,40,768]{2,1,0:T(8,128)(2,1)}), bf16[32,40,768]{2,1,0:T(8,128)(2,1)}, u32[]{:S(2)}, u32[]{:S(2)}) async-start(bf16[32,40,768]{2,1,0:T(8,128)(2,1)} %bitcast.24), calls=%async_computation | async-start | bytes 3932160 | tf_op jit(solution)/shard_map/all_to_all | solution.py:224
  64.2 2.9 %collective-permute-start.9 = (bf16[40,128]{1,0:T(8,128)(2,1)S(1)}, bf16[40,128]{1,0:T(8,128)(2,1)S(1)}, u32[]{:S(2)}, u32[]{:S(2)}) collective-permute-start(bf16[40,128]{1,0:T(8,128)(2,1)S(1)} %fusion.2), channel_id=1, source_target_pairs={{0,1},{1,0},{2,3},{3,2},{4,5},{5,4},{6,7},{7,6},{8,9},{9,8},{10,11... | collective-permute-start | bytes 30728 | tf_op jit(solution)/shard_map/ppermute | solution.py:188
  67.1 0.5 collective-permute-start.10
  67.6 22.9 %collective-permute-done.9 = bf16[40,128]{1,0:T(8,128)(2,1)S(1)} collective-permute-done((bf16[40,128]{1,0:T(8,128)(2,1)S(1)}, bf16[40,128]{1,0:T(8,128)(2,1)S(1)}, u32[]{:S(2)}, u32[]{:S(2)}) %collective-permute-start.9) | collective-permute-done | bytes 10272 | tf_op jit(solution)/shard_map/ppermute | solution.py:188
  90.5 4.1 %all-to-all-done.parts_ref = bf16[32,40,768]{2,1,0:T(8,128)(2,1)} async-done(((bf16[32,40,768]{2,1,0:T(8,128)(2,1)}), bf16[32,40,768]{2,1,0:T(8,128)(2,1)}, u32[]{:S(2)}, u32[]{:S(2)}) %all-to-all-start) | async-done | bytes 1966112 | tf_op jit(solution)/shard_map/all_to_all | solution.py:224
  94.6 1.5 fusion.1
  96.1 0.7 collective-permute-start.6
  96.8 1.0 collective-permute-done.6
  99.1 3.4 %collective-permute-start.7 = (f32[1,1]{1,0:T(1,128)}, f32[1,1]{1,0:T(1,128)}, u32[]{:S(2)}, u32[]{:S(2)}) collective-permute-start(f32[1,1]{1,0:T(1,128)} %add.30), channel_id=1, source_target_pairs={{0,1},{1,0},{2,3},{3,2},{4,5},{5,4},{6,7},{7,6},{8,9},{9,8},{10,11... | collective-permute-start | bytes 20 | tf_op jit(solution)/shard_map/ppermute | solution.py:188
  102.4 0.3 collective-permute-done.7
  103.4 5.4 %collective-permute-start.8 = (f32[1,1]{1,0:T(1,128)}, f32[1,1]{1,0:T(1,128)}, u32[]{:S(2)}, u32[]{:S(2)}) collective-permute-start(f32[1,1]{1,0:T(1,128)} %add.31), channel_id=1, source_target_pairs={{0,3},{1,2},{2,1},{3,0},{4,7},{5,6},{6,5},{7,4},{8,11},{9,10},{10,... | collective-permute-start | bytes 20 | tf_op jit(solution)/shard_map/ppermute | solution.py:188
  108.8 0.3 collective-permute-done.8
  109.8 0.0 collective-permute-done.10.qa_ref
  109.8 1.9 %shard_map.74 = bf16[32,40,640]{2,1,0:T(8,128)(2,1)S(1)} custom-call(f32[1,1]{1,0:T(1,128)S(6)} %mul.15.damping_ref, bf16[32,40,768]{2,1,0:T(8,128)(2,1)} %all-to-all-done.parts_ref, bf16[40,128]{1,0:T(8,128)(2,1)S(1)} %broadcast_select_fusion.qg_ref, bf16[128,640]{1,0:T(8,128)(2,1)S(1)} %collective-permute-done.10.qa_ref), custom_call_target="tpu_custom_call" | custom-call | tf_op jit(solution)/shard_map/pallas_call | solution.py:46
  111.7 24.6 %all_to_all.10 = bf16[32,40,640]{2,1,0:T(8,128)(2,1)S(1)} all-to-all(bf16[32,40,640]{2,1,0:T(8,128)(2,1)S(1)} %shard_map.74), channel_id=1, replica_groups=mesh['x'=4,'zl'=2,'y'=4,'c'=2,'m'=4] {'x','zl','y'}, dimensions={0} | all-to-all | bytes 3276800 | tf_op jit(solution)/shard_map/all_to_all | solution.py:232
  136.3 4.5 %shard_map.75 = f32[2,4,128]{2,1,0:T(4,128)S(1)} custom-call(s32[2,4]{1,0:T(2,128)S(1)} %pad_add_fusion.lengths_ref, bf16[1280,640]{1,0:T(8,128)(2,1)S(1)} %bitcast.25, bf16[640,512]{1,0:T(8,128)(2,1)} %fusion.g00, bf16[640,512]{1,0:T(8,128)(2,1)} %collective-permute-done.1.g01, bf16[640,512]{1,0:T(8,128)(2,1)} %collective-permute-done.2.g10, ...), custom_call_target="tpu_custom_call" | custom-call | tf_op jit(solution)/shard_map/pallas_call | solution.py:46
  140.8 3.7 %collective-permute-start.11 = (f32[4,128]{1,0:T(4,128)S(1)}, f32[4,128]{1,0:T(4,128)S(1)}, u32[]{:S(2)}, u32[]{:S(2)}) collective-permute-start(f32[4,128]{1,0:T(4,128)S(1)} %slice_bitcast_fusion), channel_id=1, source_target_pairs={{0,4},{1,5},{2,6},{3,7},{4,0},{5,1},{6,2},{7,3},{8,12},{9,13},{10,... | collective-permute-start | bytes 6152 | tf_op jit(solution)/shard_map/ppermute | solution.py:188
  144.5 0.8 collective-permute-done.11
  145.3 1.0 collective-permute-start.12
  146.3 2.3 %collective-permute-done.12 = f32[4,128]{1,0:T(4,128)S(1)} collective-permute-done((f32[4,128]{1,0:T(4,128)S(1)}, f32[4,128]{1,0:T(4,128)S(1)}, u32[]{:S(2)}, u32[]{:S(2)}) %collective-permute-start.12) | collective-permute-done | bytes 2080 | tf_op jit(solution)/shard_map/ppermute | solution.py:188
  148.6 3.1 %collective-permute-start.13 = (f32[4,128]{1,0:T(4,128)S(1)}, f32[4,128]{1,0:T(4,128)S(1)}, u32[]{:S(2)}, u32[]{:S(2)}) collective-permute-start(f32[4,128]{1,0:T(4,128)S(1)} %add.34), channel_id=1, source_target_pairs={{0,3},{1,2},{2,1},{3,0},{4,7},{5,6},{6,5},{7,4},{8,11},{9,10},{10,... | collective-permute-start | bytes 6152 | tf_op jit(solution)/shard_map/ppermute | solution.py:188
  151.7 1.5 collective-permute-done.13
  153.2 0.6 slice_reduce_fusion
  (7 shorter events, 0.0 us)
Async XLA Ops:
  0.0 5.9 %copy-start = (bf16[2560,640]{1,0:T(8,128)(2,1)S(1)}, bf16[2560,640]{1,0:T(8,128)(2,1)}, u32[]{:S(2)}) copy-start(bf16[2560,640]{1,0:T(8,128)(2,1)} %param.13) | copy-start | bytes 9830404
  0.0 5.9 %copy-start.4 = (bf16[512,2560]{1,0:T(8,128)(2,1)S(1)}, bf16[512,2560]{1,0:T(8,128)(2,1)}, u32[]{:S(2)}) copy-start(bf16[512,2560]{1,0:T(8,128)(2,1)} %param.8) | copy-start | bytes 7864324
  5.9 13.7 %copy-start.3 = (s32[4]{0:T(128)S(1)}, s32[4]{0:T(128)}, u32[]{:S(2)}) copy-start(s32[4]{0:T(128)} %param.9) | copy-start | bytes 52
  5.9 36.8 %copy-start.2 = (bf16[128,2560]{1,0:T(8,128)(2,1)S(1)}, bf16[128,2560]{1,0:T(8,128)(2,1)}, u32[]{:S(2)}) copy-start(bf16[128,2560]{1,0:T(8,128)(2,1)} %param.11) | copy-start | bytes 1966084
  8.7 32.0 %collective-permute-start.2 = (bf16[640,512]{1,0:T(8,128)(2,1)}, bf16[640,512]{1,0:T(8,128)(2,1)}, u32[]{:S(2)}, u32[]{:S(2)}) collective-permute-start(bf16[640,512]{1,0:T(8,128)(2,1)} %fusion.g00), channel_id=1, source_target_pairs={{0,1},{1,0},{2,3},{3,2},{4,5},{5,4},{6,7},{7,6},{8,9},{9,8},{10,11... | collective-permute-start | bytes 1966088 | tf_op jit(solution)/shard_map/ppermute | solution.py:188
  12.5 35.2 %collective-permute-start.1 = (bf16[640,512]{1,0:T(8,128)(2,1)}, bf16[640,512]{1,0:T(8,128)(2,1)}, u32[]{:S(2)}, u32[]{:S(2)}) collective-permute-start(bf16[640,512]{1,0:T(8,128)(2,1)} %fusion.g00), channel_id=1, source_target_pairs={{0,4},{1,5},{2,6},{3,7},{4,0},{5,1},{6,2},{7,3},{8,12},{9,13},{10,... | collective-permute-start | bytes 1966088 | tf_op jit(solution)/shard_map/ppermute | solution.py:188
  13.5 34.2 %collective-permute-start.5 = (bf16[512,640]{1,0:T(8,128)(2,1)}, bf16[512,640]{1,0:T(8,128)(2,1)}, u32[]{:S(2)}, u32[]{:S(2)}) collective-permute-start(bf16[512,640]{1,0:T(8,128)(2,1)} %convolution_convert_fusion.1), channel_id=1, source_target_pairs={{0,7},{1,6},{2,5},{3,4},{4,0},{5,1},{6,2},{7,3},{8,15},{9,14},{10,... | collective-permute-start | bytes 1966088 | tf_op jit(solution)/shard_map/ppermute | solution.py:188
  13.5 34.2 %collective-permute-start.4 = (bf16[512,640]{1,0:T(8,128)(2,1)}, bf16[512,640]{1,0:T(8,128)(2,1)}, u32[]{:S(2)}, u32[]{:S(2)}) collective-permute-start(bf16[512,640]{1,0:T(8,128)(2,1)} %convolution_convert_fusion.1), channel_id=1, source_target_pairs={{0,0},{1,1},{2,2},{3,3},{4,7},{5,6},{6,5},{7,4},{8,8},{9,9},{10,10... | collective-permute-start | bytes 1966088 | tf_op jit(solution)/shard_map/ppermute | solution.py:188
  19.6 28.1 %collective-permute-start = (s32[4]{0:T(128)S(1)}, s32[4]{0:T(128)S(1)}, u32[]{:S(2)}, u32[]{:S(2)}) collective-permute-start(s32[4]{0:T(128)S(1)} %copy-done.3), channel_id=1, source_target_pairs={{0,4},{1,5},{2,6},{3,7},{4,0},{5,1},{6,2},{7,3},{8,12},{9,13},{10,... | collective-permute-start | bytes 56 | tf_op jit(solution)/shard_map/ppermute | solution.py:188
  40.7 7.0 %collective-permute-start.3 = (bf16[640,512]{1,0:T(8,128)(2,1)}, bf16[640,512]{1,0:T(8,128)(2,1)}, u32[]{:S(2)}, u32[]{:S(2)}) collective-permute-start(bf16[640,512]{1,0:T(8,128)(2,1)} %collective-permute-done.2.g10), channel_id=1, source_target_pairs={{0,4},{1,5},{2,6},{3,7},{4,0},{5,1},{6,2},{7,3},{8,12},{9,13},{10,... | collective-permute-start | bytes 1966088 | tf_op jit(solution)/shard_map/ppermute | solution.py:188
  55.4 1.3 copy-start.1
  56.7 38.0 %all-to-all-start = ((bf16[32,40,768]{2,1,0:T(8,128)(2,1)}), bf16[32,40,768]{2,1,0:T(8,128)(2,1)}, u32[]{:S(2)}, u32[]{:S(2)}) async-start(bf16[32,40,768]{2,1,0:T(8,128)(2,1)} %bitcast.24), calls=%async_computation | async-start | bytes 3932160 | tf_op jit(solution)/shard_map/all_to_all | solution.py:224
  64.2 26.3 %collective-permute-start.9 = (bf16[40,128]{1,0:T(8,128)(2,1)S(1)}, bf16[40,128]{1,0:T(8,128)(2,1)S(1)}, u32[]{:S(2)}, u32[]{:S(2)}) collective-permute-start(bf16[40,128]{1,0:T(8,128)(2,1)S(1)} %fusion.2), channel_id=1, source_target_pairs={{0,1},{1,0},{2,3},{3,2},{4,5},{5,4},{6,7},{7,6},{8,9},{9,8},{10,11... | collective-permute-start | bytes 30728 | tf_op jit(solution)/shard_map/ppermute | solution.py:188
  67.1 42.7 %collective-permute-start.10 = (bf16[128,640]{1,0:T(8,128)(2,1)}, bf16[128,640]{1,0:T(8,128)(2,1)S(1)}, u32[]{:S(2)}, u32[]{:S(2)}) collective-permute-start(bf16[128,640]{1,0:T(8,128)(2,1)} %convolution_convert_fusion.2), channel_id=1, source_target_pairs={{0,7},{1,6},{2,5},{3,4},{4,0},{5,1},{6,2},{7,3},{8,15},{9,14},{10,... | collective-permute-start | bytes 491528 | tf_op jit(solution)/shard_map/ppermute | solution.py:188
  96.1 1.6 %collective-permute-start.6 = (f32[1,1]{1,0:T(1,128)}, f32[1,1]{1,0:T(1,128)}, u32[]{:S(2)}, u32[]{:S(2)}) collective-permute-start(f32[1,1]{1,0:T(1,128)} %bitcast.5), channel_id=1, source_target_pairs={{0,4},{1,5},{2,6},{3,7},{4,0},{5,1},{6,2},{7,3},{8,12},{9,13},{10,... | collective-permute-start | bytes 20 | tf_op jit(solution)/shard_map/ppermute | solution.py:188
  99.1 3.7 %collective-permute-start.7 = (f32[1,1]{1,0:T(1,128)}, f32[1,1]{1,0:T(1,128)}, u32[]{:S(2)}, u32[]{:S(2)}) collective-permute-start(f32[1,1]{1,0:T(1,128)} %add.30), channel_id=1, source_target_pairs={{0,1},{1,0},{2,3},{3,2},{4,5},{5,4},{6,7},{7,6},{8,9},{9,8},{10,11... | collective-permute-start | bytes 20 | tf_op jit(solution)/shard_map/ppermute | solution.py:188
  103.4 5.7 %collective-permute-start.8 = (f32[1,1]{1,0:T(1,128)}, f32[1,1]{1,0:T(1,128)}, u32[]{:S(2)}, u32[]{:S(2)}) collective-permute-start(f32[1,1]{1,0:T(1,128)} %add.31), channel_id=1, source_target_pairs={{0,3},{1,2},{2,1},{3,0},{4,7},{5,6},{6,5},{7,4},{8,11},{9,10},{10,... | collective-permute-start | bytes 20 | tf_op jit(solution)/shard_map/ppermute | solution.py:188
  140.8 4.5 %collective-permute-start.11 = (f32[4,128]{1,0:T(4,128)S(1)}, f32[4,128]{1,0:T(4,128)S(1)}, u32[]{:S(2)}, u32[]{:S(2)}) collective-permute-start(f32[4,128]{1,0:T(4,128)S(1)} %slice_bitcast_fusion), channel_id=1, source_target_pairs={{0,4},{1,5},{2,6},{3,7},{4,0},{5,1},{6,2},{7,3},{8,12},{9,13},{10,... | collective-permute-start | bytes 6152 | tf_op jit(solution)/shard_map/ppermute | solution.py:188
  145.3 3.3 %collective-permute-start.12 = (f32[4,128]{1,0:T(4,128)S(1)}, f32[4,128]{1,0:T(4,128)S(1)}, u32[]{:S(2)}, u32[]{:S(2)}) collective-permute-start(f32[4,128]{1,0:T(4,128)S(1)} %fusion.3), channel_id=1, source_target_pairs={{0,1},{1,0},{2,3},{3,2},{4,5},{5,4},{6,7},{7,6},{8,9},{9,8},{10,11... | collective-permute-start | bytes 6152 | tf_op jit(solution)/shard_map/ppermute | solution.py:188
  148.6 4.5 %collective-permute-start.13 = (f32[4,128]{1,0:T(4,128)S(1)}, f32[4,128]{1,0:T(4,128)S(1)}, u32[]{:S(2)}, u32[]{:S(2)}) collective-permute-start(f32[4,128]{1,0:T(4,128)S(1)} %add.34), channel_id=1, source_target_pairs={{0,3},{1,2},{2,1},{3,0},{4,7},{5,6},{6,5},{7,4},{8,11},{9,10},{10,... | collective-permute-start | bytes 6152 | tf_op jit(solution)/shard_map/ppermute | solution.py:188

commit v3 on v2

--- a/solution.py
+++ b/solution.py
@@ -71,68 +71,113 @@
     return chosen
 
 
-def curvature_kernel(rt, lengths_ref, g00, g01, g10, g11, a0_ref, a1_ref, out_ref, masked, wide):
-    acts = (a0_ref, a1_ref)
-    tokens, cols = a0_ref.shape
-    width = g00.shape[0]
+def block_curvature(grads, places, masked, wide, finished):
+    total = None
+    for b in range(2):
+        product = dot(grads[b][...], wide[b], ((1,), (0,)))
+        total = product * product if total is None else total + product * product
+    for b, slot, at in places:
+        product = dot(grads[b][:, pl.ds(at, HALF)], masked[slot], ((1,), (0,)))
+        total = total + product * product
+    finished[...] = total.astype(bf16)
+    return jnp.sum(total, axis=0, keepdims=True)
+
+
+def places_of(lengths_ref):
     count = lengths_ref.shape[1]
-    row = lax.broadcasted_iota(jnp.int32, (HALF, 1), 0)
-    rows = lax.broadcasted_iota(jnp.int32, (tokens, 1), 0)
-    places = []
+    wides, places = [], []
     for b in range(2):
         bounds = bounds_of(lengths_ref, b)
         starts, ends = [v[0] for v in bounds], [v[1] for v in bounds]
         across = jnp.int32(count - 1)
         for j, (start, finish) in enumerate(bounds):
             across = jnp.where((start < HALF) & (finish > HALF), j, across)
-        inside = (rows >= pick(across, starts)) & (rows < pick(across, ends))
-        wide[b] = jnp.where(inside, acts[b][...], jnp.zeros((tokens, cols), bf16))
+        wides.append((pick(across, starts), pick(across, ends)))
         for k in range(count - 1):
             which = k + (k >= across).astype(jnp.int32)
-            start, finish = pick(which, starts), pick(which, ends)
-            base = jnp.where(start >= HALF, HALF, 0)
-            at = pl.multiple_of(base, HALF)
-            inside = (row + base >= start) & (row + base < finish)
-            window = acts[b][pl.ds(at, HALF), :]
-            masked[b * (count - 1) + k] = jnp.where(inside, window, jnp.zeros_like(window))
-            places.append((b, b * (count - 1) + k, at))
-
-    sums = jnp.zeros((1, cols), f32)
-    for member, grads in enumerate(((g00, g01), (g10, g11))):
-
-        def body(i, sums, member=member, grads=grads):
-            r = pl.multiple_of(i * rt, rt)
-            total = None
-            for b in range(2):
-                product = dot(grads[b][pl.ds(r, rt), :], wide[b], ((1,), (0,)))
-                total = product * product if total is None else total + product * product
-            for b, slot, at in places:
-                product = dot(grads[b][pl.ds(r, rt), pl.ds(at, HALF)], masked[slot], ((1,), (0,)))
-                total = total + product * product
-            out_ref[pl.ds(member * width + r, rt), 0:cols] = total.astype(bf16)
-            return sums + jnp.sum(total, axis=0, keepdims=True)
-
-        sums = lax.fori_loop(0, width // rt, body, sums)
+            start = pick(which, starts)
+            at = pl.multiple_of(jnp.where(start >= HALF, HALF, 0), HALF)
+            places.append((b, b * (count - 1) + k, at, start, pick(which, ends)))
+    return wides, places
+
+
+def near_kernel(lengths_ref, g00, g01, a0_ref, a1_ref, out_hbm, masked, wide, sums_ref, finished, sem):
+    acts = (a0_ref, a1_ref)
+    tokens, cols = a0_ref.shape
+    row = lax.broadcasted_iota(jnp.int32, (HALF, 1), 0)
+    rows = lax.broadcasted_iota(jnp.int32, (tokens, 1), 0)
+    wides, places = places_of(lengths_ref)
+    for b, (start, finish) in enumerate(wides):
+        inside = (rows >= start) & (rows < finish)
+        wide[b] = jnp.where(inside, acts[b][...], jnp.zeros((tokens, cols), bf16))
+    for b, slot, at, start, finish in places:
+        inside = (row + at >= start) & (row + at < finish)
+        window = acts[b][pl.ds(at, HALF), :]
+        masked[slot] = jnp.where(inside, window, jnp.zeros_like(window))
+    sums_ref[...] = block_curvature((g00, g01), [p[:3] for p in places], masked, wide, finished)
+    width = finished.shape[0]
+    copy = pltpu.make_async_copy(finished, out_hbm.at[0:width, 0:cols], sem)
+    copy.start()
+    copy.wait()
+
+
+def far_kernel(lengths_ref, _, g10, g11, masked, wide, sums_ref, out_hbm, finished, terms_ref, sems):
+    places = places_of(lengths_ref)[1]
+    sums = sums_ref[...] + block_curvature((g10, g11), [p[:3] for p in places], masked, wide, finished)
+    width, cols = finished.shape
+    copy = pltpu.make_async_copy(finished, out_hbm.at[width : 2 * width, 0:cols], sems.at[0])
+    copy.start()
     total = jnp.sum(sums, axis=1, keepdims=True)
-    high = total.astype(bf16)
-    rest = total - high.astype(f32)
-    middle = rest.astype(bf16)
-    low = (rest - middle.astype(f32)).astype(bf16)
+    high = total.astype(bf16).astype(f32)
+    middle = (total - high).astype(bf16).astype(f32)
+    low = total - high - middle
     lane = lax.broadcasted_iota(jnp.int32, (1, 128), 1)
-    terms = jnp.where(lane == 0, high.astype(f32), jnp.where(lane == 1, middle.astype(f32), low.astype(f32)))
-    terms = jnp.where(lane < 3, terms, 0.0)
-    out_ref[:, cols:] = jnp.broadcast_to(terms, (out_ref.shape[0], 128)).astype(bf16)
-
-
-def curvature_of(lengths, g00, g01, g10, g11, a0, a1):
+    terms = jnp.where(lane == 0, high, jnp.where(lane == 1, middle, jnp.where(lane == 2, low, 0.0)))
+    terms_ref[...] = jnp.broadcast_to(terms, terms_ref.shape).astype(bf16)
+    also = pltpu.make_async_copy(terms_ref, out_hbm.at[:, cols : cols + 128], sems.at[1])
+    also.start()
+    copy.wait()
+    also.wait()
+
+
+def near_curvature(lengths, g00, g01, a0, a1):
     width = g00.shape[0]
     tokens, cols = a0.shape
-    count = lengths.shape[1]
-    return local_call(
-        functools.partial(curvature_kernel, width),
-        [jax.ShapeDtypeStruct((2 * width, cols + 128), bf16)],
-        [pltpu.VMEM((2 * (count - 1), HALF, cols), bf16), pltpu.VMEM((2, tokens, cols), bf16)],
-    )(lengths, g00, g01, g10, g11, a0, a1)[0]
+    others = 2 * (lengths.shape[1] - 1)
+    here = pl.BlockSpec(memory_space=pltpu.VMEM)
+    return pl.pallas_call(
+        near_kernel,
+        in_specs=[pl.BlockSpec(memory_space=pltpu.SMEM)] + [here] * 4,
+        out_specs=[pl.BlockSpec(memory_space=pltpu.HBM), here, here, here],
+        out_shape=[
+            pltpu.HBM((2 * width, cols + 128), bf16),
+            jax.ShapeDtypeStruct((others, HALF, cols), bf16),
+            jax.ShapeDtypeStruct((2, tokens, cols), bf16),
+            jax.ShapeDtypeStruct((1, cols), f32),
+        ],
+        scratch_shapes=[pltpu.VMEM((width, cols), bf16), pltpu.SemaphoreType.DMA],
+        compiler_params=params(),
+    )(lengths, *in_vmem(g00, g01, a0, a1))
+
+
+def far_curvature(lengths, started, g10, g11, masked, wide, sums):
+    width = g10.shape[0]
+    cols = sums.shape[1]
+    here = pl.BlockSpec(memory_space=pltpu.VMEM)
+    anywhere = pl.BlockSpec(memory_space=pltpu.HBM)
+    return pl.pallas_call(
+        far_kernel,
+        in_specs=[pl.BlockSpec(memory_space=pltpu.SMEM), anywhere] + [here] * 5,
+        out_specs=anywhere,
+        out_shape=pltpu.HBM(started.shape, started.dtype),
+        input_output_aliases={1: 0},
+        scratch_shapes=[
+            pltpu.VMEM((width, cols), bf16),
+            pltpu.VMEM((2 * width, 128), bf16),
+            pltpu.SemaphoreType.DMA((2,)),
+        ],
+        compiler_params=params(),
+    )(lengths, started, *in_vmem(g10, g11, masked, wide, sums))
 
 
 def precond_kernel(scale, damping_ref, parts_ref, qg_ref, qa_ref, out_ref):
@@ -206,7 +251,6 @@
     g00, query_acts, query_grads = lax.optimization_barrier((g00, query_acts, query_grads))
     g10 = moved(g00, GRADS_PARTNER)
     g01 = moved(g00, OTHER_CORE)
-    g11 = moved(g10, OTHER_CORE)
     both = jnp.stack([lengths, moved(lengths, OTHER_CORE)])
 
     width, cols = g00.shape[0], a0.shape[1]
@@ -215,12 +259,15 @@
     qa = rotate(query_acts, basis_in)
     qg_own = rotate_transposed(query_grads, basis_out)
     qg_mine = lax.dynamic_slice_in_dim(qg_own, lax.rem(ring, inner) * chunk, chunk, 0)
-    a1, qa, qg_mine = lax.optimization_barrier((a1, qa, qg_mine))
+    g10, qa, qg_mine = lax.optimization_barrier((g10, qa, qg_mine))
+    g11 = moved(g10, OTHER_CORE)
     qa = moved(qa, ACTS_OTHER)
     qg_far = moved(qg_mine, GRADS_PARTNER)
+
+    started, masked, wide, sums = near_curvature(both, g00, g01, a0, a1)
+    g11, qa, qg_far = lax.optimization_barrier((g11, qa, qg_far))
     qg = jnp.where(ring < inner, qg_mine, qg_far)
-
-    curvature = curvature_of(both, g00, g01, g10, g11, a0, a1)
+    curvature = far_curvature(both, started, g10, g11, masked, wide, sums)
     parts = lax.all_to_all(curvature.reshape(ring_size, chunk, cols + 128), RING, 0, 0, tiled=True)
     total = jnp.sum(parts[:, 0, cols : cols + 3].astype(f32)).reshape(1, 1)
     total = over_partners(total + moved(total, OTHER_CORE))

time: 155 us -> 157 us (1.013)
  waiting for transfers between devices: 49.3 us -> 53.3 us
  starting transfers between devices: 46 us -> 42.4 us
  Pallas kernels: 14 us -> 16.8 us
    all_to_all x1, waiting for transfers between devices: 4.1 us -> 23.8 us  [shards(): lax.all_to_all(curvature.reshape(ring_size, chunk, cols + 128), RING, 0,...]
    ppermute x14, waiting for transfers between devices: 45.2 us -> 29.5 us  [moved(): return lax.ppermute(array, BLOCKS, pairs)]
    pallas_call x0 -> x2, Pallas kernels: none -> 10.6 us  [the longest x1 5.51 us: near_curvature(): pl.pallas_call(near_kernel, in_specs=[pl.BlockSpec(memory_space=pltpu.SME...]
    pallas_call x3 -> x2, Pallas kernels: 14 us -> 6.2 us  [call(): pl.pallas_call(kernel, in_specs=[there] * scalars + [here] * (len(operand...]
    ppermute x14, starting transfers between devices: 38.5 us -> 33.8 us  [moved(): return lax.ppermute(array, BLOCKS, pairs)]
  transfers between devices with their start and end apart: 15 -> 15, of which waited for: 9 -> 11; matrix products, arithmetic and copies ran while one was open for 4% -> 3% of each run, Pallas kernels for 0% -> 4%
where the time goes in v3:
time: 157 us; the launch traced here: 156 us
  waiting for transfers between devices  53.3 us (34%)
  starting transfers between devices  42.4 us (27%)
  blocking collectives  23.8 us (15%)
  Pallas kernels  16.8 us (11%)
  matrix products  12.3 us (8%)
  between operations  2.86 us (2%)
  local copies, waits for them, and re-layouts  2.59 us (2%)
    ppermute x14, starting transfers between devices, moved(): return lax.ppermute(array, BLOCKS, pairs)  33.8 us
    ppermute x14, waiting for transfers between devices, moved(): return lax.ppermute(array, BLOCKS, pairs)  29.5 us
    all_to_all x1, blocking collectives, shards(): lax.all_to_all(mine, RING, 0, 0, tiled=True).reshape(2 * width, cols)  23.8 us
    all_to_all x1, waiting for transfers between devices, shards(): lax.all_to_all(curvature.reshape(ring_size, chunk, cols + 128), RING, 0,...  23.8 us
    dot_general x4, matrix products, dot(): lax.dot_general(a, b, (contract, ((), ())), preferred_element_type=f32)  12.3 us
    all_to_all x1, starting transfers between devices, shards(): lax.all_to_all(curvature.reshape(ring_size, chunk, cols + 128), RING, 0,...  8.62 us
    pallas_call x2, Pallas kernels, call(): pl.pallas_call(kernel, in_specs=[there] * scalars + [here] * (len(operand...  6.2 us
    pallas_call x1, Pallas kernels, near_curvature(): pl.pallas_call(near_kernel, in_specs=[pl.BlockSpec(memory_space=pltpu.SME...  5.51 us
  transfers between devices with their start and end apart: 15, of which 11 were waited for; matrix products, arithmetic and copies ran while one was open for 3% of the time, Pallas kernels for 4%

profile of v3, /device:TPU:1, one launch (start us, length us, event | category | flops | bytes accessed | tf_op | source)
XLA Modules:
  0.0 155.7 jit_solution(16195247119966046543)
XLA Ops:
  0.0 0.0 copy-start
  0.0 0.0 copy-start.7
  0.0 0.0 copy-start.3
  0.0 1.9 %copy-done = bf16[2560,640]{1,0:T(8,128)(2,1)S(1)} copy-done((bf16[2560,640]{1,0:T(8,128)(2,1)S(1)}, bf16[2560,640]{1,0:T(8,128)(2,1)}, u32[]{:S(2)}) %copy-start) | copy-done | bytes 3276824
  1.9 5.5 %convolution_convert_fusion.1 = bf16[512,640]{1,0:T(8,128)(2,1)} fusion(bf16[512,2560]{1,0:T(8,128)(2,1)} %param.7, bf16[2560,640]{1,0:T(8,128)(2,1)S(1)} %copy-done), kind=kOutput, calls=%fused_computation.1 | convolution fusion | flops 1678049280 | bytes 6553600 | tf_op jit(solution)/shard_map/dot_general | solution.py:27
  7.5 0.0 copy-done.7
  7.5 0.0 copy-done.3
  7.5 2.7 %fusion.g00 = bf16[640,512]{1,0:T(8,128)(2,1)} fusion(bf16[512,2560]{1,0:T(8,128)(2,1)S(1)} %copy-done.7, bf16[2560,640]{1,0:T(8,128)(2,1)S(1)} %copy-done.3), kind=kOutput, calls=%fused_computation.2 | convolution fusion | flops 1678049280 | bytes 6553600 | tf_op jit(solution)/shard_map/dot_general | solution.py:27
  10.2 3.8 %collective-permute-start.4 = (bf16[640,512]{1,0:T(8,128)(2,1)}, bf16[640,512]{1,0:T(8,128)(2,1)}, u32[]{:S(2)}, u32[]{:S(2)}) collective-permute-start(bf16[640,512]{1,0:T(8,128)(2,1)} %fusion.g00), channel_id=1, source_target_pairs={{0,1},{1,0},{2,3},{3,2},{4,5},{5,4},{6,7},{7,6},{8,9},{9,8},{10,11... | collective-permute-start | bytes 1966088 | tf_op jit(solution)/shard_map/ppermute | solution.py:233
  14.0 1.0 collective-permute-start.1
  15.0 0.0 collective-permute-start.3
  15.0 6.1 %collective-permute-start.2 = (bf16[512,640]{1,0:T(8,128)(2,1)}, bf16[512,640]{1,0:T(8,128)(2,1)}, u32[]{:S(2)}, u32[]{:S(2)}) collective-permute-start(bf16[512,640]{1,0:T(8,128)(2,1)} %convolution_convert_fusion.1), channel_id=1, source_target_pairs={{0,0},{1,1},{2,2},{3,3},{4,7},{5,6},{6,5},{7,4},{8,8},{9,9},{10,10... | collective-permute-start | bytes 1966088 | tf_op jit(solution)/shard_map/ppermute | solution.py:233
  21.1 0.0 copy-start.4
  21.1 0.0 copy-start.5
  21.1 2.6 %convolution_convert_fusion.2 = bf16[128,640]{1,0:T(8,128)(2,1)} fusion(bf16[128,2560]{1,0:T(8,128)(2,1)} %param.10, bf16[2560,640]{1,0:T(8,128)(2,1)S(1)} %copy-done), kind=kOutput, calls=%fused_computation.3 | convolution fusion | flops 419512320 | bytes 4096000 | tf_op jit(solution)/shard_map/dot_general | solution.py:27
  23.7 0.0 copy-done.4
  23.7 0.0 copy-done.5
  23.7 0.0 copy-start.6
  23.7 1.4 fusion.4
  25.2 17.1 %collective-permute-done.4.g10 = bf16[640,512]{1,0:T(8,128)(2,1)} collective-permute-done((bf16[640,512]{1,0:T(8,128)(2,1)}, bf16[640,512]{1,0:T(8,128)(2,1)}, u32[]{:S(2)}, u32[]{:S(2)}) %collective-permute-start.4) | collective-permute-done | bytes 655392 | tf_op jit(solution)/shard_map/ppermute | solution.py:233
  42.3 2.0 %collective-permute-start.5 = (bf16[640,512]{1,0:T(8,128)(2,1)}, bf16[640,512]{1,0:T(8,128)(2,1)S(1)}, u32[]{:S(2)}, u32[]{:S(2)}) collective-permute-start(bf16[640,512]{1,0:T(8,128)(2,1)} %collective-permute-done.4.g10), channel_id=1, source_target_pairs={{0,4},{1,5},{2,6},{3,7},{4,0},{5,1},{6,2},{7,3},{8,12},{9,13},{10,... | collective-permute-start | bytes 1966088 | tf_op jit(solution)/shard_map/ppermute | solution.py:233
  44.2 0.0 copy-done.6
  44.2 0.0 collective-permute-start
  44.2 1.5 collective-permute-done
  45.8 0.2 collective-permute-start.6
  46.0 0.0 collective-permute-done.1.g01
  46.0 0.0 collective-permute-start.7
  46.0 0.0 collective-permute-done.3.a1_ref
  46.0 2.8 %collective-permute-done.2.a0_ref = bf16[512,640]{1,0:T(8,128)(2,1)} collective-permute-done((bf16[512,640]{1,0:T(8,128)(2,1)}, bf16[512,640]{1,0:T(8,128)(2,1)}, u32[]{:S(2)}, u32[]{:S(2)}) %collective-permute-start.2) | collective-permute-done | bytes 655392 | tf_op jit(solution)/shard_map/ppermute | solution.py:233
  48.8 5.5 %shard_map.73 = (bf16[1280,768]{1,0:T(8,128)(2,1)}, bf16[6,256,640]{2,1,0:T(8,128)(2,1)S(1)}, bf16[2,512,640]{2,1,0:T(8,128)(2,1)S(1)}, f32[1,640]{1,0:T(1,128)S(1)}) custom-call(s32[2,4]{1,0:T(2,128)S(1)} %pad_add_fusion.lengths_ref, bf16[640,512]{1,0:T(8,128)(2,1)} %fusion.g00, bf16[640,512]{1,0:T(8,128)(2,1)} %collective-permute-done.1.g01, ...), custom_call_target="tpu_custom_call" | custom-call | tf_op jit(solution)/shard_map/pallas_call | solution.py:148
  54.3 0.0 collective-permute-done.7
  54.3 0.4 collective-permute-done.6.qa_ref
  54.6 0.0 collective-permute-done.5.g11
  54.7 0.0 copy-start.1
  54.7 5.1 %shard_map.74 = bf16[1280,768]{1,0:T(8,128)(2,1)} custom-call(s32[2,4]{1,0:T(2,128)S(1)} %pad_add_fusion.lengths_ref, bf16[1280,768]{1,0:T(8,128)(2,1)} %get-tuple-element.23._, bf16[640,512]{1,0:T(8,128)(2,1)} %collective-permute-done.4.g10, bf16[640,512]{1,0:T(8,128)(2,1)S(1)} %collective-permute-done.5.g11, ...), custom_call_target="tpu_custom_call", output_to_operand_aliasing={{}: (1, {})} | custom-call | tf_op jit(solution)/shard_map/pallas_call | solution.py:168
  59.8 0.0 copy-done.1
  59.8 8.6 %all-to-all-start = ((bf16[32,40,768]{2,1,0:T(8,128)(2,1)}), bf16[32,40,768]{2,1,0:T(8,128)(2,1)}, u32[]{:S(2)}, u32[]{:S(2)}) async-start(bf16[32,40,768]{2,1,0:T(8,128)(2,1)} %bitcast.25), calls=%async_computation | async-start | bytes 3932160 | tf_op jit(solution)/shard_map/all_to_all | solution.py:271
  68.4 23.8 %all-to-all-done.parts_ref = bf16[32,40,768]{2,1,0:T(8,128)(2,1)} async-done(((bf16[32,40,768]{2,1,0:T(8,128)(2,1)}), bf16[32,40,768]{2,1,0:T(8,128)(2,1)}, u32[]{:S(2)}, u32[]{:S(2)}) %all-to-all-start) | async-done | bytes 1966112 | tf_op jit(solution)/shard_map/all_to_all | solution.py:271
  92.3 1.5 fusion.1
  93.7 3.6 %collective-permute-start.8 = (f32[1,1]{1,0:T(1,128)}, f32[1,1]{1,0:T(1,128)}, u32[]{:S(2)}, u32[]{:S(2)}) collective-permute-start(f32[1,1]{1,0:T(1,128)} %bitcast.5), channel_id=1, source_target_pairs={{0,4},{1,5},{2,6},{3,7},{4,0},{5,1},{6,2},{7,3},{8,12},{9,13},{10,... | collective-permute-start | bytes 20 | tf_op jit(solution)/shard_map/ppermute | solution.py:233
  97.3 1.0 collective-permute-done.8
  99.6 2.0 %collective-permute-start.9 = (f32[1,1]{1,0:T(1,128)}, f32[1,1]{1,0:T(1,128)}, u32[]{:S(2)}, u32[]{:S(2)}) collective-permute-start(f32[1,1]{1,0:T(1,128)} %add.30), channel_id=1, source_target_pairs={{0,1},{1,0},{2,3},{3,2},{4,5},{5,4},{6,7},{7,6},{8,9},{9,8},{10,11... | collective-permute-start | bytes 20 | tf_op jit(solution)/shard_map/ppermute | solution.py:233
  101.7 1.4 collective-permute-done.9
  103.8 7.9 %collective-permute-start.10 = (f32[1,1]{1,0:T(1,128)}, f32[1,1]{1,0:T(1,128)}, u32[]{:S(2)}, u32[]{:S(2)}) collective-permute-start(f32[1,1]{1,0:T(1,128)} %add.31), channel_id=1, source_target_pairs={{0,3},{1,2},{2,1},{3,0},{4,7},{5,6},{6,5},{7,4},{8,11},{9,10},{10,... | collective-permute-start | bytes 20 | tf_op jit(solution)/shard_map/ppermute | solution.py:233
  111.7 0.3 collective-permute-done.10
  112.7 0.0 copy-start.2
  112.7 1.9 %shard_map.75 = bf16[32,40,640]{2,1,0:T(8,128)(2,1)S(1)} custom-call(f32[1,1]{1,0:T(1,128)S(6)} %mul.15.damping_ref, bf16[32,40,768]{2,1,0:T(8,128)(2,1)} %all-to-all-done.parts_ref, bf16[40,128]{1,0:T(8,128)(2,1)S(1)} %broadcast_select_fusion.qg_ref, bf16[128,640]{1,0:T(8,128)(2,1)S(1)} %collective-permute-done.6.qa_ref), custom_call_target="tpu_custom_call" | custom-call | tf_op jit(solution)/shard_map/pallas_call | solution.py:46
  114.7 23.8 %all_to_all.10 = bf16[32,40,640]{2,1,0:T(8,128)(2,1)S(1)} all-to-all(bf16[32,40,640]{2,1,0:T(8,128)(2,1)S(1)} %shard_map.75), channel_id=1, replica_groups=mesh['x'=4,'zl'=2,'y'=4,'c'=2,'m'=4] {'x','zl','y'}, dimensions={0} | all-to-all | bytes 3276800 | tf_op jit(solution)/shard_map/all_to_all | solution.py:279
  138.5 0.0 copy-done.2
  138.5 4.3 %shard_map.76 = f32[2,4,128]{2,1,0:T(4,128)S(1)} custom-call(s32[2,4]{1,0:T(2,128)S(1)} %pad_add_fusion.lengths_ref, bf16[1280,640]{1,0:T(8,128)(2,1)S(1)} %bitcast.24, bf16[640,512]{1,0:T(8,128)(2,1)} %fusion.g00, bf16[640,512]{1,0:T(8,128)(2,1)} %collective-permute-done.1.g01, bf16[640,512]{1,0:T(8,128)(2,1)} %collective-permute-done.4.g10, ...), custom_call_target="tpu_custom_call" | custom-call | tf_op jit(solution)/shard_map/pallas_call | solution.py:46
  142.8 3.5 %collective-permute-start.11 = (f32[4,128]{1,0:T(4,128)S(1)}, f32[4,128]{1,0:T(4,128)S(1)}, u32[]{:S(2)}, u32[]{:S(2)}) collective-permute-start(f32[4,128]{1,0:T(4,128)S(1)} %slice_bitcast_fusion), channel_id=1, source_target_pairs={{0,4},{1,5},{2,6},{3,7},{4,0},{5,1},{6,2},{7,3},{8,12},{9,13},{10,... | collective-permute-start | bytes 6152 | tf_op jit(solution)/shard_map/ppermute | solution.py:233
  146.3 0.8 collective-permute-done.11
  147.1 0.1 collective-permute-start.12
  147.2 3.3 %collective-permute-done.12 = f32[4,128]{1,0:T(4,128)S(1)} collective-permute-done((f32[4,128]{1,0:T(4,128)S(1)}, f32[4,128]{1,0:T(4,128)S(1)}, u32[]{:S(2)}, u32[]{:S(2)}) %collective-permute-start.12) | collective-permute-done | bytes 2080 | tf_op jit(solution)/shard_map/ppermute | solution.py:233
  150.5 3.6 %collective-permute-start.13 = (f32[4,128]{1,0:T(4,128)S(1)}, f32[4,128]{1,0:T(4,128)S(1)}, u32[]{:S(2)}, u32[]{:S(2)}) collective-permute-start(f32[4,128]{1,0:T(4,128)S(1)} %add.34), channel_id=1, source_target_pairs={{0,3},{1,2},{2,1},{3,0},{4,7},{5,6},{6,5},{7,4},{8,11},{9,10},{10,... | collective-permute-start | bytes 6152 | tf_op jit(solution)/shard_map/ppermute | solution.py:233
  154.1 1.0 collective-permute-done.13
  155.0 0.6 slice_reduce_fusion
  (7 shorter events, 0.0 us)
Async XLA Ops:
  0.0 1.9 %copy-start = (bf16[2560,640]{1,0:T(8,128)(2,1)S(1)}, bf16[2560,640]{1,0:T(8,128)(2,1)}, u32[]{:S(2)}) copy-start(bf16[2560,640]{1,0:T(8,128)(2,1)} %param.12) | copy-start | bytes 9830404
  0.0 7.5 %copy-start.7 = (bf16[512,2560]{1,0:T(8,128)(2,1)S(1)}, bf16[512,2560]{1,0:T(8,128)(2,1)}, u32[]{:S(2)}) copy-start(bf16[512,2560]{1,0:T(8,128)(2,1)} %param.8) | copy-start | bytes 7864324
  0.0 7.5 %copy-start.3 = (bf16[2560,640]{1,0:T(8,128)(2,1)S(1)}, bf16[2560,640]{1,0:T(8,128)(2,1)}, u32[]{:S(2)}) copy-start(bf16[2560,640]{1,0:T(8,128)(2,1)} %param.13) | copy-start | bytes 9830404
  10.2 32.1 %collective-permute-start.4 = (bf16[640,512]{1,0:T(8,128)(2,1)}, bf16[640,512]{1,0:T(8,128)(2,1)}, u32[]{:S(2)}, u32[]{:S(2)}) collective-permute-start(bf16[640,512]{1,0:T(8,128)(2,1)} %fusion.g00), channel_id=1, source_target_pairs={{0,1},{1,0},{2,3},{3,2},{4,5},{5,4},{6,7},{7,6},{8,9},{9,8},{10,11... | collective-permute-start | bytes 1966088 | tf_op jit(solution)/shard_map/ppermute | solution.py:233
  14.0 31.9 %collective-permute-start.1 = (bf16[640,512]{1,0:T(8,128)(2,1)}, bf16[640,512]{1,0:T(8,128)(2,1)}, u32[]{:S(2)}, u32[]{:S(2)}) collective-permute-start(bf16[640,512]{1,0:T(8,128)(2,1)} %fusion.g00), channel_id=1, source_target_pairs={{0,4},{1,5},{2,6},{3,7},{4,0},{5,1},{6,2},{7,3},{8,12},{9,13},{10,... | collective-permute-start | bytes 1966088 | tf_op jit(solution)/shard_map/ppermute | solution.py:233
  15.0 31.0 %collective-permute-start.3 = (bf16[512,640]{1,0:T(8,128)(2,1)}, bf16[512,640]{1,0:T(8,128)(2,1)}, u32[]{:S(2)}, u32[]{:S(2)}) collective-permute-start(bf16[512,640]{1,0:T(8,128)(2,1)} %convolution_convert_fusion.1), channel_id=1, source_target_pairs={{0,7},{1,6},{2,5},{3,4},{4,0},{5,1},{6,2},{7,3},{8,15},{9,14},{10,... | collective-permute-start | bytes 1966088 | tf_op jit(solution)/shard_map/ppermute | solution.py:233
  15.0 33.8 %collective-permute-start.2 = (bf16[512,640]{1,0:T(8,128)(2,1)}, bf16[512,640]{1,0:T(8,128)(2,1)}, u32[]{:S(2)}, u32[]{:S(2)}) collective-permute-start(bf16[512,640]{1,0:T(8,128)(2,1)} %convolution_convert_fusion.1), channel_id=1, source_target_pairs={{0,0},{1,1},{2,2},{3,3},{4,7},{5,6},{6,5},{7,4},{8,8},{9,9},{10,10... | collective-permute-start | bytes 1966088 | tf_op jit(solution)/shard_map/ppermute | solution.py:233
  21.1 2.6 %copy-start.4 = (bf16[2560,640]{1,0:T(8,128)(2,1)S(1)}, bf16[2560,640]{1,0:T(8,128)(2,1)}, u32[]{:S(2)}) copy-start(bf16[2560,640]{1,0:T(8,128)(2,1)} %param.13) | copy-start | bytes 9830404
  21.1 2.6 %copy-start.5 = (bf16[128,2560]{1,0:T(8,128)(2,1)S(1)}, bf16[128,2560]{1,0:T(8,128)(2,1)}, u32[]{:S(2)}) copy-start(bf16[128,2560]{1,0:T(8,128)(2,1)} %param.11) | copy-start | bytes 1966084
  23.7 20.5 %copy-start.6 = (s32[4]{0:T(128)S(1)}, s32[4]{0:T(128)}, u32[]{:S(2)}) copy-start(s32[4]{0:T(128)} %param.9) | copy-start | bytes 52
  42.3 12.4 %collective-permute-start.5 = (bf16[640,512]{1,0:T(8,128)(2,1)}, bf16[640,512]{1,0:T(8,128)(2,1)S(1)}, u32[]{:S(2)}, u32[]{:S(2)}) collective-permute-start(bf16[640,512]{1,0:T(8,128)(2,1)} %collective-permute-done.4.g10), channel_id=1, source_target_pairs={{0,4},{1,5},{2,6},{3,7},{4,0},{5,1},{6,2},{7,3},{8,12},{9,13},{10,... | collective-permute-start | bytes 1966088 | tf_op jit(solution)/shard_map/ppermute | solution.py:233
  44.2 1.5 collective-permute-start
  45.8 8.9 %collective-permute-start.6 = (bf16[128,640]{1,0:T(8,128)(2,1)}, bf16[128,640]{1,0:T(8,128)(2,1)S(1)}, u32[]{:S(2)}, u32[]{:S(2)}) collective-permute-start(bf16[128,640]{1,0:T(8,128)(2,1)} %convolution_convert_fusion.2), channel_id=1, source_target_pairs={{0,7},{1,6},{2,5},{3,4},{4,0},{5,1},{6,2},{7,3},{8,15},{9,14},{10,... | collective-permute-start | bytes 491528 | tf_op jit(solution)/shard_map/ppermute | solution.py:233
  46.0 8.3 %collective-permute-start.7 = (bf16[40,128]{1,0:T(8,128)(2,1)S(1)}, bf16[40,128]{1,0:T(8,128)(2,1)S(1)}, u32[]{:S(2)}, u32[]{:S(2)}) collective-permute-start(bf16[40,128]{1,0:T(8,128)(2,1)S(1)} %fusion.2), channel_id=1, source_target_pairs={{0,1},{1,0},{2,3},{3,2},{4,5},{5,4},{6,7},{7,6},{8,9},{9,8},{10,11... | collective-permute-start | bytes 30728 | tf_op jit(solution)/shard_map/ppermute | solution.py:233
  54.7 5.1 %copy-start.1 = (bf16[640,512]{1,0:T(8,128)(2,1)}, bf16[640,512]{1,0:T(8,128)(2,1)S(1)}, u32[]{:S(2)}) copy-start(bf16[640,512]{1,0:T(8,128)(2,1)S(1)} %collective-permute-done.5.g11) | copy-start | bytes 1966084
  59.8 32.5 %all-to-all-start = ((bf16[32,40,768]{2,1,0:T(8,128)(2,1)}), bf16[32,40,768]{2,1,0:T(8,128)(2,1)}, u32[]{:S(2)}, u32[]{:S(2)}) async-start(bf16[32,40,768]{2,1,0:T(8,128)(2,1)} %bitcast.25), calls=%async_computation | async-start | bytes 3932160 | tf_op jit(solution)/shard_map/all_to_all | solution.py:271
  93.7 4.6 %collective-permute-start.8 = (f32[1,1]{1,0:T(1,128)}, f32[1,1]{1,0:T(1,128)}, u32[]{:S(2)}, u32[]{:S(2)}) collective-permute-start(f32[1,1]{1,0:T(1,128)} %bitcast.5), channel_id=1, source_target_pairs={{0,4},{1,5},{2,6},{3,7},{4,0},{5,1},{6,2},{7,3},{8,12},{9,13},{10,... | collective-permute-start | bytes 20 | tf_op jit(solution)/shard_map/ppermute | solution.py:233
  99.6 3.5 %collective-permute-start.9 = (f32[1,1]{1,0:T(1,128)}, f32[1,1]{1,0:T(1,128)}, u32[]{:S(2)}, u32[]{:S(2)}) collective-permute-start(f32[1,1]{1,0:T(1,128)} %add.30), channel_id=1, source_target_pairs={{0,1},{1,0},{2,3},{3,2},{4,5},{5,4},{6,7},{7,6},{8,9},{9,8},{10,11... | collective-permute-start | bytes 20 | tf_op jit(solution)/shard_map/ppermute | solution.py:233
  103.8 8.2 %collective-permute-start.10 = (f32[1,1]{1,0:T(1,128)}, f32[1,1]{1,0:T(1,128)}, u32[]{:S(2)}, u32[]{:S(2)}) collective-permute-start(f32[1,1]{1,0:T(1,128)} %add.31), channel_id=1, source_target_pairs={{0,3},{1,2},{2,1},{3,0},{4,7},{5,6},{6,5},{7,4},{8,11},{9,10},{10,... | collective-permute-start | bytes 20 | tf_op jit(solution)/shard_map/ppermute | solution.py:233
  112.7 25.8 %copy-start.2 = (bf16[640,512]{1,0:T(8,128)(2,1)S(1)}, bf16[640,512]{1,0:T(8,128)(2,1)}, u32[]{:S(2)}) copy-start(bf16[640,512]{1,0:T(8,128)(2,1)} %copy-done.1) | copy-start | bytes 1966084
  142.8 4.4 %collective-permute-start.11 = (f32[4,128]{1,0:T(4,128)S(1)}, f32[4,128]{1,0:T(4,128)S(1)}, u32[]{:S(2)}, u32[]{:S(2)}) collective-permute-start(f32[4,128]{1,0:T(4,128)S(1)} %slice_bitcast_fusion), channel_id=1, source_target_pairs={{0,4},{1,5},{2,6},{3,7},{4,0},{5,1},{6,2},{7,3},{8,12},{9,13},{10,... | collective-permute-start | bytes 6152 | tf_op jit(solution)/shard_map/ppermute | solution.py:233
  147.1 3.3 %collective-permute-start.12 = (f32[4,128]{1,0:T(4,128)S(1)}, f32[4,128]{1,0:T(4,128)S(1)}, u32[]{:S(2)}, u32[]{:S(2)}) collective-permute-start(f32[4,128]{1,0:T(4,128)S(1)} %fusion.3), channel_id=1, source_target_pairs={{0,1},{1,0},{2,3},{3,2},{4,5},{5,4},{6,7},{7,6},{8,9},{9,8},{10,11... | collective-permute-start | bytes 6152 | tf_op jit(solution)/shard_map/ppermute | solution.py:233
  150.5 4.5 %collective-permute-start.13 = (f32[4,128]{1,0:T(4,128)S(1)}, f32[4,128]{1,0:T(4,128)S(1)}, u32[]{:S(2)}, u32[]{:S(2)}) collective-permute-start(f32[4,128]{1,0:T(4,128)S(1)} %add.34), channel_id=1, source_target_pairs={{0,3},{1,2},{2,1},{3,0},{4,7},{5,6},{6,5},{7,4},{8,11},{9,10},{10,... | collective-permute-start | bytes 6152 | tf_op jit(solution)/shard_map/ppermute | solution.py:233

commit v4 on v3

--- a/solution.py
+++ b/solution.py
@@ -14,7 +14,7 @@
 RING = ("x", "zl", "y")
 BLOCKS = ("c", "m")
 HALF = 256
-VMEM = 24 * 1024 * 1024
+VMEM = 16 * 1024 * 1024
 f32 = jnp.float32
 bf16 = jnp.bfloat16
 
@@ -200,22 +200,33 @@
 
 def score_kernel(lengths_ref, p_ref, g00, g01, g10, g11, a0_ref, a1_ref, out_ref):
     width, tokens = g00.shape
+    count = lengths_ref.shape[1]
     lane = lax.broadcasted_iota(jnp.int32, (1, tokens), 1)
+    line = lax.broadcasted_iota(jnp.int32, (count, 1), 0)
+    found = []
     for b, (near, far, acts) in enumerate(((g00, g10, a0_ref), (g01, g11, a1_ref))):
         sums = jnp.zeros((1, tokens), f32)
         for member, grads in enumerate((near, far)):
-            moved = dot(p_ref[member * width : (member + 1) * width, :], acts[...], ((1,), (1,)))
-            sums = sums + jnp.sum(grads[...].astype(f32) * moved, axis=0, keepdims=True)
+            product = dot(p_ref[member * width : (member + 1) * width, :], acts[...], ((1,), (1,)))
+            sums = sums + jnp.sum(grads[...].astype(f32) * product, axis=0, keepdims=True)
+        rows = jnp.zeros((count, 1), f32)
         for j, (start, finish) in enumerate(bounds_of(lengths_ref, b)):
             inside = (lane >= start) & (lane < finish)
             value = jnp.sum(jnp.where(inside, sums, 0.0), axis=1, keepdims=True)
-            out_ref[b, j : j + 1, :] = jnp.broadcast_to(value, (1, out_ref.shape[2]))
+            rows = jnp.where(line == j, value, rows)
+        found.append(jnp.broadcast_to(rows, (count, 128)))
+    first = lengths_ref[2, 0] == 0
+    half = out_ref.shape[0] // 2
+    for i in range(half):
+        out_ref[i] = jnp.where(first, found[0], found[1])
+        out_ref[half + i] = jnp.where(first, found[1], found[0])
 
 
 def scores_of(lengths, precond, g00, g01, g10, g11, a0, a1):
-    return local_call(
-        score_kernel, [jax.ShapeDtypeStruct((2, lengths.shape[1], 128), f32)]
-    )(lengths, precond, g00, g01, g10, g11, a0, a1)[0]
+    shape = (lax.axis_size("c") * lax.axis_size("m"), lengths.shape[1], 128)
+    return local_call(score_kernel, [jax.ShapeDtypeStruct(shape, f32)])(
+        lengths, precond, g00, g01, g10, g11, a0, a1
+    )[0]
 
 
 def routes(f):
@@ -224,7 +235,6 @@
 
 OTHER_CORE = routes(lambda c, m: (1 - c, m))
 GRADS_PARTNER = routes(lambda c, m: (c, m ^ 1))
-ACTS_PARTNER = routes(lambda c, m: (c, 3 - m))
 ACTS_SAME = routes(lambda c, m: (0, m) if c == 0 else (1, 3 - m))
 ACTS_OTHER = routes(lambda c, m: (0, m) if c == 1 else (1, 3 - m))
 
@@ -233,14 +243,14 @@
     return lax.ppermute(array, BLOCKS, pairs)
 
 
-def over_partners(value):
-    value = value + moved(value, GRADS_PARTNER)
-    return value + moved(value, ACTS_PARTNER)
+def summed(parts, axes):
+    return jnp.sum(lax.all_to_all(parts, axes, 0, 0, tiled=True), axis=0)
 
 
 def shards(train_acts, train_grads, lengths, query_acts, query_grads, basis_in, basis_out):
     ring = lax.axis_index(RING)
     ring_size = lax.axis_size(RING)
+    blocks = lax.axis_size("c") * lax.axis_size("m")
     count = lengths.shape[0]
 
     acts = rotate(train_acts, basis_in)
@@ -248,10 +258,12 @@
     a1 = moved(acts, ACTS_OTHER)
     a0 = moved(acts, ACTS_SAME)
     g00 = rotate_transposed(train_grads, basis_out)
-    g00, query_acts, query_grads = lax.optimization_barrier((g00, query_acts, query_grads))
+    other = moved(lengths, OTHER_CORE)
+    g00, other, query_acts, query_grads = lax.optimization_barrier((g00, other, query_acts, query_grads))
     g10 = moved(g00, GRADS_PARTNER)
     g01 = moved(g00, OTHER_CORE)
-    both = jnp.stack([lengths, moved(lengths, OTHER_CORE)])
+    core = lax.broadcast_in_dim(lax.axis_index("c"), lengths.shape, ())
+    both = jnp.stack([lengths, other, core])
 
     width, cols = g00.shape[0], a0.shape[1]
     chunk = 2 * width // ring_size
@@ -259,27 +271,27 @@
     qa = rotate(query_acts, basis_in)
     qg_own = rotate_transposed(query_grads, basis_out)
     qg_mine = lax.dynamic_slice_in_dim(qg_own, lax.rem(ring, inner) * chunk, chunk, 0)
-    g10, qa, qg_mine = lax.optimization_barrier((g10, qa, qg_mine))
+    g10, qa, qg_mine, both = lax.optimization_barrier((g10, qa, qg_mine, both))
     g11 = moved(g10, OTHER_CORE)
+
+    started, masked, wide, sums = near_curvature(both, g00, g01, a0, a1)
+    sums, qa, qg_mine = lax.optimization_barrier((sums, qa, qg_mine))
     qa = moved(qa, ACTS_OTHER)
     qg_far = moved(qg_mine, GRADS_PARTNER)
-
-    started, masked, wide, sums = near_curvature(both, g00, g01, a0, a1)
-    g11, qa, qg_far = lax.optimization_barrier((g11, qa, qg_far))
+    curvature = far_curvature(both, started, g10, g11, masked, wide, sums)
+    curvature, qa, qg_far = lax.optimization_barrier((curvature, qa, qg_far))
     qg = jnp.where(ring < inner, qg_mine, qg_far)
-    curvature = far_curvature(both, started, g10, g11, masked, wide, sums)
     parts = lax.all_to_all(curvature.reshape(ring_size, chunk, cols + 128), RING, 0, 0, tiled=True)
-    total = jnp.sum(parts[:, 0, cols : cols + 3].astype(f32)).reshape(1, 1)
-    total = over_partners(total + moved(total, OTHER_CORE))
+    total = jnp.sum(parts[:, 0, cols : cols + 3].astype(f32))
+    total = summed(jnp.broadcast_to(total, (blocks, 1, 1)), BLOCKS)
     scale = 1.0 / (count * lax.axis_size(DP))
-    entries = 2 * width * cols * 8
+    entries = 2 * width * cols * blocks
     damping = total * (DAMPING_RATIO * scale / entries)
 
     mine = precond_of(scale, damping, parts, qg, qa)
     precond = lax.all_to_all(mine, RING, 0, 0, tiled=True).reshape(2 * width, cols)
     found = scores_of(both, precond, g00, g01, g10, g11, a0, a1)
-    found = over_partners(found[0] + moved(found[1], OTHER_CORE))
-    return found[:, 0].reshape(1, count)
+    return summed(found, BLOCKS)[:, 0].reshape(1, count)
 
 
 def solution(mesh):

time: 157 us -> 167 us (1.064)
  blocking collectives: 23.8 us -> 37.5 us
  starting transfers between devices: 42.4 us -> 35.7 us
  waiting for transfers between devices: 53.3 us -> 58.4 us
  between operations: 2.86 us -> 0.88 us
    ppermute x14 -> x8, starting transfers between devices: 33.8 us -> 19.7 us  [moved(): return lax.ppermute(array, BLOCKS, pairs)]
    all_to_all x0 -> x1, blocking collectives: none -> 12.1 us  [summed(): return jnp.sum(lax.all_to_all(parts, axes, 0, 0, tiled=True), axis=0)]
    all_to_all x0 -> x1, waiting for transfers between devices: none -> 6.97 us  [summed(): return jnp.sum(lax.all_to_all(parts, axes, 0, 0, tiled=True), axis=0)]
    all_to_all x0 -> x1, starting transfers between devices: none -> 5.99 us  [summed(): return jnp.sum(lax.all_to_all(parts, axes, 0, 0, tiled=True), axis=0)]
    ppermute x14 -> x8, waiting for transfers between devices: 29.5 us -> 25 us  [moved(): return lax.ppermute(array, BLOCKS, pairs)]
    all_to_all x1, waiting for transfers between devices: 23.8 us -> 26.5 us  [shards(): lax.all_to_all(curvature.reshape(ring_size, chunk, cols + 128), RING, 0,...]
  transfers between devices with their start and end apart: 15 -> 10, of which waited for: 11 -> 3; matrix products, arithmetic and copies ran while one was open for 3% -> 4% of each run, Pallas kernels for 4% -> 6%
where the time goes in v4:
time: 167 us; the launch traced here: 166 us
  waiting for transfers between devices  58.4 us (35%)
  blocking collectives  37.5 us (22%)
  starting transfers between devices  35.7 us (21%)
  Pallas kernels  15.5 us (9%)
  matrix products  11.6 us (7%)
  local copies, waits for them, and re-layouts  4.13 us (2%)
  other arithmetic  2.18 us (1%)
    all_to_all x1, waiting for transfers between devices, shards(): lax.all_to_all(curvature.reshape(ring_size, chunk, cols + 128), RING, 0,...  26.5 us
    all_to_all x1, blocking collectives, shards(): lax.all_to_all(mine, RING, 0, 0, tiled=True).reshape(2 * width, cols)  25.5 us
    ppermute x8, waiting for transfers between devices, moved(): return lax.ppermute(array, BLOCKS, pairs)  25 us
    ppermute x8, starting transfers between devices, moved(): return lax.ppermute(array, BLOCKS, pairs)  19.7 us
    all_to_all x1, blocking collectives, summed(): return jnp.sum(lax.all_to_all(parts, axes, 0, 0, tiled=True), axis=0)  12.1 us
    dot_general x4, matrix products, dot(): lax.dot_general(a, b, (contract, ((), ())), preferred_element_type=f32)  11.6 us
    all_to_all x1, starting transfers between devices, shards(): lax.all_to_all(curvature.reshape(ring_size, chunk, cols + 128), RING, 0,...  9.98 us
    all_to_all x1, waiting for transfers between devices, summed(): return jnp.sum(lax.all_to_all(parts, axes, 0, 0, tiled=True), axis=0)  6.97 us
  transfers between devices with their start and end apart: 10, of which 3 were waited for; matrix products, arithmetic and copies ran while one was open for 4% of the time, Pallas kernels for 6%

profile of v4, /device:TPU:1, one launch (start us, length us, event | category | flops | bytes accessed | tf_op | source)
XLA Modules:
  0.0 165.9 jit_solution(14750454289466075545)
XLA Ops:
  0.0 0.0 copy-start
  0.0 0.0 copy-start.12
  0.0 1.9 %copy-done = bf16[2560,640]{1,0:T(8,128)(2,1)S(1)} copy-done((bf16[2560,640]{1,0:T(8,128)(2,1)S(1)}, bf16[2560,640]{1,0:T(8,128)(2,1)}, u32[]{:S(2)}) %copy-start) | copy-done | bytes 3276824
  1.9 4.8 %convolution_convert_fusion.1 = bf16[512,640]{1,0:T(8,128)(2,1)} fusion(bf16[512,2560]{1,0:T(8,128)(2,1)} %param.7, bf16[2560,640]{1,0:T(8,128)(2,1)S(1)} %copy-done), kind=kOutput, calls=%fused_computation.1 | convolution fusion | flops 1678049280 | bytes 6553600 | tf_op jit(solution)/shard_map/dot_general | solution.py:27
  6.7 3.2 %collective-permute-start.4 = (bf16[512,640]{1,0:T(8,128)(2,1)}, bf16[512,640]{1,0:T(8,128)(2,1)}, u32[]{:S(2)}, u32[]{:S(2)}) collective-permute-start(bf16[512,640]{1,0:T(8,128)(2,1)} %convolution_convert_fusion.1), channel_id=1, source_target_pairs={{0,7},{1,6},{2,5},{3,4},{4,0},{5,1},{6,2},{7,3},{8,15},{9,14},{10,... | collective-permute-start | bytes 1966088 | tf_op jit(solution)/shard_map/ppermute | solution.py:243
  9.9 6.2 %collective-permute-start.3 = (bf16[512,640]{1,0:T(8,128)(2,1)}, bf16[512,640]{1,0:T(8,128)(2,1)}, u32[]{:S(2)}, u32[]{:S(2)}) collective-permute-start(bf16[512,640]{1,0:T(8,128)(2,1)} %convolution_convert_fusion.1), channel_id=1, source_target_pairs={{0,0},{1,1},{2,2},{3,3},{4,7},{5,6},{6,5},{7,4},{8,8},{9,9},{10,10... | collective-permute-start | bytes 1966088 | tf_op jit(solution)/shard_map/ppermute | solution.py:243
  16.1 0.0 copy-done.12
  16.1 4.4 %collective-permute-start = (s32[4]{0:T(128)S(1)}, s32[4]{0:T(128)S(1)}, u32[]{:S(2)}, u32[]{:S(2)}) collective-permute-start(s32[4]{0:T(128)S(1)} %copy-done.12), channel_id=1, source_target_pairs={{0,4},{1,5},{2,6},{3,7},{4,0},{5,1},{6,2},{7,3},{8,12},{9,13},{10,... | collective-permute-start | bytes 56 | tf_op jit(solution)/shard_map/ppermute | solution.py:243
  20.5 0.1 pad.2.clone
  20.6 0.0 copy-start.10
  20.6 4.7 %fusion.g00 = bf16[640,512]{1,0:T(8,128)(2,1)S(1)} fusion(bf16[512,2560]{1,0:T(8,128)(2,1)} %param.8, bf16[2560,640]{1,0:T(8,128)(2,1)} %param.13), kind=kOutput, calls=%fused_computation.2 | convolution fusion | flops 1678049280 | bytes 6553600 | tf_op jit(solution)/shard_map/dot_general | solution.py:27
  25.3 0.0 copy-start.1
  25.3 0.0 copy-start.9
  25.3 0.0 copy-start.11
  25.3 0.0 collective-permute-done
  25.3 0.1 collective-permute-start.2
  25.4 1.3 collective-permute-start.1
  26.7 0.0 copy-done.10
  26.7 0.7 convolution_convert_fusion.2
  27.4 0.1 copy-done.9
  27.4 0.1 copy-done.11
  27.6 1.4 fusion.3
  29.0 0.1 add_add_fusion.lengths_ref
  29.1 25.0 %collective-permute-done.1.g10 = bf16[640,512]{1,0:T(8,128)(2,1)S(1)} collective-permute-done((bf16[640,512]{1,0:T(8,128)(2,1)S(1)}, bf16[640,512]{1,0:T(8,128)(2,1)S(1)}, u32[]{:S(2)}, u32[]{:S(2)}) %collective-permute-start.1) | collective-permute-done | bytes 655392 | tf_op jit(solution)/shard_map/ppermute | solution.py:243
  54.1 0.0 copy-start.5
  54.1 1.1 collective-permute-start.5
  55.2 0.0 collective-permute-done.4.a1_ref
  55.2 0.0 collective-permute-done.3.a0_ref
  55.2 0.0 collective-permute-done.2.g01
  55.2 0.0 copy-done.1
  55.2 0.0 copy-start.3
  55.2 5.4 %shard_map.73 = (bf16[1280,768]{1,0:T(8,128)(2,1)}, bf16[6,256,640]{2,1,0:T(8,128)(2,1)S(1)}, bf16[2,512,640]{2,1,0:T(8,128)(2,1)S(1)}, f32[1,640]{1,0:T(1,128)S(1)}) custom-call(s32[3,4]{1,0:T(4,128)S(1)} %add_add_fusion.lengths_ref, bf16[640,512]{1,0:T(8,128)(2,1)S(1)} %fusion.g00, bf16[640,512]{1,0:T(8,128)(2,1)S(1)} %collective-permute-done.2.g01, ...), custom_call_target="tpu_custom_call" | custom-call | tf_op jit(solution)/shard_map/pallas_call | solution.py:148
  60.6 0.3 collective-permute-start.6
  60.9 3.2 %collective-permute-start.7 = (bf16[40,128]{1,0:T(8,128)(2,1)S(1)}, bf16[40,128]{1,0:T(8,128)(2,1)S(1)}, u32[]{:S(2)}, u32[]{:S(2)}) collective-permute-start(bf16[40,128]{1,0:T(8,128)(2,1)S(1)} %fusion.2), channel_id=1, source_target_pairs={{0,1},{1,0},{2,3},{3,2},{4,5},{5,4},{6,7},{7,6},{8,9},{9,8},{10,11... | collective-permute-start | bytes 30728 | tf_op jit(solution)/shard_map/ppermute | solution.py:243
  64.2 0.0 collective-permute-done.5.g11
  64.2 0.0 copy-start.7
  64.2 4.4 %shard_map.74 = bf16[1280,768]{1,0:T(8,128)(2,1)} custom-call(s32[3,4]{1,0:T(4,128)S(1)} %add_add_fusion.lengths_ref, bf16[1280,768]{1,0:T(8,128)(2,1)} %get-tuple-element.32._, bf16[640,512]{1,0:T(8,128)(2,1)S(1)} %collective-permute-done.1.g10, bf16[640,512]{1,0:T(8,128)(2,1)S(1)} %collective-permute-done.5.g11, ...), custom_call_target="tpu_custom_call", output_to_operand_aliasing={{}: (1, {})} | custom-call | tf_op jit(solution)/shard_map/pallas_call | solution.py:168
  68.6 0.0 copy-done.5
  68.6 0.0 copy-done.3
  68.6 0.0 copy-done.7
  68.6 0.0 collective-permute-done.7
  68.6 0.0 collective-permute-done.6.qa_ref
  68.6 10.0 %all-to-all-start = ((bf16[32,40,768]{2,1,0:T(8,128)(2,1)}), bf16[32,40,768]{2,1,0:T(8,128)(2,1)}, u32[]{:S(2)}, u32[]{:S(2)}) async-start(bf16[32,40,768]{2,1,0:T(8,128)(2,1)} %bitcast.20), calls=%async_computation | async-start | bytes 3932160 | tf_op jit(solution)/shard_map/all_to_all | solution.py:284
  78.6 26.5 %all-to-all-done.parts_ref = bf16[32,40,768]{2,1,0:T(8,128)(2,1)} async-done(((bf16[32,40,768]{2,1,0:T(8,128)(2,1)}), bf16[32,40,768]{2,1,0:T(8,128)(2,1)}, u32[]{:S(2)}, u32[]{:S(2)}) %all-to-all-start) | async-done | bytes 1966112 | tf_op jit(solution)/shard_map/all_to_all | solution.py:284
  105.1 1.5 fusion.1
  106.6 1.2 broadcast_in_dim.3
  107.8 6.0 %all-to-all-start.1 = ((f32[8,1,1]{2,1,0:T(1,128)}), f32[8,1,1]{2,1,0:T(1,128)S(1)}, u32[]{:S(2)}, u32[]{:S(2)}) async-start(f32[8,1,1]{2,1,0:T(1,128)} %broadcast_in_dim.3), calls=%async_computation.1 | async-start | bytes 8192 | tf_op jit(solution)/shard_map/all_to_all | solution.py:247
  113.8 7.0 %all-to-all-done.1 = f32[8,1,1]{2,1,0:T(1,128)S(1)} async-done(((f32[8,1,1]{2,1,0:T(1,128)}), f32[8,1,1]{2,1,0:T(1,128)S(1)}, u32[]{:S(2)}, u32[]{:S(2)}) %all-to-all-start.1) | async-done | bytes 64 | tf_op jit(solution)/shard_map/all_to_all | solution.py:247
  120.8 0.6 reduce_sum.28
  122.0 0.0 copy-start.2
  122.1 0.0 copy-start.4
  122.1 0.0 copy-start.6
  122.1 0.0 copy-start.8
  122.1 2.0 %shard_map.75 = bf16[32,40,640]{2,1,0:T(8,128)(2,1)S(1)} custom-call(f32[1,1]{1,0:T(1,128)} %bitcast.5.damping_ref, bf16[32,40,768]{2,1,0:T(8,128)(2,1)} %all-to-all-done.parts_ref, bf16[40,128]{1,0:T(8,128)(2,1)S(1)} %broadcast_select_fusion.qg_ref, bf16[128,640]{1,0:T(8,128)(2,1)S(1)} %collective-permute-done.6.qa_ref), custom_call_target="tpu_custom_call" | custom-call | tf_op jit(solution)/shard_map/pallas_call | solution.py:46
  124.1 25.5 %all_to_all.20 = bf16[32,40,640]{2,1,0:T(8,128)(2,1)S(1)} all-to-all(bf16[32,40,640]{2,1,0:T(8,128)(2,1)S(1)} %shard_map.75), channel_id=1, replica_groups=mesh['x'=4,'zl'=2,'y'=4,'c'=2,'m'=4] {'x','zl','y'}, dimensions={0} | all-to-all | bytes 3276800 | tf_op jit(solution)/shard_map/all_to_all | solution.py:292
  149.6 0.0 copy-done.2
  149.6 0.0 copy-done.4
  149.6 0.0 copy-done.6
  149.6 0.0 copy-done.8
  149.6 3.6 %shard_map.76 = f32[8,4,128]{2,1,0:T(4,128)S(1)} custom-call(s32[3,4]{1,0:T(4,128)S(1)} %add_add_fusion.lengths_ref, bf16[1280,640]{1,0:T(8,128)(2,1)S(1)} %bitcast.19, bf16[640,512]{1,0:T(8,128)(2,1)S(1)} %copy-done.2, bf16[640,512]{1,0:T(8,128)(2,1)S(1)} %copy-done.4, bf16[640,512]{1,0:T(8,128)(2,1)S(1)} %copy-done.6, bf16[640,512]{1,0:T(8,128)(2,1)S(1)} %copy-done.8, ...), custom_call_target="tpu_custom_call" | custom-call | tf_op jit(solution)/shard_map/pallas_call | solution.py:46
  153.2 12.1 %all_to_all.21 = f32[8,4,128]{2,1,0:T(4,128)S(1)} all-to-all(f32[8,4,128]{2,1,0:T(4,128)S(1)} %shard_map.76), channel_id=1, replica_groups=mesh['x'=4,'zl'=2,'y'=4,'c'=2,'m'=4] {'c','m'}, dimensions={0} | all-to-all | bytes 32768 | tf_op jit(solution)/shard_map/all_to_all | solution.py:247
  165.3 0.6 slice_reduce_fusion
  (3 shorter events, 0.0 us)
Async XLA Ops:
  0.0 1.9 %copy-start = (bf16[2560,640]{1,0:T(8,128)(2,1)S(1)}, bf16[2560,640]{1,0:T(8,128)(2,1)}, u32[]{:S(2)}) copy-start(bf16[2560,640]{1,0:T(8,128)(2,1)} %param.12) | copy-start | bytes 9830404
  0.0 16.1 %copy-start.12 = (s32[4]{0:T(128)S(1)}, s32[4]{0:T(128)}, u32[]{:S(2)}) copy-start(s32[4]{0:T(128)} %param.9) | copy-start | bytes 52
  6.7 48.5 %collective-permute-start.4 = (bf16[512,640]{1,0:T(8,128)(2,1)}, bf16[512,640]{1,0:T(8,128)(2,1)}, u32[]{:S(2)}, u32[]{:S(2)}) collective-permute-start(bf16[512,640]{1,0:T(8,128)(2,1)} %convolution_convert_fusion.1), channel_id=1, source_target_pairs={{0,7},{1,6},{2,5},{3,4},{4,0},{5,1},{6,2},{7,3},{8,15},{9,14},{10,... | collective-permute-start | bytes 1966088 | tf_op jit(solution)/shard_map/ppermute | solution.py:243
  9.9 45.2 %collective-permute-start.3 = (bf16[512,640]{1,0:T(8,128)(2,1)}, bf16[512,640]{1,0:T(8,128)(2,1)}, u32[]{:S(2)}, u32[]{:S(2)}) collective-permute-start(bf16[512,640]{1,0:T(8,128)(2,1)} %convolution_convert_fusion.1), channel_id=1, source_target_pairs={{0,0},{1,1},{2,2},{3,3},{4,7},{5,6},{6,5},{7,4},{8,8},{9,9},{10,10... | collective-permute-start | bytes 1966088 | tf_op jit(solution)/shard_map/ppermute | solution.py:243
  16.1 9.2 %collective-permute-start = (s32[4]{0:T(128)S(1)}, s32[4]{0:T(128)S(1)}, u32[]{:S(2)}, u32[]{:S(2)}) collective-permute-start(s32[4]{0:T(128)S(1)} %copy-done.12), channel_id=1, source_target_pairs={{0,4},{1,5},{2,6},{3,7},{4,0},{5,1},{6,2},{7,3},{8,12},{9,13},{10,... | collective-permute-start | bytes 56 | tf_op jit(solution)/shard_map/ppermute | solution.py:243
  20.6 6.1 %copy-start.10 = (bf16[128,2560]{1,0:T(8,128)(2,1)S(1)}, bf16[128,2560]{1,0:T(8,128)(2,1)}, u32[]{:S(2)}) copy-start(bf16[128,2560]{1,0:T(8,128)(2,1)} %param.10) | copy-start | bytes 1966084
  25.3 29.9 %copy-start.1 = (bf16[640,512]{1,0:T(8,128)(2,1)}, bf16[640,512]{1,0:T(8,128)(2,1)S(1)}, u32[]{:S(2)}) copy-start(bf16[640,512]{1,0:T(8,128)(2,1)S(1)} %fusion.g00) | copy-start | bytes 1966084
  25.3 2.2 %copy-start.9 = (bf16[2560,640]{1,0:T(8,128)(2,1)S(1)}, bf16[2560,640]{1,0:T(8,128)(2,1)}, u32[]{:S(2)}) copy-start(bf16[2560,640]{1,0:T(8,128)(2,1)} %param.13) | copy-start | bytes 9830404
  25.3 2.3 %copy-start.11 = (bf16[128,2560]{1,0:T(8,128)(2,1)S(1)}, bf16[128,2560]{1,0:T(8,128)(2,1)}, u32[]{:S(2)}) copy-start(bf16[128,2560]{1,0:T(8,128)(2,1)} %param.11) | copy-start | bytes 1966084
  25.3 29.9 %collective-permute-start.2 = (bf16[640,512]{1,0:T(8,128)(2,1)S(1)}, bf16[640,512]{1,0:T(8,128)(2,1)S(1)}, u32[]{:S(2)}, u32[]{:S(2)}) collective-permute-start(bf16[640,512]{1,0:T(8,128)(2,1)S(1)} %fusion.g00), channel_id=1, source_target_pairs={{0,4},{1,5},{2,6},{3,7},{4,0},{5,1},{6,2},{7,3},{8,12},{9,13},{10,... | collective-permute-start | bytes 1966088 | tf_op jit(solution)/shard_map/ppermute | solution.py:243
  25.4 28.7 %collective-permute-start.1 = (bf16[640,512]{1,0:T(8,128)(2,1)S(1)}, bf16[640,512]{1,0:T(8,128)(2,1)S(1)}, u32[]{:S(2)}, u32[]{:S(2)}) collective-permute-start(bf16[640,512]{1,0:T(8,128)(2,1)S(1)} %fusion.g00), channel_id=1, source_target_pairs={{0,1},{1,0},{2,3},{3,2},{4,5},{5,4},{6,7},{7,6},{8,9},{9,8},{10,11... | collective-permute-start | bytes 1966088 | tf_op jit(solution)/shard_map/ppermute | solution.py:243
  54.1 14.5 %copy-start.5 = (bf16[640,512]{1,0:T(8,128)(2,1)}, bf16[640,512]{1,0:T(8,128)(2,1)S(1)}, u32[]{:S(2)}) copy-start(bf16[640,512]{1,0:T(8,128)(2,1)S(1)} %collective-permute-done.1.g10) | copy-start | bytes 1966084
  54.1 10.1 %collective-permute-start.5 = (bf16[640,512]{1,0:T(8,128)(2,1)S(1)}, bf16[640,512]{1,0:T(8,128)(2,1)S(1)}, u32[]{:S(2)}, u32[]{:S(2)}) collective-permute-start(bf16[640,512]{1,0:T(8,128)(2,1)S(1)} %collective-permute-done.1.g10), channel_id=1, source_target_pairs={{0,4},{1,5},{2,6},{3,7},{4,0},{5,1},{6,2},{7,3},{8,12},{9,13},{10,... | collective-permute-start | bytes 1966088 | tf_op jit(solution)/shard_map/ppermute | solution.py:243
  55.2 13.4 %copy-start.3 = (bf16[640,512]{1,0:T(8,128)(2,1)}, bf16[640,512]{1,0:T(8,128)(2,1)S(1)}, u32[]{:S(2)}) copy-start(bf16[640,512]{1,0:T(8,128)(2,1)S(1)} %collective-permute-done.2.g01) | copy-start | bytes 1966084
  60.6 8.0 %collective-permute-start.6 = (bf16[128,640]{1,0:T(8,128)(2,1)S(1)}, bf16[128,640]{1,0:T(8,128)(2,1)S(1)}, u32[]{:S(2)}, u32[]{:S(2)}) collective-permute-start(bf16[128,640]{1,0:T(8,128)(2,1)S(1)} %convolution_convert_fusion.2), channel_id=1, source_target_pairs={{0,7},{1,6},{2,5},{3,4},{4,0},{5,1},{6,2},{7,3},{8,15},{9,14},{10,... | collective-permute-start | bytes 491528 | tf_op jit(solution)/shard_map/ppermute | solution.py:243
  60.9 7.7 %collective-permute-start.7 = (bf16[40,128]{1,0:T(8,128)(2,1)S(1)}, bf16[40,128]{1,0:T(8,128)(2,1)S(1)}, u32[]{:S(2)}, u32[]{:S(2)}) collective-permute-start(bf16[40,128]{1,0:T(8,128)(2,1)S(1)} %fusion.2), channel_id=1, source_target_pairs={{0,1},{1,0},{2,3},{3,2},{4,5},{5,4},{6,7},{7,6},{8,9},{9,8},{10,11... | collective-permute-start | bytes 30728 | tf_op jit(solution)/shard_map/ppermute | solution.py:243
  64.2 4.5 %copy-start.7 = (bf16[640,512]{1,0:T(8,128)(2,1)}, bf16[640,512]{1,0:T(8,128)(2,1)S(1)}, u32[]{:S(2)}) copy-start(bf16[640,512]{1,0:T(8,128)(2,1)S(1)} %collective-permute-done.5.g11) | copy-start | bytes 1966084
  68.6 36.5 %all-to-all-start = ((bf16[32,40,768]{2,1,0:T(8,128)(2,1)}), bf16[32,40,768]{2,1,0:T(8,128)(2,1)}, u32[]{:S(2)}, u32[]{:S(2)}) async-start(bf16[32,40,768]{2,1,0:T(8,128)(2,1)} %bitcast.20), calls=%async_computation | async-start | bytes 3932160 | tf_op jit(solution)/shard_map/all_to_all | solution.py:284
  107.8 13.0 %all-to-all-start.1 = ((f32[8,1,1]{2,1,0:T(1,128)}), f32[8,1,1]{2,1,0:T(1,128)S(1)}, u32[]{:S(2)}, u32[]{:S(2)}) async-start(f32[8,1,1]{2,1,0:T(1,128)} %broadcast_in_dim.3), calls=%async_computation.1 | async-start | bytes 8192 | tf_op jit(solution)/shard_map/all_to_all | solution.py:247
  122.0 27.5 %copy-start.2 = (bf16[640,512]{1,0:T(8,128)(2,1)S(1)}, bf16[640,512]{1,0:T(8,128)(2,1)}, u32[]{:S(2)}) copy-start(bf16[640,512]{1,0:T(8,128)(2,1)} %copy-done.1) | copy-start | bytes 1966084
  122.1 27.5 %copy-start.4 = (bf16[640,512]{1,0:T(8,128)(2,1)S(1)}, bf16[640,512]{1,0:T(8,128)(2,1)}, u32[]{:S(2)}) copy-start(bf16[640,512]{1,0:T(8,128)(2,1)} %copy-done.3) | copy-start | bytes 1966084
  122.1 27.5 %copy-start.6 = (bf16[640,512]{1,0:T(8,128)(2,1)S(1)}, bf16[640,512]{1,0:T(8,128)(2,1)}, u32[]{:S(2)}) copy-start(bf16[640,512]{1,0:T(8,128)(2,1)} %copy-done.5) | copy-start | bytes 1966084
  122.1 27.5 %copy-start.8 = (bf16[640,512]{1,0:T(8,128)(2,1)S(1)}, bf16[640,512]{1,0:T(8,128)(2,1)}, u32[]{:S(2)}) copy-start(bf16[640,512]{1,0:T(8,128)(2,1)} %copy-done.7) | copy-start | bytes 1966084

commit v5 on v4

--- a/solution.py
+++ b/solution.py
@@ -101,9 +101,12 @@
     return wides, places
 
 
-def near_kernel(lengths_ref, g00, g01, a0_ref, a1_ref, out_hbm, masked, wide, sums_ref, finished, sem):
+def curvature_kernel(
+    lengths_ref, g00, g01, g10, g11, a0_ref, a1_ref, out_hbm, masked, wide, near, far, terms_ref, sems
+):
     acts = (a0_ref, a1_ref)
     tokens, cols = a0_ref.shape
+    width = g00.shape[0]
     row = lax.broadcasted_iota(jnp.int32, (HALF, 1), 0)
     rows = lax.broadcasted_iota(jnp.int32, (tokens, 1), 0)
     wides, places = places_of(lengths_ref)
@@ -114,19 +117,13 @@
         inside = (row + at >= start) & (row + at < finish)
         window = acts[b][pl.ds(at, HALF), :]
         masked[slot] = jnp.where(inside, window, jnp.zeros_like(window))
-    sums_ref[...] = block_curvature((g00, g01), [p[:3] for p in places], masked, wide, finished)
-    width = finished.shape[0]
-    copy = pltpu.make_async_copy(finished, out_hbm.at[0:width, 0:cols], sem)
-    copy.start()
-    copy.wait()
-
-
-def far_kernel(lengths_ref, _, g10, g11, masked, wide, sums_ref, out_hbm, finished, terms_ref, sems):
-    places = places_of(lengths_ref)[1]
-    sums = sums_ref[...] + block_curvature((g10, g11), [p[:3] for p in places], masked, wide, finished)
-    width, cols = finished.shape
-    copy = pltpu.make_async_copy(finished, out_hbm.at[width : 2 * width, 0:cols], sems.at[0])
-    copy.start()
+    places = [p[:3] for p in places]
+    sums = block_curvature((g00, g01), places, masked, wide, near)
+    first = pltpu.make_async_copy(near, out_hbm.at[0:width, 0:cols], sems.at[0])
+    first.start()
+    sums = sums + block_curvature((g10, g11), places, masked, wide, far)
+    second = pltpu.make_async_copy(far, out_hbm.at[width : 2 * width, 0:cols], sems.at[1])
+    second.start()
     total = jnp.sum(sums, axis=1, keepdims=True)
     high = total.astype(bf16).astype(f32)
     middle = (total - high).astype(bf16).astype(f32)
@@ -134,50 +131,33 @@
     lane = lax.broadcasted_iota(jnp.int32, (1, 128), 1)
     terms = jnp.where(lane == 0, high, jnp.where(lane == 1, middle, jnp.where(lane == 2, low, 0.0)))
     terms_ref[...] = jnp.broadcast_to(terms, terms_ref.shape).astype(bf16)
-    also = pltpu.make_async_copy(terms_ref, out_hbm.at[:, cols : cols + 128], sems.at[1])
-    also.start()
-    copy.wait()
-    also.wait()
-
-
-def near_curvature(lengths, g00, g01, a0, a1):
+    third = pltpu.make_async_copy(terms_ref, out_hbm.at[:, cols : cols + 128], sems.at[2])
+    third.start()
+    first.wait()
+    second.wait()
+    third.wait()
+
+
+def curvature_of(lengths, g00, g01, g10, g11, a0, a1):
     width = g00.shape[0]
     tokens, cols = a0.shape
     others = 2 * (lengths.shape[1] - 1)
     here = pl.BlockSpec(memory_space=pltpu.VMEM)
     return pl.pallas_call(
-        near_kernel,
-        in_specs=[pl.BlockSpec(memory_space=pltpu.SMEM)] + [here] * 4,
-        out_specs=[pl.BlockSpec(memory_space=pltpu.HBM), here, here, here],
-        out_shape=[
-            pltpu.HBM((2 * width, cols + 128), bf16),
-            jax.ShapeDtypeStruct((others, HALF, cols), bf16),
-            jax.ShapeDtypeStruct((2, tokens, cols), bf16),
-            jax.ShapeDtypeStruct((1, cols), f32),
-        ],
-        scratch_shapes=[pltpu.VMEM((width, cols), bf16), pltpu.SemaphoreType.DMA],
-        compiler_params=params(),
-    )(lengths, *in_vmem(g00, g01, a0, a1))
-
-
-def far_curvature(lengths, started, g10, g11, masked, wide, sums):
-    width = g10.shape[0]
-    cols = sums.shape[1]
-    here = pl.BlockSpec(memory_space=pltpu.VMEM)
-    anywhere = pl.BlockSpec(memory_space=pltpu.HBM)
-    return pl.pallas_call(
-        far_kernel,
-        in_specs=[pl.BlockSpec(memory_space=pltpu.SMEM), anywhere] + [here] * 5,
-        out_specs=anywhere,
-        out_shape=pltpu.HBM(started.shape, started.dtype),
-        input_output_aliases={1: 0},
+        curvature_kernel,
+        in_specs=[pl.BlockSpec(memory_space=pltpu.SMEM)] + [here] * 6,
+        out_specs=pl.BlockSpec(memory_space=pltpu.HBM),
+        out_shape=pltpu.HBM((2 * width, cols + 128), bf16),
         scratch_shapes=[
+            pltpu.VMEM((others, HALF, cols), bf16),
+            pltpu.VMEM((2, tokens, cols), bf16),
+            pltpu.VMEM((width, cols), bf16),
             pltpu.VMEM((width, cols), bf16),
             pltpu.VMEM((2 * width, 128), bf16),
-            pltpu.SemaphoreType.DMA((2,)),
+            pltpu.SemaphoreType.DMA((3,)),
         ],
         compiler_params=params(),
-    )(lengths, started, *in_vmem(g10, g11, masked, wide, sums))
+    )(lengths, *in_vmem(g00, g01, g10, g11, a0, a1))
 
 
 def precond_kernel(scale, damping_ref, parts_ref, qg_ref, qa_ref, out_ref):
@@ -253,15 +233,15 @@
     blocks = lax.axis_size("c") * lax.axis_size("m")
     count = lengths.shape[0]
 
+    other = moved(lengths, OTHER_CORE)
+    g00 = rotate_transposed(train_grads, basis_out)
+    g00, other, train_acts = lax.optimization_barrier((g00, other, train_acts))
+    g10 = moved(g00, GRADS_PARTNER)
+    g01 = moved(g00, OTHER_CORE)
     acts = rotate(train_acts, basis_in)
-    acts, train_grads = lax.optimization_barrier((acts, train_grads))
+    acts, g01, query_acts, query_grads = lax.optimization_barrier((acts, g01, query_acts, query_grads))
     a1 = moved(acts, ACTS_OTHER)
     a0 = moved(acts, ACTS_SAME)
-    g00 = rotate_transposed(train_grads, basis_out)
-    other = moved(lengths, OTHER_CORE)
-    g00, other, query_acts, query_grads = lax.optimization_barrier((g00, other, query_acts, query_grads))
-    g10 = moved(g00, GRADS_PARTNER)
-    g01 = moved(g00, OTHER_CORE)
     core = lax.broadcast_in_dim(lax.axis_index("c"), lengths.shape, ())
     both = jnp.stack([lengths, other, core])
 
@@ -273,12 +253,10 @@
     qg_mine = lax.dynamic_slice_in_dim(qg_own, lax.rem(ring, inner) * chunk, chunk, 0)
     g10, qa, qg_mine, both = lax.optimization_barrier((g10, qa, qg_mine, both))
     g11 = moved(g10, OTHER_CORE)
-
-    started, masked, wide, sums = near_curvature(both, g00, g01, a0, a1)
-    sums, qa, qg_mine = lax.optimization_barrier((sums, qa, qg_mine))
+    a0, a1, qa, qg_mine = lax.optimization_barrier((a0, a1, qa, qg_mine))
     qa = moved(qa, ACTS_OTHER)
     qg_far = moved(qg_mine, GRADS_PARTNER)
-    curvature = far_curvature(both, started, g10, g11, masked, wide, sums)
+    curvature = curvature_of(both, g00, g01, g10, g11, a0, a1)
     curvature, qa, qg_far = lax.optimization_barrier((curvature, qa, qg_far))
     qg = jnp.where(ring < inner, qg_mine, qg_far)
     parts = lax.all_to_all(curvature.reshape(ring_size, chunk, cols + 128), RING, 0, 0, tiled=True)

time: 167 us -> 152 us (0.910)
  waiting for transfers between devices: 58.4 us -> 53.7 us
  starting transfers between devices: 35.7 us -> 32.3 us
  Pallas kernels: 15.5 us -> 12.1 us
  matrix products: 11.6 us -> 9.1 us
  local copies, waits for them, and re-layouts: 4.13 us -> 2.03 us
    ppermute x8, starting transfers between devices: 19.7 us -> 13.5 us  [moved(): return lax.ppermute(array, BLOCKS, pairs)]
    all_to_all x1, starting transfers between devices: 5.99 us -> 10.9 us  [summed(): return jnp.sum(lax.all_to_all(parts, axes, 0, 0, tiled=True), axis=0)]
    all_to_all x1, waiting for transfers between devices: 26.5 us -> 23.2 us  [shards(): lax.all_to_all(curvature.reshape(ring_size, chunk, cols + 128), RING, 0,...]
    pallas_call x2 -> x1, Pallas kernels: 9.86 us -> 7.2 us  [curvature_of(): pl.pallas_call(curvature_kernel, in_specs=[pl.BlockSpec(memory_space=pltp...]
    dot_general x4, matrix products: 11.6 us -> 9.1 us  [dot(): lax.dot_general(a, b, (contract, ((), ())), preferred_element_type=f32)]
    unnamed x26 -> x36, local copies, waits for them, and re-layouts: 2.2 us -> 0.08 us
    all_to_all x1, starting transfers between devices: 9.98 us -> 8.01 us  [shards(): lax.all_to_all(curvature.reshape(ring_size, chunk, cols + 128), RING, 0,...]
  transfers between devices with their start and end apart: 10 -> 10, of which waited for: 3 -> 5; matrix products, arithmetic and copies ran while one was open for 4% -> 6% of each run, Pallas kernels for 6% -> 5%
where the time goes in v5:
time: 152 us; the launch traced here: 151 us
  waiting for transfers between devices  53.7 us (35%)
  blocking collectives  38.9 us (26%)
  starting transfers between devices  32.3 us (21%)
  Pallas kernels  12.1 us (8%)
  matrix products  9.1 us (6%)
  other arithmetic  2.18 us (1%)
  local copies, waits for them, and re-layouts  2.03 us (1%)
    all_to_all x1, blocking collectives, shards(): lax.all_to_all(mine, RING, 0, 0, tiled=True).reshape(2 * width, cols)  26.7 us
    ppermute x8, waiting for transfers between devices, moved(): return lax.ppermute(array, BLOCKS, pairs)  23.7 us
    all_to_all x1, waiting for transfers between devices, shards(): lax.all_to_all(curvature.reshape(ring_size, chunk, cols + 128), RING, 0,...  23.2 us
    ppermute x8, starting transfers between devices, moved(): return lax.ppermute(array, BLOCKS, pairs)  13.5 us
    all_to_all x1, blocking collectives, summed(): return jnp.sum(lax.all_to_all(parts, axes, 0, 0, tiled=True), axis=0)  12.3 us
    all_to_all x1, starting transfers between devices, summed(): return jnp.sum(lax.all_to_all(parts, axes, 0, 0, tiled=True), axis=0)  10.9 us
    dot_general x4, matrix products, dot(): lax.dot_general(a, b, (contract, ((), ())), preferred_element_type=f32)  9.1 us
    all_to_all x1, starting transfers between devices, shards(): lax.all_to_all(curvature.reshape(ring_size, chunk, cols + 128), RING, 0,...  8.01 us
  transfers between devices with their start and end apart: 10, of which 5 were waited for; matrix products, arithmetic and copies ran while one was open for 6% of the time, Pallas kernels for 5%

profile of v5, /device:TPU:1, one launch (start us, length us, event | category | flops | bytes accessed | tf_op | source)
XLA Modules:
  0.0 151.3 jit_solution(890969337097777876)
XLA Ops:
  0.0 0.0 copy-start
  0.0 3.2 %collective-permute-start = (s32[4]{0:T(128)}, s32[4]{0:T(128)S(1)}, u32[]{:S(2)}, u32[]{:S(2)}) collective-permute-start(s32[4]{0:T(128)} %param.9), channel_id=1, source_target_pairs={{0,4},{1,5},{2,6},{3,7},{4,0},{5,1},{6,2},{7,3},{8,12},{9,13},{10,... | collective-permute-start | bytes 56 | tf_op jit(solution)/shard_map/ppermute | solution.py:223
  3.2 0.1 pad.2.clone
  3.3 4.8 %convolution_convert_fusion.1.g00 = bf16[640,512]{1,0:T(8,128)(2,1)S(1)} fusion(bf16[2560,640]{1,0:T(8,128)(2,1)} %param.13, bf16[512,2560]{1,0:T(8,128)(2,1)} %param.8), kind=kOutput, calls=%fused_computation.1 | convolution fusion | flops 1678049280 | bytes 6553600 | tf_op jit(solution)/shard_map/dot_general | solution.py:27
  8.1 0.0 copy-start.1
  8.1 0.0 collective-permute-done
  8.1 0.1 collective-permute-start.2
  8.2 1.4 collective-permute-start.1
  9.7 0.0 copy-done.16
  9.7 0.1 add_add_fusion.lengths_ref
  9.7 0.0 copy-done
  9.7 0.0 copy-done.17
  9.8 2.2 %convolution_convert_fusion = bf16[512,640]{1,0:T(8,128)(2,1)S(1)} fusion(bf16[512,2560]{1,0:T(8,128)(2,1)S(1)} %copy-done.17, bf16[2560,640]{1,0:T(8,128)(2,1)S(1)} %copy-done), kind=kOutput, calls=%fused_computation | convolution fusion | flops 1678049280 | bytes 6553600 | tf_op jit(solution)/shard_map/dot_general | solution.py:27
  12.0 0.0 copy-start.13
  12.0 0.0 copy-start.15
  12.0 0.0 collective-permute-done.2.g01
  12.0 0.0 copy-start.3
  12.0 0.8 collective-permute-start.5
  12.8 6.2 %collective-permute-start.4 = (bf16[512,640]{1,0:T(8,128)(2,1)S(1)}, bf16[512,640]{1,0:T(8,128)(2,1)S(1)}, u32[]{:S(2)}, u32[]{:S(2)}) collective-permute-start(bf16[512,640]{1,0:T(8,128)(2,1)S(1)} %convolution_convert_fusion), channel_id=1, source_target_pairs={{0,0},{1,1},{2,2},{3,3},{4,7},{5,6},{6,5},{7,4},{8,8},{9,9},{10,10... | collective-permute-start | bytes 1966088 | tf_op jit(solution)/shard_map/ppermute | solution.py:223
  19.0 0.0 copy-done.14
  19.0 0.7 convolution_convert_fusion.2
  19.7 0.0 copy-done.13
  19.7 0.0 copy-done.15
  19.7 1.4 fusion.2
  21.2 18.4 %collective-permute-done.1.g10 = bf16[640,512]{1,0:T(8,128)(2,1)S(1)} collective-permute-done((bf16[640,512]{1,0:T(8,128)(2,1)S(1)}, bf16[640,512]{1,0:T(8,128)(2,1)S(1)}, u32[]{:S(2)}, u32[]{:S(2)}) %collective-permute-start.1) | collective-permute-done | bytes 655392 | tf_op jit(solution)/shard_map/ppermute | solution.py:223
  39.6 0.9 collective-permute-start.3
  40.5 3.4 %collective-permute-done.5.a1_ref = bf16[512,640]{1,0:T(8,128)(2,1)S(1)} collective-permute-done((bf16[512,640]{1,0:T(8,128)(2,1)S(1)}, bf16[512,640]{1,0:T(8,128)(2,1)S(1)}, u32[]{:S(2)}, u32[]{:S(2)}) %collective-permute-start.5) | collective-permute-done | bytes 655392 | tf_op jit(solution)/shard_map/ppermute | solution.py:223
  43.9 1.9 %collective-permute-done.4.a0_ref = bf16[512,640]{1,0:T(8,128)(2,1)S(1)} collective-permute-done((bf16[512,640]{1,0:T(8,128)(2,1)S(1)}, bf16[512,640]{1,0:T(8,128)(2,1)S(1)}, u32[]{:S(2)}, u32[]{:S(2)}) %collective-permute-start.4) | collective-permute-done | bytes 655392 | tf_op jit(solution)/shard_map/ppermute | solution.py:223
  45.7 0.0 collective-permute-start.6
  45.7 0.8 collective-permute-start.7
  46.5 0.0 collective-permute-done.3.g11
  46.6 0.0 copy-done.1
  46.6 0.0 copy-done.3
  46.6 0.0 copy-start.11
  46.6 7.2 %shard_map.73 = bf16[1280,768]{1,0:T(8,128)(2,1)} custom-call(s32[3,4]{1,0:T(4,128)S(1)} %add_add_fusion.lengths_ref, bf16[640,512]{1,0:T(8,128)(2,1)S(1)} %convolution_convert_fusion.1.g00, bf16[640,512]{1,0:T(8,128)(2,1)S(1)} %collective-permute-done.2.g01, bf16[640,512]{1,0:T(8,128)(2,1)S(1)} %collective-permute-done.1.g10, ...), custom_call_target="tpu_custom_call" | custom-call | tf_op jit(solution)/shard_map/pallas_call | solution.py:146
  53.8 0.0 copy-done.5
  53.8 0.0 copy-done.7
  53.8 0.0 copy-done.9
  53.8 0.0 copy-done.11
  53.8 0.0 collective-permute-done.7
  53.8 0.0 collective-permute-done.6.qa_ref
  53.8 8.0 %all-to-all-start = ((bf16[32,40,768]{2,1,0:T(8,128)(2,1)}), bf16[32,40,768]{2,1,0:T(8,128)(2,1)}, u32[]{:S(2)}, u32[]{:S(2)}) async-start(bf16[32,40,768]{2,1,0:T(8,128)(2,1)} %bitcast.18), calls=%async_computation | async-start | bytes 3932160 | tf_op jit(solution)/shard_map/all_to_all | solution.py:262
  61.9 23.2 %all-to-all-done.parts_ref = bf16[32,40,768]{2,1,0:T(8,128)(2,1)} async-done(((bf16[32,40,768]{2,1,0:T(8,128)(2,1)}), bf16[32,40,768]{2,1,0:T(8,128)(2,1)}, u32[]{:S(2)}, u32[]{:S(2)}) %all-to-all-start) | async-done | bytes 1966112 | tf_op jit(solution)/shard_map/all_to_all | solution.py:262
  85.0 1.5 fusion
  86.5 1.2 broadcast_in_dim.3
  87.7 10.9 %all-to-all-start.1 = ((f32[8,1,1]{2,1,0:T(1,128)}), f32[8,1,1]{2,1,0:T(1,128)S(1)}, u32[]{:S(2)}, u32[]{:S(2)}) async-start(f32[8,1,1]{2,1,0:T(1,128)} %broadcast_in_dim.3), calls=%async_computation.1 | async-start | bytes 8192 | tf_op jit(solution)/shard_map/all_to_all | solution.py:227
  98.6 6.8 %all-to-all-done.1 = f32[8,1,1]{2,1,0:T(1,128)S(1)} async-done(((f32[8,1,1]{2,1,0:T(1,128)}), f32[8,1,1]{2,1,0:T(1,128)S(1)}, u32[]{:S(2)}, u32[]{:S(2)}) %all-to-all-start.1) | async-done | bytes 64 | tf_op jit(solution)/shard_map/all_to_all | solution.py:227
  105.4 0.6 reduce_sum.28
  106.7 0.0 copy-start.2
  106.7 0.0 copy-start.4
  106.7 0.0 copy-start.6
  106.7 0.0 copy-start.8
  106.7 0.0 copy-start.10
  106.8 0.0 copy-start.12
  106.8 2.0 %shard_map.74 = bf16[32,40,640]{2,1,0:T(8,128)(2,1)S(1)} custom-call(f32[1,1]{1,0:T(1,128)} %bitcast.4.damping_ref, bf16[32,40,768]{2,1,0:T(8,128)(2,1)} %all-to-all-done.parts_ref, bf16[40,128]{1,0:T(8,128)(2,1)S(1)} %broadcast_select_fusion.qg_ref, bf16[128,640]{1,0:T(8,128)(2,1)S(1)} %collective-permute-done.6.qa_ref), custom_call_target="tpu_custom_call" | custom-call | tf_op jit(solution)/shard_map/pallas_call | solution.py:46
  108.8 26.7 %all_to_all.20 = bf16[32,40,640]{2,1,0:T(8,128)(2,1)S(1)} all-to-all(bf16[32,40,640]{2,1,0:T(8,128)(2,1)S(1)} %shard_map.74), channel_id=1, replica_groups=mesh['x'=4,'zl'=2,'y'=4,'c'=2,'m'=4] {'x','zl','y'}, dimensions={0} | all-to-all | bytes 3276800 | tf_op jit(solution)/shard_map/all_to_all | solution.py:270
  135.5 0.0 copy-done.2
  135.5 0.0 copy-done.4
  135.5 0.0 copy-done.6
  135.5 0.0 copy-done.8
  135.5 0.0 copy-done.10
  135.5 2.9 %shard_map.75 = f32[8,4,128]{2,1,0:T(4,128)S(1)} custom-call(s32[3,4]{1,0:T(4,128)S(1)} %add_add_fusion.lengths_ref, bf16[1280,640]{1,0:T(8,128)(2,1)S(1)} %bitcast.17, bf16[640,512]{1,0:T(8,128)(2,1)S(1)} %copy-done.2, bf16[640,512]{1,0:T(8,128)(2,1)S(1)} %copy-done.4, bf16[640,512]{1,0:T(8,128)(2,1)S(1)} %copy-done.6, bf16[640,512]{1,0:T(8,128)(2,1)S(1)} %copy-done.12, ...), custom_call_target="tpu_custom_call" | custom-call | tf_op jit(solution)/shard_map/pallas_call | solution.py:46
  138.4 12.3 %all_to_all.21 = f32[8,4,128]{2,1,0:T(4,128)S(1)} all-to-all(f32[8,4,128]{2,1,0:T(4,128)S(1)} %shard_map.75), channel_id=1, replica_groups=mesh['x'=4,'zl'=2,'y'=4,'c'=2,'m'=4] {'c','m'}, dimensions={0} | all-to-all | bytes 32768 | tf_op jit(solution)/shard_map/all_to_all | solution.py:227
  150.7 0.6 slice_reduce_fusion
  (10 shorter events, 0.0 us)
Async XLA Ops:
  0.0 9.7 %copy-start = (bf16[2560,640]{1,0:T(8,128)(2,1)S(1)}, bf16[2560,640]{1,0:T(8,128)(2,1)}, u32[]{:S(2)}) copy-start(bf16[2560,640]{1,0:T(8,128)(2,1)} %param.12) | copy-start | bytes 9830404
  0.0 8.1 %collective-permute-start = (s32[4]{0:T(128)}, s32[4]{0:T(128)S(1)}, u32[]{:S(2)}, u32[]{:S(2)}) collective-permute-start(s32[4]{0:T(128)} %param.9), channel_id=1, source_target_pairs={{0,4},{1,5},{2,6},{3,7},{4,0},{5,1},{6,2},{7,3},{8,12},{9,13},{10,... | collective-permute-start | bytes 56 | tf_op jit(solution)/shard_map/ppermute | solution.py:223
  3.3 6.4 %copy-start.16 = (s32[4]{0:T(128)S(1)}, s32[4]{0:T(128)}, u32[]{:S(2)}) copy-start(s32[4]{0:T(128)} %param.9) | copy-start | bytes 52
  3.3 6.4 %copy-start.17 = (bf16[512,2560]{1,0:T(8,128)(2,1)S(1)}, bf16[512,2560]{1,0:T(8,128)(2,1)}, u32[]{:S(2)}) copy-start(bf16[512,2560]{1,0:T(8,128)(2,1)} %param.7) | copy-start | bytes 7864324
  8.1 38.4 %copy-start.1 = (bf16[640,512]{1,0:T(8,128)(2,1)}, bf16[640,512]{1,0:T(8,128)(2,1)S(1)}, u32[]{:S(2)}) copy-start(bf16[640,512]{1,0:T(8,128)(2,1)S(1)} %convolution_convert_fusion.1.g00) | copy-start | bytes 1966084
  8.1 3.8 %collective-permute-start.2 = (bf16[640,512]{1,0:T(8,128)(2,1)S(1)}, bf16[640,512]{1,0:T(8,128)(2,1)S(1)}, u32[]{:S(2)}, u32[]{:S(2)}) collective-permute-start(bf16[640,512]{1,0:T(8,128)(2,1)S(1)} %convolution_convert_fusion.1.g00), channel_id=1, source_target_pairs={{0,4},{1,5},{2,6},{3,7},{4,0},{5,1},{6,2},{7,3},{8,12},{9,13},{10,... | collective-permute-start | bytes 1966088 | tf_op jit(solution)/shard_map/ppermute | solution.py:223
  8.2 31.4 %collective-permute-start.1 = (bf16[640,512]{1,0:T(8,128)(2,1)S(1)}, bf16[640,512]{1,0:T(8,128)(2,1)S(1)}, u32[]{:S(2)}, u32[]{:S(2)}) collective-permute-start(bf16[640,512]{1,0:T(8,128)(2,1)S(1)} %convolution_convert_fusion.1.g00), channel_id=1, source_target_pairs={{0,1},{1,0},{2,3},{3,2},{4,5},{5,4},{6,7},{7,6},{8,9},{9,8},{10,11... | collective-permute-start | bytes 1966088 | tf_op jit(solution)/shard_map/ppermute | solution.py:223
  9.8 9.2 %copy-start.14 = (bf16[128,2560]{1,0:T(8,128)(2,1)S(1)}, bf16[128,2560]{1,0:T(8,128)(2,1)}, u32[]{:S(2)}) copy-start(bf16[128,2560]{1,0:T(8,128)(2,1)} %param.10) | copy-start | bytes 1966084
  12.0 7.8 %copy-start.13 = (bf16[2560,640]{1,0:T(8,128)(2,1)S(1)}, bf16[2560,640]{1,0:T(8,128)(2,1)}, u32[]{:S(2)}) copy-start(bf16[2560,640]{1,0:T(8,128)(2,1)} %param.13) | copy-start | bytes 9830404
  12.0 7.7 %copy-start.15 = (bf16[128,2560]{1,0:T(8,128)(2,1)S(1)}, bf16[128,2560]{1,0:T(8,128)(2,1)}, u32[]{:S(2)}) copy-start(bf16[128,2560]{1,0:T(8,128)(2,1)} %param.11) | copy-start | bytes 1966084
  12.0 34.6 %copy-start.3 = (bf16[640,512]{1,0:T(8,128)(2,1)}, bf16[640,512]{1,0:T(8,128)(2,1)S(1)}, u32[]{:S(2)}) copy-start(bf16[640,512]{1,0:T(8,128)(2,1)S(1)} %collective-permute-done.2.g01) | copy-start | bytes 1966084
  12.0 31.9 %collective-permute-start.5 = (bf16[512,640]{1,0:T(8,128)(2,1)S(1)}, bf16[512,640]{1,0:T(8,128)(2,1)S(1)}, u32[]{:S(2)}, u32[]{:S(2)}) collective-permute-start(bf16[512,640]{1,0:T(8,128)(2,1)S(1)} %convolution_convert_fusion), channel_id=1, source_target_pairs={{0,7},{1,6},{2,5},{3,4},{4,0},{5,1},{6,2},{7,3},{8,15},{9,14},{10,... | collective-permute-start | bytes 1966088 | tf_op jit(solution)/shard_map/ppermute | solution.py:223
  12.8 33.0 %collective-permute-start.4 = (bf16[512,640]{1,0:T(8,128)(2,1)S(1)}, bf16[512,640]{1,0:T(8,128)(2,1)S(1)}, u32[]{:S(2)}, u32[]{:S(2)}) collective-permute-start(bf16[512,640]{1,0:T(8,128)(2,1)S(1)} %convolution_convert_fusion), channel_id=1, source_target_pairs={{0,0},{1,1},{2,2},{3,3},{4,7},{5,6},{6,5},{7,4},{8,8},{9,9},{10,10... | collective-permute-start | bytes 1966088 | tf_op jit(solution)/shard_map/ppermute | solution.py:223
  39.6 14.1 %copy-start.5 = (bf16[640,512]{1,0:T(8,128)(2,1)}, bf16[640,512]{1,0:T(8,128)(2,1)S(1)}, u32[]{:S(2)}) copy-start(bf16[640,512]{1,0:T(8,128)(2,1)S(1)} %collective-permute-done.1.g10) | copy-start | bytes 1966084
  39.6 6.9 %collective-permute-start.3 = (bf16[640,512]{1,0:T(8,128)(2,1)S(1)}, bf16[640,512]{1,0:T(8,128)(2,1)S(1)}, u32[]{:S(2)}, u32[]{:S(2)}) collective-permute-start(bf16[640,512]{1,0:T(8,128)(2,1)S(1)} %collective-permute-done.1.g10), channel_id=1, source_target_pairs={{0,4},{1,5},{2,6},{3,7},{4,0},{5,1},{6,2},{7,3},{8,12},{9,13},{10,... | collective-permute-start | bytes 1966088 | tf_op jit(solution)/shard_map/ppermute | solution.py:223
  43.9 9.9 %copy-start.7 = (bf16[512,640]{1,0:T(8,128)(2,1)}, bf16[512,640]{1,0:T(8,128)(2,1)S(1)}, u32[]{:S(2)}) copy-start(bf16[512,640]{1,0:T(8,128)(2,1)S(1)} %collective-permute-done.5.a1_ref) | copy-start | bytes 1966084
  45.7 8.1 %copy-start.9 = (bf16[512,640]{1,0:T(8,128)(2,1)}, bf16[512,640]{1,0:T(8,128)(2,1)S(1)}, u32[]{:S(2)}) copy-start(bf16[512,640]{1,0:T(8,128)(2,1)S(1)} %collective-permute-done.4.a0_ref) | copy-start | bytes 1966084
  45.7 8.1 %collective-permute-start.6 = (bf16[128,640]{1,0:T(8,128)(2,1)S(1)}, bf16[128,640]{1,0:T(8,128)(2,1)S(1)}, u32[]{:S(2)}, u32[]{:S(2)}) collective-permute-start(bf16[128,640]{1,0:T(8,128)(2,1)S(1)} %convolution_convert_fusion.2), channel_id=1, source_target_pairs={{0,7},{1,6},{2,5},{3,4},{4,0},{5,1},{6,2},{7,3},{8,15},{9,14},{10,... | collective-permute-start | bytes 491528 | tf_op jit(solution)/shard_map/ppermute | solution.py:223
  45.7 8.1 %collective-permute-start.7 = (bf16[40,128]{1,0:T(8,128)(2,1)S(1)}, bf16[40,128]{1,0:T(8,128)(2,1)S(1)}, u32[]{:S(2)}, u32[]{:S(2)}) collective-permute-start(bf16[40,128]{1,0:T(8,128)(2,1)S(1)} %fusion.1), channel_id=1, source_target_pairs={{0,1},{1,0},{2,3},{3,2},{4,5},{5,4},{6,7},{7,6},{8,9},{9,8},{10,11... | collective-permute-start | bytes 30728 | tf_op jit(solution)/shard_map/ppermute | solution.py:223
  46.6 7.2 %copy-start.11 = (bf16[640,512]{1,0:T(8,128)(2,1)}, bf16[640,512]{1,0:T(8,128)(2,1)S(1)}, u32[]{:S(2)}) copy-start(bf16[640,512]{1,0:T(8,128)(2,1)S(1)} %collective-permute-done.3.g11) | copy-start | bytes 1966084
  53.8 31.2 %all-to-all-start = ((bf16[32,40,768]{2,1,0:T(8,128)(2,1)}), bf16[32,40,768]{2,1,0:T(8,128)(2,1)}, u32[]{:S(2)}, u32[]{:S(2)}) async-start(bf16[32,40,768]{2,1,0:T(8,128)(2,1)} %bitcast.18), calls=%async_computation | async-start | bytes 3932160 | tf_op jit(solution)/shard_map/all_to_all | solution.py:262
  87.7 17.7 %all-to-all-start.1 = ((f32[8,1,1]{2,1,0:T(1,128)}), f32[8,1,1]{2,1,0:T(1,128)S(1)}, u32[]{:S(2)}, u32[]{:S(2)}) async-start(f32[8,1,1]{2,1,0:T(1,128)} %broadcast_in_dim.3), calls=%async_computation.1 | async-start | bytes 8192 | tf_op jit(solution)/shard_map/all_to_all | solution.py:227
  106.7 28.8 %copy-start.2 = (bf16[640,512]{1,0:T(8,128)(2,1)S(1)}, bf16[640,512]{1,0:T(8,128)(2,1)}, u32[]{:S(2)}) copy-start(bf16[640,512]{1,0:T(8,128)(2,1)} %copy-done.1) | copy-start | bytes 1966084
  106.7 28.8 %copy-start.4 = (bf16[640,512]{1,0:T(8,128)(2,1)S(1)}, bf16[640,512]{1,0:T(8,128)(2,1)}, u32[]{:S(2)}) copy-start(bf16[640,512]{1,0:T(8,128)(2,1)} %copy-done.3) | copy-start | bytes 1966084
  106.7 28.8 %copy-start.6 = (bf16[640,512]{1,0:T(8,128)(2,1)S(1)}, bf16[640,512]{1,0:T(8,128)(2,1)}, u32[]{:S(2)}) copy-start(bf16[640,512]{1,0:T(8,128)(2,1)} %copy-done.5) | copy-start | bytes 1966084
  106.7 28.8 %copy-start.8 = (bf16[512,640]{1,0:T(8,128)(2,1)S(1)}, bf16[512,640]{1,0:T(8,128)(2,1)}, u32[]{:S(2)}) copy-start(bf16[512,640]{1,0:T(8,128)(2,1)} %copy-done.7) | copy-start | bytes 1966084
  106.7 28.8 %copy-start.10 = (bf16[512,640]{1,0:T(8,128)(2,1)S(1)}, bf16[512,640]{1,0:T(8,128)(2,1)}, u32[]{:S(2)}) copy-start(bf16[512,640]{1,0:T(8,128)(2,1)} %copy-done.9) | copy-start | bytes 1966084
  106.8 28.8 %copy-start.12 = (bf16[640,512]{1,0:T(8,128)(2,1)S(1)}, bf16[640,512]{1,0:T(8,128)(2,1)}, u32[]{:S(2)}) copy-start(bf16[640,512]{1,0:T(8,128)(2,1)} %copy-done.11) | copy-start | bytes 1966084

commit v6 on v5

--- a/solution.py
+++ b/solution.py
@@ -160,22 +160,37 @@
     )(lengths, *in_vmem(g00, g01, g10, g11, a0, a1))
 
 
-def precond_kernel(scale, damping_ref, parts_ref, qg_ref, qa_ref, out_ref):
-    cols = qa_ref.shape[1]
-    total = parts_ref[0, :, 0:cols].astype(f32)
+def reduce_kernel(parts_ref, chunk_ref, total_ref):
+    cols = chunk_ref.shape[1]
+    chunk = parts_ref[0, :, 0:cols].astype(f32)
+    terms = parts_ref[0, 0:8, cols:].astype(f32)
     for j in range(1, parts_ref.shape[0]):
-        total = total + parts_ref[j, :, 0:cols].astype(f32)
+        chunk = chunk + parts_ref[j, :, 0:cols].astype(f32)
+        terms = terms + parts_ref[j, 0:8, cols:].astype(f32)
+    chunk_ref[...] = chunk
+    total_ref[...] = jnp.broadcast_to(jnp.sum(terms, axis=1, keepdims=True), total_ref.shape)
+
+
+def reduced(parts, cols):
+    shapes = [(parts.shape[1], cols), (8, 128)]
+    return local_call(
+        reduce_kernel, [jax.ShapeDtypeStruct(s, f32) for s in shapes], scalars=0
+    )(parts)
+
+
+def precond_kernel(scale, damping_scale, chunk_ref, total_ref, more_ref, qg_ref, qa_ref, out_ref):
+    damping = (total_ref[0:1, 0:1] + more_ref[0:1, 0:1]) * damping_scale
     query = dot(qg_ref[...], qa_ref[...], ((1,), (0,)))
-    value = (query / (total * scale + damping_ref[0, 0])).astype(bf16)
+    value = (query / (chunk_ref[...] * scale + damping)).astype(bf16)
     for j in range(out_ref.shape[0]):
         out_ref[j] = value
 
 
-def precond_of(scale, damping, parts, qg, qa):
-    shape = (parts.shape[0], parts.shape[1], qa.shape[1])
+def precond_of(copies, scale, damping_scale, chunk, total, more, qg, qa):
+    shape = (copies, *chunk.shape)
     return local_call(
-        functools.partial(precond_kernel, scale), [jax.ShapeDtypeStruct(shape, bf16)]
-    )(damping, parts, qg, qa)[0]
+        functools.partial(precond_kernel, scale, damping_scale), [jax.ShapeDtypeStruct(shape, bf16)], scalars=0
+    )(chunk, total, more, qg, qa)[0]
 
 
 def score_kernel(lengths_ref, p_ref, g00, g01, g10, g11, a0_ref, a1_ref, out_ref):
@@ -215,6 +230,7 @@
 
 OTHER_CORE = routes(lambda c, m: (1 - c, m))
 GRADS_PARTNER = routes(lambda c, m: (c, m ^ 1))
+ACTS_PARTNER = routes(lambda c, m: (c, 3 - m))
 ACTS_SAME = routes(lambda c, m: (0, m) if c == 0 else (1, 3 - m))
 ACTS_OTHER = routes(lambda c, m: (0, m) if c == 1 else (1, 3 - m))
 
@@ -253,20 +269,19 @@
     qg_mine = lax.dynamic_slice_in_dim(qg_own, lax.rem(ring, inner) * chunk, chunk, 0)
     g10, qa, qg_mine, both = lax.optimization_barrier((g10, qa, qg_mine, both))
     g11 = moved(g10, OTHER_CORE)
-    a0, a1, qa, qg_mine = lax.optimization_barrier((a0, a1, qa, qg_mine))
     qa = moved(qa, ACTS_OTHER)
     qg_far = moved(qg_mine, GRADS_PARTNER)
     curvature = curvature_of(both, g00, g01, g10, g11, a0, a1)
     curvature, qa, qg_far = lax.optimization_barrier((curvature, qa, qg_far))
     qg = jnp.where(ring < inner, qg_mine, qg_far)
     parts = lax.all_to_all(curvature.reshape(ring_size, chunk, cols + 128), RING, 0, 0, tiled=True)
-    total = jnp.sum(parts[:, 0, cols : cols + 3].astype(f32))
-    total = summed(jnp.broadcast_to(total, (blocks, 1, 1)), BLOCKS)
+    mine, total = reduced(parts, cols)
+    total = total + moved(total, OTHER_CORE)
+    total = total + moved(total, GRADS_PARTNER)
+    more = moved(total, ACTS_PARTNER)
     scale = 1.0 / (count * lax.axis_size(DP))
-    entries = 2 * width * cols * blocks
-    damping = total * (DAMPING_RATIO * scale / entries)
-
-    mine = precond_of(scale, damping, parts, qg, qa)
+    damping_scale = DAMPING_RATIO * scale / (2 * width * cols * blocks)
+    mine = precond_of(ring_size, scale, damping_scale, mine, total, more, qg, qa)
     precond = lax.all_to_all(mine, RING, 0, 0, tiled=True).reshape(2 * width, cols)
     found = scores_of(both, precond, g00, g01, g10, g11, a0, a1)
     return summed(found, BLOCKS)[:, 0].reshape(1, count)

time: 152 us -> 141 us (0.928)
  blocking collectives: 38.9 us -> 72.7 us
  waiting for transfers between devices: 53.7 us -> 31.4 us
  starting transfers between devices: 32.3 us -> 16.2 us
    all_to_all x0 -> x1, blocking collectives: none -> 34.1 us  [shards(): lax.all_to_all(curvature.reshape(ring_size, chunk, cols + 128), RING, 0,...]
    all_to_all x2 -> x0, waiting for transfers between devices: 30 us -> none  [the longest x1 23.2 us: shards(): lax.all_to_all(curvature.reshape(ring_size, chunk, cols + 128), RING, 0,...]
    all_to_all x2 -> x0, starting transfers between devices: 18.9 us -> none  [the longest x1 10.9 us: summed(): return jnp.sum(lax.all_to_all(parts, axes, 0, 0, tiled=True), axis=0)]
    ppermute x8 -> x11, waiting for transfers between devices: 23.7 us -> 31.4 us  [moved(): return lax.ppermute(array, BLOCKS, pairs)]
    ppermute x8 -> x11, starting transfers between devices: 13.5 us -> 16.2 us  [moved(): return lax.ppermute(array, BLOCKS, pairs)]
    all_to_all x1, blocking collectives: 26.7 us -> 24.1 us  [shards(): lax.all_to_all(mine, RING, 0, 0, tiled=True).reshape(2 * width, cols)]
    all_to_all x1, blocking collectives: 12.3 us -> 14.5 us  [summed(): return jnp.sum(lax.all_to_all(parts, axes, 0, 0, tiled=True), axis=0)]
    pallas_call x2 -> x3, Pallas kernels: 4.91 us -> 3.45 us  [call(): pl.pallas_call(kernel, in_specs=[there] * scalars + [here] * (len(operand...]
  transfers between devices with their start and end apart: 10 -> 11, of which waited for: 5 -> 6; matrix products, arithmetic and copies ran while one was open for 6% -> 6% of each run, Pallas kernels for 5% -> 5%
where the time goes in v6:
time: 141 us
  blocking collectives  72.7 us (52%)
  waiting for transfers between devices  31.4 us (22%)
  starting transfers between devices  16.2 us (11%)
  Pallas kernels  10.7 us (8%)
  matrix products  8.09 us (6%)
    all_to_all x1, blocking collectives, shards(): lax.all_to_all(curvature.reshape(ring_size, chunk, cols + 128), RING, 0,...  34.1 us
    ppermute x11, waiting for transfers between devices, moved(): return lax.ppermute(array, BLOCKS, pairs)  31.4 us
    all_to_all x1, blocking collectives, shards(): lax.all_to_all(mine, RING, 0, 0, tiled=True).reshape(2 * width, cols)  24.1 us
    ppermute x11, starting transfers between devices, moved(): return lax.ppermute(array, BLOCKS, pairs)  16.2 us
    all_to_all x1, blocking collectives, summed(): return jnp.sum(lax.all_to_all(parts, axes, 0, 0, tiled=True), axis=0)  14.5 us
    dot_general x4, matrix products, dot(): lax.dot_general(a, b, (contract, ((), ())), preferred_element_type=f32)  8.09 us
    pallas_call x1, Pallas kernels, curvature_of(): pl.pallas_call(curvature_kernel, in_specs=[pl.BlockSpec(memory_space=pltp...  7.27 us
    pallas_call x3, Pallas kernels, call(): pl.pallas_call(kernel, in_specs=[there] * scalars + [here] * (len(operand...  3.45 us
  transfers between devices with their start and end apart: 11, of which 6 were waited for; matrix products, arithmetic and copies ran while one was open for 6% of the time, Pallas kernels for 5%

profile of v6, /device:TPU:1, one launch (start us, length us, event | category | flops | bytes accessed | tf_op | source)
XLA Modules:
  0.0 140.9 jit_solution(4204660329582669624)
XLA Ops:
  0.0 0.0 copy-start
  0.0 3.2 %collective-permute-start = (s32[4]{0:T(128)}, s32[4]{0:T(128)S(1)}, u32[]{:S(2)}, u32[]{:S(2)}) collective-permute-start(s32[4]{0:T(128)} %param.9), channel_id=1, source_target_pairs={{0,4},{1,5},{2,6},{3,7},{4,0},{5,1},{6,2},{7,3},{8,12},{9,13},{10,... | collective-permute-start | bytes 56 | tf_op jit(solution)/shard_map/ppermute | solution.py:239
  3.2 0.1 pad.2.clone
  3.3 0.0 copy-done
  3.3 3.8 %convolution_convert_fusion.1.g00 = bf16[640,512]{1,0:T(8,128)(2,1)S(1)} fusion(bf16[2560,640]{1,0:T(8,128)(2,1)S(1)} %copy-done, bf16[512,2560]{1,0:T(8,128)(2,1)} %param.8), kind=kOutput, calls=%fused_computation.1 | convolution fusion | flops 1678049280 | bytes 6553600 | tf_op jit(solution)/shard_map/dot_general | solution.py:27
  7.1 0.0 copy-start.1
  7.1 0.0 collective-permute-done
  7.2 1.9 %collective-permute-start.2 = (bf16[640,512]{1,0:T(8,128)(2,1)S(1)}, bf16[640,512]{1,0:T(8,128)(2,1)S(1)}, u32[]{:S(2)}, u32[]{:S(2)}) collective-permute-start(bf16[640,512]{1,0:T(8,128)(2,1)S(1)} %convolution_convert_fusion.1.g00), channel_id=1, source_target_pairs={{0,4},{1,5},{2,6},{3,7},{4,0},{5,1},{6,2},{7,3},{8,12},{9,13},{10,... | collective-permute-start | bytes 1966088 | tf_op jit(solution)/shard_map/ppermute | solution.py:239
  9.1 1.3 collective-permute-start.1
  10.4 0.0 copy-done.18
  10.4 0.1 add_add_fusion.lengths_ref
  10.4 0.0 copy-done.13
  10.4 0.0 copy-done.19
  10.4 2.2 %convolution_convert_fusion = bf16[512,640]{1,0:T(8,128)(2,1)S(1)} fusion(bf16[512,2560]{1,0:T(8,128)(2,1)S(1)} %copy-done.19, bf16[2560,640]{1,0:T(8,128)(2,1)S(1)} %copy-done.13), kind=kOutput, calls=%fused_computation | convolution fusion | flops 1678049280 | bytes 6553600 | tf_op jit(solution)/shard_map/dot_general | solution.py:27
  12.6 0.0 copy-start.15
  12.6 0.0 collective-permute-done.2.g01
  12.7 0.0 copy-start.3
  12.7 0.4 collective-permute-start.5
  13.1 6.1 %collective-permute-start.4 = (bf16[512,640]{1,0:T(8,128)(2,1)S(1)}, bf16[512,640]{1,0:T(8,128)(2,1)S(1)}, u32[]{:S(2)}, u32[]{:S(2)}) collective-permute-start(bf16[512,640]{1,0:T(8,128)(2,1)S(1)} %convolution_convert_fusion), channel_id=1, source_target_pairs={{0,0},{1,1},{2,2},{3,3},{4,7},{5,6},{6,5},{7,4},{8,8},{9,9},{10,10... | collective-permute-start | bytes 1966088 | tf_op jit(solution)/shard_map/ppermute | solution.py:239
  19.2 0.0 copy-done.14
  19.2 1.4 %fusion.1 = bf16[128,640]{0,1:T(8,128)(2,1)S(1)} fusion(bf16[128,2560]{1,0:T(8,128)(2,1)S(1)} %copy-done.14, bf16[2560,640]{1,0:T(8,128)(2,1)S(1)} %copy-done), kind=kOutput, calls=%fused_computation.8 | convolution fusion | flops 419430400 | bytes 4096000 | tf_op jit(solution)/shard_map/dot_general | solution.py:27
  20.7 0.0 copy-done.15
  20.7 0.0 copy-start.16
  20.7 0.7 convolution_convert_fusion.2
  21.4 19.1 %collective-permute-done.1.g10 = bf16[640,512]{1,0:T(8,128)(2,1)S(1)} collective-permute-done((bf16[640,512]{1,0:T(8,128)(2,1)S(1)}, bf16[640,512]{1,0:T(8,128)(2,1)S(1)}, u32[]{:S(2)}, u32[]{:S(2)}) %collective-permute-start.1) | collective-permute-done | bytes 655392 | tf_op jit(solution)/shard_map/ppermute | solution.py:239
  40.5 0.8 collective-permute-start.3
  41.3 0.0 collective-permute-start.6
  41.3 0.0 collective-permute-start.7
  41.3 3.1 %collective-permute-done.5.a1_ref = bf16[512,640]{1,0:T(8,128)(2,1)S(1)} collective-permute-done((bf16[512,640]{1,0:T(8,128)(2,1)S(1)}, bf16[512,640]{1,0:T(8,128)(2,1)S(1)}, u32[]{:S(2)}, u32[]{:S(2)}) %collective-permute-start.5) | collective-permute-done | bytes 655392 | tf_op jit(solution)/shard_map/ppermute | solution.py:239
  44.4 1.7 %collective-permute-done.4.a0_ref = bf16[512,640]{1,0:T(8,128)(2,1)S(1)} collective-permute-done((bf16[512,640]{1,0:T(8,128)(2,1)S(1)}, bf16[512,640]{1,0:T(8,128)(2,1)S(1)}, u32[]{:S(2)}, u32[]{:S(2)}) %collective-permute-start.4) | collective-permute-done | bytes 655392 | tf_op jit(solution)/shard_map/ppermute | solution.py:239
  46.1 0.0 collective-permute-done.3.g11
  46.1 0.0 copy-done.1
  46.1 0.0 copy-done.3
  46.2 0.0 copy-start.11
  46.2 7.3 %shard_map.73 = bf16[1280,768]{1,0:T(8,128)(2,1)} custom-call(s32[3,4]{1,0:T(4,128)S(1)} %add_add_fusion.lengths_ref, bf16[640,512]{1,0:T(8,128)(2,1)S(1)} %convolution_convert_fusion.1.g00, bf16[640,512]{1,0:T(8,128)(2,1)S(1)} %collective-permute-done.2.g01, bf16[640,512]{1,0:T(8,128)(2,1)S(1)} %collective-permute-done.1.g10, ...), custom_call_target="tpu_custom_call" | custom-call | tf_op jit(solution)/shard_map/pallas_call | solution.py:146
  53.4 0.0 copy-done.16
  53.4 0.0 collective-permute-done.7
  53.5 0.0 copy-start.17
  53.5 0.0 collective-permute-done.6.qa_ref
  53.5 0.0 copy-done.11
  53.5 34.1 %all_to_all.15.parts_ref = bf16[32,40,768]{2,1,0:T(8,128)(2,1)S(1)} all-to-all(bf16[32,40,768]{2,1,0:T(8,128)(2,1)} %bitcast.17), channel_id=1, replica_groups=mesh['x'=4,'zl'=2,'y'=4,'c'=2,'m'=4] {'x','zl','y'}, dimensions={0} | all-to-all | bytes 3932160 | tf_op jit(solution)/shard_map/all_to_all | solution.py:277
  87.6 0.0 copy-done.5
  87.6 0.0 copy-done.7
  87.6 0.0 copy-done.9
  87.6 0.3 shard_map.74
  87.9 1.8 %collective-permute-start.8 = (f32[8,128]{1,0:T(8,128)S(1)}, f32[8,128]{1,0:T(8,128)S(1)}, u32[]{:S(2)}, u32[]{:S(2)}) collective-permute-start(f32[8,128]{1,0:T(8,128)S(1)} %get-tuple-element.34), channel_id=1, source_target_pairs={{0,4},{1,5},{2,6},{3,7},{4,0},{5,1},{6,2},{7,3},{8,12},{9,13},{10,... | collective-permute-start | bytes 12296 | tf_op jit(solution)/shard_map/ppermute | solution.py:239
  89.7 0.8 collective-permute-done.8
  90.6 0.0 copy-done.17
  90.6 0.1 collective-permute-start.9
  90.7 0.0 copy-start.10
  90.7 0.0 copy-start.12
  90.7 3.2 %collective-permute-done.9 = f32[8,128]{1,0:T(8,128)S(1)} collective-permute-done((f32[8,128]{1,0:T(8,128)S(1)}, f32[8,128]{1,0:T(8,128)S(1)}, u32[]{:S(2)}, u32[]{:S(2)}) %collective-permute-start.9) | collective-permute-done | bytes 4128 | tf_op jit(solution)/shard_map/ppermute | solution.py:239
  93.9 0.5 collective-permute-start.10
  94.5 0.7 broadcast_select_fusion.qg_ref
  95.2 3.3 %collective-permute-done.10.more_ref = f32[8,128]{1,0:T(8,128)S(1)} collective-permute-done((f32[8,128]{1,0:T(8,128)S(1)}, f32[8,128]{1,0:T(8,128)S(1)}, u32[]{:S(2)}, u32[]{:S(2)}) %collective-permute-start.10) | collective-permute-done | bytes 4128 | tf_op jit(solution)/shard_map/ppermute | solution.py:239
  98.5 0.3 shard_map.75
  98.8 24.1 %all_to_all.16 = bf16[32,40,640]{2,1,0:T(8,128)(2,1)S(1)} all-to-all(bf16[32,40,640]{2,1,0:T(8,128)(2,1)S(1)} %shard_map.75), channel_id=1, replica_groups=mesh['x'=4,'zl'=2,'y'=4,'c'=2,'m'=4] {'x','zl','y'}, dimensions={0} | all-to-all | bytes 3276800 | tf_op jit(solution)/shard_map/all_to_all | solution.py:285
  122.8 0.0 copy-done.2
  122.8 0.0 copy-done.4
  122.8 0.0 copy-done.6
  122.8 0.0 copy-done.8
  122.9 2.9 %shard_map.76 = f32[8,4,128]{2,1,0:T(4,128)S(1)} custom-call(s32[3,4]{1,0:T(4,128)S(1)} %add_add_fusion.lengths_ref, bf16[1280,640]{1,0:T(8,128)(2,1)S(1)} %bitcast.16, bf16[640,512]{1,0:T(8,128)(2,1)S(1)} %copy-done.2, bf16[640,512]{1,0:T(8,128)(2,1)S(1)} %copy-done.4, bf16[640,512]{1,0:T(8,128)(2,1)S(1)} %copy-done.6, bf16[640,512]{1,0:T(8,128)(2,1)S(1)} %copy-done.12, ...), custom_call_target="tpu_custom_call" | custom-call | tf_op jit(solution)/shard_map/pallas_call | solution.py:46
  125.8 14.5 %all_to_all.17 = f32[8,4,128]{2,1,0:T(4,128)S(1)} all-to-all(f32[8,4,128]{2,1,0:T(4,128)S(1)} %shard_map.76), channel_id=1, replica_groups=mesh['x'=4,'zl'=2,'y'=4,'c'=2,'m'=4] {'c','m'}, dimensions={0} | all-to-all | bytes 32768 | tf_op jit(solution)/shard_map/all_to_all | solution.py:243
  140.3 0.6 slice_reduce_fusion
  (17 shorter events, 0.1 us)
Async XLA Ops:
  0.0 3.3 %copy-start = (bf16[2560,640]{1,0:T(8,128)(2,1)S(1)}, bf16[2560,640]{1,0:T(8,128)(2,1)}, u32[]{:S(2)}) copy-start(bf16[2560,640]{1,0:T(8,128)(2,1)} %param.13) | copy-start | bytes 9830404
  0.0 7.1 %collective-permute-start = (s32[4]{0:T(128)}, s32[4]{0:T(128)S(1)}, u32[]{:S(2)}, u32[]{:S(2)}) collective-permute-start(s32[4]{0:T(128)} %param.9), channel_id=1, source_target_pairs={{0,4},{1,5},{2,6},{3,7},{4,0},{5,1},{6,2},{7,3},{8,12},{9,13},{10,... | collective-permute-start | bytes 56 | tf_op jit(solution)/shard_map/ppermute | solution.py:239
  3.3 7.0 %copy-start.18 = (s32[4]{0:T(128)S(1)}, s32[4]{0:T(128)}, u32[]{:S(2)}) copy-start(s32[4]{0:T(128)} %param.9) | copy-start | bytes 52
  3.3 7.1 %copy-start.13 = (bf16[2560,640]{1,0:T(8,128)(2,1)S(1)}, bf16[2560,640]{1,0:T(8,128)(2,1)}, u32[]{:S(2)}) copy-start(bf16[2560,640]{1,0:T(8,128)(2,1)} %param.12) | copy-start | bytes 9830404
  3.3 7.1 %copy-start.19 = (bf16[512,2560]{1,0:T(8,128)(2,1)S(1)}, bf16[512,2560]{1,0:T(8,128)(2,1)}, u32[]{:S(2)}) copy-start(bf16[512,2560]{1,0:T(8,128)(2,1)} %param.7) | copy-start | bytes 7864324
  7.1 39.0 %copy-start.1 = (bf16[640,512]{1,0:T(8,128)(2,1)}, bf16[640,512]{1,0:T(8,128)(2,1)S(1)}, u32[]{:S(2)}) copy-start(bf16[640,512]{1,0:T(8,128)(2,1)S(1)} %convolution_convert_fusion.1.g00) | copy-start | bytes 1966084
  7.2 5.5 %collective-permute-start.2 = (bf16[640,512]{1,0:T(8,128)(2,1)S(1)}, bf16[640,512]{1,0:T(8,128)(2,1)S(1)}, u32[]{:S(2)}, u32[]{:S(2)}) collective-permute-start(bf16[640,512]{1,0:T(8,128)(2,1)S(1)} %convolution_convert_fusion.1.g00), channel_id=1, source_target_pairs={{0,4},{1,5},{2,6},{3,7},{4,0},{5,1},{6,2},{7,3},{8,12},{9,13},{10,... | collective-permute-start | bytes 1966088 | tf_op jit(solution)/shard_map/ppermute | solution.py:239
  9.1 31.4 %collective-permute-start.1 = (bf16[640,512]{1,0:T(8,128)(2,1)S(1)}, bf16[640,512]{1,0:T(8,128)(2,1)S(1)}, u32[]{:S(2)}, u32[]{:S(2)}) collective-permute-start(bf16[640,512]{1,0:T(8,128)(2,1)S(1)} %convolution_convert_fusion.1.g00), channel_id=1, source_target_pairs={{0,1},{1,0},{2,3},{3,2},{4,5},{5,4},{6,7},{7,6},{8,9},{9,8},{10,11... | collective-permute-start | bytes 1966088 | tf_op jit(solution)/shard_map/ppermute | solution.py:239
  10.4 8.8 %copy-start.14 = (bf16[128,2560]{1,0:T(8,128)(2,1)S(1)}, bf16[128,2560]{1,0:T(8,128)(2,1)}, u32[]{:S(2)}) copy-start(bf16[128,2560]{1,0:T(8,128)(2,1)} %param.11) | copy-start | bytes 1966084
  12.6 8.0 %copy-start.15 = (bf16[128,2560]{1,0:T(8,128)(2,1)S(1)}, bf16[128,2560]{1,0:T(8,128)(2,1)}, u32[]{:S(2)}) copy-start(bf16[128,2560]{1,0:T(8,128)(2,1)} %param.10) | copy-start | bytes 1966084
  12.7 33.5 %copy-start.3 = (bf16[640,512]{1,0:T(8,128)(2,1)}, bf16[640,512]{1,0:T(8,128)(2,1)S(1)}, u32[]{:S(2)}) copy-start(bf16[640,512]{1,0:T(8,128)(2,1)S(1)} %collective-permute-done.2.g01) | copy-start | bytes 1966084
  12.7 31.7 %collective-permute-start.5 = (bf16[512,640]{1,0:T(8,128)(2,1)S(1)}, bf16[512,640]{1,0:T(8,128)(2,1)S(1)}, u32[]{:S(2)}, u32[]{:S(2)}) collective-permute-start(bf16[512,640]{1,0:T(8,128)(2,1)S(1)} %convolution_convert_fusion), channel_id=1, source_target_pairs={{0,7},{1,6},{2,5},{3,4},{4,0},{5,1},{6,2},{7,3},{8,15},{9,14},{10,... | collective-permute-start | bytes 1966088 | tf_op jit(solution)/shard_map/ppermute | solution.py:239
  13.1 33.0 %collective-permute-start.4 = (bf16[512,640]{1,0:T(8,128)(2,1)S(1)}, bf16[512,640]{1,0:T(8,128)(2,1)S(1)}, u32[]{:S(2)}, u32[]{:S(2)}) collective-permute-start(bf16[512,640]{1,0:T(8,128)(2,1)S(1)} %convolution_convert_fusion), channel_id=1, source_target_pairs={{0,0},{1,1},{2,2},{3,3},{4,7},{5,6},{6,5},{7,4},{8,8},{9,9},{10,10... | collective-permute-start | bytes 1966088 | tf_op jit(solution)/shard_map/ppermute | solution.py:239
  20.7 32.8 %copy-start.16 = (bf16[40,128]{1,0:T(8,128)(2,1)}, bf16[40,128]{1,0:T(8,128)(2,1)S(1)}, u32[]{:S(2)}) copy-start(bf16[40,128]{1,0:T(8,128)(2,1)S(1)} %fusion) | copy-start | bytes 30724
  40.5 47.1 %copy-start.5 = (bf16[640,512]{1,0:T(8,128)(2,1)}, bf16[640,512]{1,0:T(8,128)(2,1)S(1)}, u32[]{:S(2)}) copy-start(bf16[640,512]{1,0:T(8,128)(2,1)S(1)} %collective-permute-done.1.g10) | copy-start | bytes 1966084
  40.5 5.6 %collective-permute-start.3 = (bf16[640,512]{1,0:T(8,128)(2,1)S(1)}, bf16[640,512]{1,0:T(8,128)(2,1)S(1)}, u32[]{:S(2)}, u32[]{:S(2)}) collective-permute-start(bf16[640,512]{1,0:T(8,128)(2,1)S(1)} %collective-permute-done.1.g10), channel_id=1, source_target_pairs={{0,4},{1,5},{2,6},{3,7},{4,0},{5,1},{6,2},{7,3},{8,12},{9,13},{10,... | collective-permute-start | bytes 1966088 | tf_op jit(solution)/shard_map/ppermute | solution.py:239
  41.3 12.2 %collective-permute-start.6 = (bf16[128,640]{1,0:T(8,128)(2,1)S(1)}, bf16[128,640]{1,0:T(8,128)(2,1)S(1)}, u32[]{:S(2)}, u32[]{:S(2)}) collective-permute-start(bf16[128,640]{1,0:T(8,128)(2,1)S(1)} %convolution_convert_fusion.2), channel_id=1, source_target_pairs={{0,7},{1,6},{2,5},{3,4},{4,0},{5,1},{6,2},{7,3},{8,15},{9,14},{10,... | collective-permute-start | bytes 491528 | tf_op jit(solution)/shard_map/ppermute | solution.py:239
  41.3 12.2 %collective-permute-start.7 = (bf16[40,128]{1,0:T(8,128)(2,1)S(1)}, bf16[40,128]{1,0:T(8,128)(2,1)S(1)}, u32[]{:S(2)}, u32[]{:S(2)}) collective-permute-start(bf16[40,128]{1,0:T(8,128)(2,1)S(1)} %fusion), channel_id=1, source_target_pairs={{0,1},{1,0},{2,3},{3,2},{4,5},{5,4},{6,7},{7,6},{8,9},{9,8},{10,11... | collective-permute-start | bytes 30728 | tf_op jit(solution)/shard_map/ppermute | solution.py:239
  44.4 43.2 %copy-start.7 = (bf16[512,640]{1,0:T(8,128)(2,1)}, bf16[512,640]{1,0:T(8,128)(2,1)S(1)}, u32[]{:S(2)}) copy-start(bf16[512,640]{1,0:T(8,128)(2,1)S(1)} %collective-permute-done.5.a1_ref) | copy-start | bytes 1966084
  46.1 41.5 %copy-start.9 = (bf16[512,640]{1,0:T(8,128)(2,1)}, bf16[512,640]{1,0:T(8,128)(2,1)S(1)}, u32[]{:S(2)}) copy-start(bf16[512,640]{1,0:T(8,128)(2,1)S(1)} %collective-permute-done.4.a0_ref) | copy-start | bytes 1966084
  46.2 7.3 %copy-start.11 = (bf16[640,512]{1,0:T(8,128)(2,1)}, bf16[640,512]{1,0:T(8,128)(2,1)S(1)}, u32[]{:S(2)}) copy-start(bf16[640,512]{1,0:T(8,128)(2,1)S(1)} %collective-permute-done.3.g11) | copy-start | bytes 1966084
  53.5 37.1 %copy-start.17 = (bf16[40,128]{1,0:T(8,128)(2,1)}, bf16[40,128]{1,0:T(8,128)(2,1)S(1)}, u32[]{:S(2)}) copy-start(bf16[40,128]{1,0:T(8,128)(2,1)S(1)} %collective-permute-done.7) | copy-start | bytes 30724
  87.9 2.6 %collective-permute-start.8 = (f32[8,128]{1,0:T(8,128)S(1)}, f32[8,128]{1,0:T(8,128)S(1)}, u32[]{:S(2)}, u32[]{:S(2)}) collective-permute-start(f32[8,128]{1,0:T(8,128)S(1)} %get-tuple-element.34), channel_id=1, source_target_pairs={{0,4},{1,5},{2,6},{3,7},{4,0},{5,1},{6,2},{7,3},{8,12},{9,13},{10,... | collective-permute-start | bytes 12296 | tf_op jit(solution)/shard_map/ppermute | solution.py:239
  90.6 3.4 %collective-permute-start.9 = (f32[8,128]{1,0:T(8,128)S(1)}, f32[8,128]{1,0:T(8,128)S(1)}, u32[]{:S(2)}, u32[]{:S(2)}) collective-permute-start(f32[8,128]{1,0:T(8,128)S(1)} %add.18), channel_id=1, source_target_pairs={{0,1},{1,0},{2,3},{3,2},{4,5},{5,4},{6,7},{7,6},{8,9},{9,8},{10,11... | collective-permute-start | bytes 12296 | tf_op jit(solution)/shard_map/ppermute | solution.py:239
  90.7 32.2 %copy-start.2 = (bf16[640,512]{1,0:T(8,128)(2,1)S(1)}, bf16[640,512]{1,0:T(8,128)(2,1)}, u32[]{:S(2)}) copy-start(bf16[640,512]{1,0:T(8,128)(2,1)} %copy-done.1) | copy-start | bytes 1966084
  90.7 32.2 %copy-start.4 = (bf16[640,512]{1,0:T(8,128)(2,1)S(1)}, bf16[640,512]{1,0:T(8,128)(2,1)}, u32[]{:S(2)}) copy-start(bf16[640,512]{1,0:T(8,128)(2,1)} %copy-done.3) | copy-start | bytes 1966084
  90.7 32.2 %copy-start.6 = (bf16[640,512]{1,0:T(8,128)(2,1)S(1)}, bf16[640,512]{1,0:T(8,128)(2,1)}, u32[]{:S(2)}) copy-start(bf16[640,512]{1,0:T(8,128)(2,1)} %copy-done.5) | copy-start | bytes 1966084
  90.7 32.2 %copy-start.8 = (bf16[512,640]{1,0:T(8,128)(2,1)S(1)}, bf16[512,640]{1,0:T(8,128)(2,1)}, u32[]{:S(2)}) copy-start(bf16[512,640]{1,0:T(8,128)(2,1)} %copy-done.7) | copy-start | bytes 1966084
  90.7 32.2 %copy-start.10 = (bf16[512,640]{1,0:T(8,128)(2,1)S(1)}, bf16[512,640]{1,0:T(8,128)(2,1)}, u32[]{:S(2)}) copy-start(bf16[512,640]{1,0:T(8,128)(2,1)} %copy-done.9) | copy-start | bytes 1966084
  90.7 32.2 %copy-start.12 = (bf16[640,512]{1,0:T(8,128)(2,1)S(1)}, bf16[640,512]{1,0:T(8,128)(2,1)}, u32[]{:S(2)}) copy-start(bf16[640,512]{1,0:T(8,128)(2,1)} %copy-done.11) | copy-start | bytes 1966084
  93.9 4.6 %collective-permute-start.10 = (f32[8,128]{1,0:T(8,128)S(1)}, f32[8,128]{1,0:T(8,128)S(1)}, u32[]{:S(2)}, u32[]{:S(2)}) collective-permute-start(f32[8,128]{1,0:T(8,128)S(1)} %add.19.total_ref), channel_id=1, source_target_pairs={{0,3},{1,2},{2,1},{3,0},{4,7},{5,6},{6,5},{7,4},{8,11},{9,10},{10,... | collective-permute-start | bytes 12296 | tf_op jit(solution)/shard_map/ppermute | solution.py:239

commit v7 on v6

--- a/solution.py
+++ b/solution.py
@@ -14,6 +14,8 @@
 RING = ("x", "zl", "y")
 BLOCKS = ("c", "m")
 HALF = 256
+LANES = 128
+SPARE = 8
 VMEM = 16 * 1024 * 1024
 f32 = jnp.float32
 bf16 = jnp.bfloat16
@@ -71,7 +73,7 @@
     return chosen
 
 
-def block_curvature(grads, places, masked, wide, finished):
+def block_curvature(grads, places, masked, wide, out_ref, first):
     total = None
     for b in range(2):
         product = dot(grads[b][...], wide[b], ((1,), (0,)))
@@ -79,7 +81,13 @@
     for b, slot, at in places:
         product = dot(grads[b][:, pl.ds(at, HALF)], masked[slot], ((1,), (0,)))
         total = total + product * product
-    finished[...] = total.astype(bf16)
+    rows, cols = total.shape
+    chunk = (out_ref.shape[1] - SPARE) * LANES // cols
+    spare = jnp.zeros((SPARE, LANES), f32)
+    for k in range(rows // chunk):
+        block = total[k * chunk : (k + 1) * chunk]
+        pieces = [block[:, j * LANES : (j + 1) * LANES] for j in range(cols // LANES)]
+        out_ref[first + k] = jnp.concatenate([*pieces, spare], axis=0).astype(bf16)
     return jnp.sum(total, axis=0, keepdims=True)
 
 
@@ -101,12 +109,9 @@
     return wides, places
 
 
-def curvature_kernel(
-    lengths_ref, g00, g01, g10, g11, a0_ref, a1_ref, out_hbm, masked, wide, near, far, terms_ref, sems
-):
+def curvature_kernel(lengths_ref, g00, g01, g10, g11, a0_ref, a1_ref, out_ref, masked, wide):
     acts = (a0_ref, a1_ref)
     tokens, cols = a0_ref.shape
-    width = g00.shape[0]
     row = lax.broadcasted_iota(jnp.int32, (HALF, 1), 0)
     rows = lax.broadcasted_iota(jnp.int32, (tokens, 1), 0)
     wides, places = places_of(lengths_ref)
@@ -118,61 +123,46 @@
         window = acts[b][pl.ds(at, HALF), :]
         masked[slot] = jnp.where(inside, window, jnp.zeros_like(window))
     places = [p[:3] for p in places]
-    sums = block_curvature((g00, g01), places, masked, wide, near)
-    first = pltpu.make_async_copy(near, out_hbm.at[0:width, 0:cols], sems.at[0])
-    first.start()
-    sums = sums + block_curvature((g10, g11), places, masked, wide, far)
-    second = pltpu.make_async_copy(far, out_hbm.at[width : 2 * width, 0:cols], sems.at[1])
-    second.start()
+    sums = block_curvature((g00, g01), places, masked, wide, out_ref, 0)
+    sums = sums + block_curvature((g10, g11), places, masked, wide, out_ref, out_ref.shape[0] // 2)
     total = jnp.sum(sums, axis=1, keepdims=True)
     high = total.astype(bf16).astype(f32)
     middle = (total - high).astype(bf16).astype(f32)
     low = total - high - middle
-    lane = lax.broadcasted_iota(jnp.int32, (1, 128), 1)
+    lane = lax.broadcasted_iota(jnp.int32, (1, LANES), 1)
     terms = jnp.where(lane == 0, high, jnp.where(lane == 1, middle, jnp.where(lane == 2, low, 0.0)))
-    terms_ref[...] = jnp.broadcast_to(terms, terms_ref.shape).astype(bf16)
-    third = pltpu.make_async_copy(terms_ref, out_hbm.at[:, cols : cols + 128], sems.at[2])
-    third.start()
-    first.wait()
-    second.wait()
-    third.wait()
-
-
-def curvature_of(lengths, g00, g01, g10, g11, a0, a1):
+    terms = jnp.broadcast_to(terms, (SPARE, LANES))
+    last = out_ref.shape[1] - 2 * SPARE
+    for k in range(out_ref.shape[0]):
+        end = out_ref[k, last:, :].astype(f32)
+        out_ref[k, last:, :] = jnp.concatenate([end[0:SPARE], terms], axis=0).astype(bf16)
+
+
+def curvature_of(chunks, lengths, g00, g01, g10, g11, a0, a1):
     width = g00.shape[0]
     tokens, cols = a0.shape
     others = 2 * (lengths.shape[1] - 1)
-    here = pl.BlockSpec(memory_space=pltpu.VMEM)
-    return pl.pallas_call(
+    shape = (chunks, 2 * width * cols // (chunks * LANES) + SPARE, LANES)
+    return local_call(
         curvature_kernel,
-        in_specs=[pl.BlockSpec(memory_space=pltpu.SMEM)] + [here] * 6,
-        out_specs=pl.BlockSpec(memory_space=pltpu.HBM),
-        out_shape=pltpu.HBM((2 * width, cols + 128), bf16),
-        scratch_shapes=[
-            pltpu.VMEM((others, HALF, cols), bf16),
-            pltpu.VMEM((2, tokens, cols), bf16),
-            pltpu.VMEM((width, cols), bf16),
-            pltpu.VMEM((width, cols), bf16),
-            pltpu.VMEM((2 * width, 128), bf16),
-            pltpu.SemaphoreType.DMA((3,)),
-        ],
-        compiler_params=params(),
-    )(lengths, *in_vmem(g00, g01, g10, g11, a0, a1))
+        [jax.ShapeDtypeStruct(shape, bf16)],
+        [pltpu.VMEM((others, HALF, cols), bf16), pltpu.VMEM((2, tokens, cols), bf16)],
+    )(lengths, g00, g01, g10, g11, a0, a1)[0]
 
 
 def reduce_kernel(parts_ref, chunk_ref, total_ref):
-    cols = chunk_ref.shape[1]
-    chunk = parts_ref[0, :, 0:cols].astype(f32)
-    terms = parts_ref[0, 0:8, cols:].astype(f32)
+    rows, cols = chunk_ref.shape
+    found = parts_ref[0].astype(f32)
     for j in range(1, parts_ref.shape[0]):
-        chunk = chunk + parts_ref[j, :, 0:cols].astype(f32)
-        terms = terms + parts_ref[j, 0:8, cols:].astype(f32)
-    chunk_ref[...] = chunk
+        found = found + parts_ref[j].astype(f32)
+    pieces = [found[j * rows : (j + 1) * rows] for j in range(cols // LANES)]
+    chunk_ref[...] = jnp.concatenate(pieces, axis=1)
+    terms = found[found.shape[0] - SPARE :]
     total_ref[...] = jnp.broadcast_to(jnp.sum(terms, axis=1, keepdims=True), total_ref.shape)
 
 
 def reduced(parts, cols):
-    shapes = [(parts.shape[1], cols), (8, 128)]
+    shapes = [((parts.shape[1] - SPARE) * LANES // cols, cols), (SPARE, LANES)]
     return local_call(
         reduce_kernel, [jax.ShapeDtypeStruct(s, f32) for s in shapes], scalars=0
     )(parts)
@@ -271,10 +261,10 @@
     g11 = moved(g10, OTHER_CORE)
     qa = moved(qa, ACTS_OTHER)
     qg_far = moved(qg_mine, GRADS_PARTNER)
-    curvature = curvature_of(both, g00, g01, g10, g11, a0, a1)
+    curvature = curvature_of(ring_size, both, g00, g01, g10, g11, a0, a1)
     curvature, qa, qg_far = lax.optimization_barrier((curvature, qa, qg_far))
     qg = jnp.where(ring < inner, qg_mine, qg_far)
-    parts = lax.all_to_all(curvature.reshape(ring_size, chunk, cols + 128), RING, 0, 0, tiled=True)
+    parts = lax.all_to_all(curvature, RING, 0, 0, tiled=True)
     mine, total = reduced(parts, cols)
     total = total + moved(total, OTHER_CORE)
     total = total + moved(total, GRADS_PARTNER)

time: 141 us -> 137 us (0.972)
  blocking collectives: 72.7 us -> 70.1 us
    pallas_call x1 -> x0, Pallas kernels: 7.27 us -> none  [curvature_of(): pl.pallas_call(curvature_kernel, in_specs=[pl.BlockSpec(memory_space=pltp...]
    pallas_call x3 -> x4, Pallas kernels: 3.45 us -> 9.69 us  [call(): pl.pallas_call(kernel, in_specs=[there] * scalars + [here] * (len(operand...]
    all_to_all x1, blocking collectives: 34.1 us -> 31.4 us  [shards(): parts = lax.all_to_all(curvature, RING, 0, 0, tiled=True)]
  transfers between devices with their start and end apart: 11 -> 11, of which waited for: 6 -> 6; matrix products, arithmetic and copies ran while one was open for 6% -> 7% of each run, Pallas kernels for 5% -> 5%
where the time goes in v7:
time: 137 us
  blocking collectives  70.1 us (51%)
  waiting for transfers between devices  30.1 us (22%)
  starting transfers between devices  16.9 us (12%)
  Pallas kernels  9.69 us (7%)
  matrix products  8.09 us (6%)
    all_to_all x1, blocking collectives, shards(): parts = lax.all_to_all(curvature, RING, 0, 0, tiled=True)  31.4 us
    ppermute x11, waiting for transfers between devices, moved(): return lax.ppermute(array, BLOCKS, pairs)  30.1 us
    all_to_all x1, blocking collectives, shards(): lax.all_to_all(mine, RING, 0, 0, tiled=True).reshape(2 * width, cols)  24.3 us
    ppermute x11, starting transfers between devices, moved(): return lax.ppermute(array, BLOCKS, pairs)  16.9 us
    all_to_all x1, blocking collectives, summed(): return jnp.sum(lax.all_to_all(parts, axes, 0, 0, tiled=True), axis=0)  14.4 us
    pallas_call x4, Pallas kernels, call(): pl.pallas_call(kernel, in_specs=[there] * scalars + [here] * (len(operand...  9.69 us
    dot_general x4, matrix products, dot(): lax.dot_general(a, b, (contract, ((), ())), preferred_element_type=f32)  8.09 us
  transfers between devices with their start and end apart: 11, of which 6 were waited for; matrix products, arithmetic and copies ran while one was open for 7% of the time, Pallas kernels for 5%

profile of v7, /device:TPU:1, one launch (start us, length us, event | category | flops | bytes accessed | tf_op | source)
XLA Modules:
  0.0 136.8 jit_solution(11959583183470533673)
XLA Ops:
  0.0 0.0 copy-start
  0.0 3.2 %collective-permute-start = (s32[4]{0:T(128)}, s32[4]{0:T(128)S(1)}, u32[]{:S(2)}, u32[]{:S(2)}) collective-permute-start(s32[4]{0:T(128)} %param.9), channel_id=1, source_target_pairs={{0,4},{1,5},{2,6},{3,7},{4,0},{5,1},{6,2},{7,3},{8,12},{9,13},{10,... | collective-permute-start | bytes 56 | tf_op jit(solution)/shard_map/ppermute | solution.py:229
  3.2 0.1 pad.2.clone
  3.3 0.0 copy-done
  3.3 3.8 %convolution_convert_fusion.1.g00 = bf16[640,512]{1,0:T(8,128)(2,1)S(1)} fusion(bf16[2560,640]{1,0:T(8,128)(2,1)S(1)} %copy-done, bf16[512,2560]{1,0:T(8,128)(2,1)} %param.8), kind=kOutput, calls=%fused_computation.1 | convolution fusion | flops 1678049280 | bytes 6553600 | tf_op jit(solution)/shard_map/dot_general | solution.py:29
  7.1 0.0 copy-start.1
  7.1 0.0 collective-permute-done
  7.2 1.9 %collective-permute-start.2 = (bf16[640,512]{1,0:T(8,128)(2,1)S(1)}, bf16[640,512]{1,0:T(8,128)(2,1)S(1)}, u32[]{:S(2)}, u32[]{:S(2)}) collective-permute-start(bf16[640,512]{1,0:T(8,128)(2,1)S(1)} %convolution_convert_fusion.1.g00), channel_id=1, source_target_pairs={{0,4},{1,5},{2,6},{3,7},{4,0},{5,1},{6,2},{7,3},{8,12},{9,13},{10,... | collective-permute-start | bytes 1966088 | tf_op jit(solution)/shard_map/ppermute | solution.py:229
  9.1 1.3 collective-permute-start.1
  10.4 0.0 copy-done.18
  10.4 0.1 add_add_fusion.lengths_ref
  10.4 0.0 copy-done.13
  10.4 0.0 copy-done.19
  10.4 2.2 %convolution_convert_fusion = bf16[512,640]{1,0:T(8,128)(2,1)S(1)} fusion(bf16[512,2560]{1,0:T(8,128)(2,1)S(1)} %copy-done.19, bf16[2560,640]{1,0:T(8,128)(2,1)S(1)} %copy-done.13), kind=kOutput, calls=%fused_computation | convolution fusion | flops 1678049280 | bytes 6553600 | tf_op jit(solution)/shard_map/dot_general | solution.py:29
  12.6 0.0 copy-start.15
  12.6 0.0 collective-permute-done.2.g01
  12.7 0.0 copy-start.3
  12.7 0.4 collective-permute-start.5
  13.1 6.1 %collective-permute-start.4 = (bf16[512,640]{1,0:T(8,128)(2,1)S(1)}, bf16[512,640]{1,0:T(8,128)(2,1)S(1)}, u32[]{:S(2)}, u32[]{:S(2)}) collective-permute-start(bf16[512,640]{1,0:T(8,128)(2,1)S(1)} %convolution_convert_fusion), channel_id=1, source_target_pairs={{0,0},{1,1},{2,2},{3,3},{4,7},{5,6},{6,5},{7,4},{8,8},{9,9},{10,10... | collective-permute-start | bytes 1966088 | tf_op jit(solution)/shard_map/ppermute | solution.py:229
  19.2 0.0 copy-done.14
  19.2 1.4 %fusion.1 = bf16[128,640]{0,1:T(8,128)(2,1)S(1)} fusion(bf16[128,2560]{1,0:T(8,128)(2,1)S(1)} %copy-done.14, bf16[2560,640]{1,0:T(8,128)(2,1)S(1)} %copy-done), kind=kOutput, calls=%fused_computation.8 | convolution fusion | flops 419430400 | bytes 4096000 | tf_op jit(solution)/shard_map/dot_general | solution.py:29
  20.7 0.0 copy-done.15
  20.7 0.0 copy-start.16
  20.7 0.7 convolution_convert_fusion.2
  21.4 19.1 %collective-permute-done.1.g10 = bf16[640,512]{1,0:T(8,128)(2,1)S(1)} collective-permute-done((bf16[640,512]{1,0:T(8,128)(2,1)S(1)}, bf16[640,512]{1,0:T(8,128)(2,1)S(1)}, u32[]{:S(2)}, u32[]{:S(2)}) %collective-permute-start.1) | collective-permute-done | bytes 655392 | tf_op jit(solution)/shard_map/ppermute | solution.py:229
  40.5 0.8 collective-permute-start.3
  41.3 0.0 collective-permute-start.6
  41.3 0.0 collective-permute-start.7
  41.3 3.1 %collective-permute-done.5.a1_ref = bf16[512,640]{1,0:T(8,128)(2,1)S(1)} collective-permute-done((bf16[512,640]{1,0:T(8,128)(2,1)S(1)}, bf16[512,640]{1,0:T(8,128)(2,1)S(1)}, u32[]{:S(2)}, u32[]{:S(2)}) %collective-permute-start.5) | collective-permute-done | bytes 655392 | tf_op jit(solution)/shard_map/ppermute | solution.py:229
  44.4 1.7 %collective-permute-done.4.a0_ref = bf16[512,640]{1,0:T(8,128)(2,1)S(1)} collective-permute-done((bf16[512,640]{1,0:T(8,128)(2,1)S(1)}, bf16[512,640]{1,0:T(8,128)(2,1)S(1)}, u32[]{:S(2)}, u32[]{:S(2)}) %collective-permute-start.4) | collective-permute-done | bytes 655392 | tf_op jit(solution)/shard_map/ppermute | solution.py:229
  46.1 0.0 collective-permute-done.3.g11
  46.1 0.0 copy-done.1
  46.1 0.0 copy-done.3
  46.2 0.0 copy-start.11
  46.2 6.2 %shard_map.73 = bf16[32,208,128]{2,1,0:T(8,128)(2,1)S(1)} custom-call(s32[3,4]{1,0:T(4,128)S(1)} %add_add_fusion.lengths_ref, bf16[640,512]{1,0:T(8,128)(2,1)S(1)} %convolution_convert_fusion.1.g00, bf16[640,512]{1,0:T(8,128)(2,1)S(1)} %collective-permute-done.2.g01, bf16[640,512]{1,0:T(8,128)(2,1)S(1)} %collective-permute-done.1.g10, ...), custom_call_target="tpu_custom_call" | custom-call | tf_op jit(solution)/shard_map/pallas_call | solution.py:48
  52.4 0.0 copy-done.16
  52.4 0.0 collective-permute-done.7
  52.4 0.0 copy-start.17
  52.4 0.0 collective-permute-done.6.qa_ref
  52.4 31.4 %all_to_all.15.parts_ref = bf16[32,208,128]{2,1,0:T(8,128)(2,1)S(1)} all-to-all(bf16[32,208,128]{2,1,0:T(8,128)(2,1)S(1)} %shard_map.73), channel_id=1, replica_groups=mesh['x'=4,'zl'=2,'y'=4,'c'=2,'m'=4] {'x','zl','y'}, dimensions={0} | all-to-all | bytes 3407872 | tf_op jit(solution)/shard_map/all_to_all | solution.py:267
  83.8 0.0 copy-done.5
  83.8 0.0 copy-done.7
  83.8 0.0 copy-done.9
  83.9 0.0 copy-done.11
  83.9 0.3 shard_map.74
  84.2 1.3 collective-permute-start.8
  85.4 0.8 collective-permute-done.8
  86.3 0.0 copy-done.17
  86.3 0.8 collective-permute-start.9
  87.0 0.0 copy-start.10
  87.0 0.0 copy-start.12
  87.1 2.6 %collective-permute-done.9 = f32[8,128]{1,0:T(8,128)S(1)} collective-permute-done((f32[8,128]{1,0:T(8,128)S(1)}, f32[8,128]{1,0:T(8,128)S(1)}, u32[]{:S(2)}, u32[]{:S(2)}) %collective-permute-start.9) | collective-permute-done | bytes 4128 | tf_op jit(solution)/shard_map/ppermute | solution.py:229
  89.6 1.1 collective-permute-start.10
  90.7 0.7 broadcast_select_fusion.qg_ref
  91.5 2.7 %collective-permute-done.10.more_ref = f32[8,128]{1,0:T(8,128)S(1)} collective-permute-done((f32[8,128]{1,0:T(8,128)S(1)}, f32[8,128]{1,0:T(8,128)S(1)}, u32[]{:S(2)}, u32[]{:S(2)}) %collective-permute-start.10) | collective-permute-done | bytes 4128 | tf_op jit(solution)/shard_map/ppermute | solution.py:229
  94.2 0.3 shard_map.75
  94.5 24.3 %all_to_all.16 = bf16[32,40,640]{2,1,0:T(8,128)(2,1)S(1)} all-to-all(bf16[32,40,640]{2,1,0:T(8,128)(2,1)S(1)} %shard_map.75), channel_id=1, replica_groups=mesh['x'=4,'zl'=2,'y'=4,'c'=2,'m'=4] {'x','zl','y'}, dimensions={0} | all-to-all | bytes 3276800 | tf_op jit(solution)/shard_map/all_to_all | solution.py:275
  118.8 0.0 copy-done.2
  118.8 0.0 copy-done.8
  118.8 0.0 copy-done.10
  118.8 0.0 copy-done.12
  118.8 2.9 %shard_map.76 = f32[8,4,128]{2,1,0:T(4,128)S(1)} custom-call(s32[3,4]{1,0:T(4,128)S(1)} %add_add_fusion.lengths_ref, bf16[1280,640]{1,0:T(8,128)(2,1)S(1)} %bitcast.15, bf16[640,512]{1,0:T(8,128)(2,1)S(1)} %copy-done.2, bf16[640,512]{1,0:T(8,128)(2,1)S(1)} %copy-done.4, bf16[640,512]{1,0:T(8,128)(2,1)S(1)} %copy-done.6, bf16[640,512]{1,0:T(8,128)(2,1)S(1)} %copy-done.12, ...), custom_call_target="tpu_custom_call" | custom-call | tf_op jit(solution)/shard_map/pallas_call | solution.py:48
  121.7 14.4 %all_to_all.17 = f32[8,4,128]{2,1,0:T(4,128)S(1)} all-to-all(f32[8,4,128]{2,1,0:T(4,128)S(1)} %shard_map.76), channel_id=1, replica_groups=mesh['x'=4,'zl'=2,'y'=4,'c'=2,'m'=4] {'c','m'}, dimensions={0} | all-to-all | bytes 32768 | tf_op jit(solution)/shard_map/all_to_all | solution.py:233
  136.1 0.6 slice_reduce_fusion
  (17 shorter events, 0.1 us)
Async XLA Ops:
  0.0 3.3 %copy-start = (bf16[2560,640]{1,0:T(8,128)(2,1)S(1)}, bf16[2560,640]{1,0:T(8,128)(2,1)}, u32[]{:S(2)}) copy-start(bf16[2560,640]{1,0:T(8,128)(2,1)} %param.13) | copy-start | bytes 9830404
  0.0 7.1 %collective-permute-start = (s32[4]{0:T(128)}, s32[4]{0:T(128)S(1)}, u32[]{:S(2)}, u32[]{:S(2)}) collective-permute-start(s32[4]{0:T(128)} %param.9), channel_id=1, source_target_pairs={{0,4},{1,5},{2,6},{3,7},{4,0},{5,1},{6,2},{7,3},{8,12},{9,13},{10,... | collective-permute-start | bytes 56 | tf_op jit(solution)/shard_map/ppermute | solution.py:229
  3.3 7.0 %copy-start.18 = (s32[4]{0:T(128)S(1)}, s32[4]{0:T(128)}, u32[]{:S(2)}) copy-start(s32[4]{0:T(128)} %param.9) | copy-start | bytes 52
  3.3 7.1 %copy-start.13 = (bf16[2560,640]{1,0:T(8,128)(2,1)S(1)}, bf16[2560,640]{1,0:T(8,128)(2,1)}, u32[]{:S(2)}) copy-start(bf16[2560,640]{1,0:T(8,128)(2,1)} %param.12) | copy-start | bytes 9830404
  3.3 7.1 %copy-start.19 = (bf16[512,2560]{1,0:T(8,128)(2,1)S(1)}, bf16[512,2560]{1,0:T(8,128)(2,1)}, u32[]{:S(2)}) copy-start(bf16[512,2560]{1,0:T(8,128)(2,1)} %param.7) | copy-start | bytes 7864324
  7.1 39.0 %copy-start.1 = (bf16[640,512]{1,0:T(8,128)(2,1)}, bf16[640,512]{1,0:T(8,128)(2,1)S(1)}, u32[]{:S(2)}) copy-start(bf16[640,512]{1,0:T(8,128)(2,1)S(1)} %convolution_convert_fusion.1.g00) | copy-start | bytes 1966084
  7.2 5.5 %collective-permute-start.2 = (bf16[640,512]{1,0:T(8,128)(2,1)S(1)}, bf16[640,512]{1,0:T(8,128)(2,1)S(1)}, u32[]{:S(2)}, u32[]{:S(2)}) collective-permute-start(bf16[640,512]{1,0:T(8,128)(2,1)S(1)} %convolution_convert_fusion.1.g00), channel_id=1, source_target_pairs={{0,4},{1,5},{2,6},{3,7},{4,0},{5,1},{6,2},{7,3},{8,12},{9,13},{10,... | collective-permute-start | bytes 1966088 | tf_op jit(solution)/shard_map/ppermute | solution.py:229
  9.1 31.4 %collective-permute-start.1 = (bf16[640,512]{1,0:T(8,128)(2,1)S(1)}, bf16[640,512]{1,0:T(8,128)(2,1)S(1)}, u32[]{:S(2)}, u32[]{:S(2)}) collective-permute-start(bf16[640,512]{1,0:T(8,128)(2,1)S(1)} %convolution_convert_fusion.1.g00), channel_id=1, source_target_pairs={{0,1},{1,0},{2,3},{3,2},{4,5},{5,4},{6,7},{7,6},{8,9},{9,8},{10,11... | collective-permute-start | bytes 1966088 | tf_op jit(solution)/shard_map/ppermute | solution.py:229
  10.4 8.8 %copy-start.14 = (bf16[128,2560]{1,0:T(8,128)(2,1)S(1)}, bf16[128,2560]{1,0:T(8,128)(2,1)}, u32[]{:S(2)}) copy-start(bf16[128,2560]{1,0:T(8,128)(2,1)} %param.11) | copy-start | bytes 1966084
  12.6 8.0 %copy-start.15 = (bf16[128,2560]{1,0:T(8,128)(2,1)S(1)}, bf16[128,2560]{1,0:T(8,128)(2,1)}, u32[]{:S(2)}) copy-start(bf16[128,2560]{1,0:T(8,128)(2,1)} %param.10) | copy-start | bytes 1966084
  12.7 33.5 %copy-start.3 = (bf16[640,512]{1,0:T(8,128)(2,1)}, bf16[640,512]{1,0:T(8,128)(2,1)S(1)}, u32[]{:S(2)}) copy-start(bf16[640,512]{1,0:T(8,128)(2,1)S(1)} %collective-permute-done.2.g01) | copy-start | bytes 1966084
  12.7 31.7 %collective-permute-start.5 = (bf16[512,640]{1,0:T(8,128)(2,1)S(1)}, bf16[512,640]{1,0:T(8,128)(2,1)S(1)}, u32[]{:S(2)}, u32[]{:S(2)}) collective-permute-start(bf16[512,640]{1,0:T(8,128)(2,1)S(1)} %convolution_convert_fusion), channel_id=1, source_target_pairs={{0,7},{1,6},{2,5},{3,4},{4,0},{5,1},{6,2},{7,3},{8,15},{9,14},{10,... | collective-permute-start | bytes 1966088 | tf_op jit(solution)/shard_map/ppermute | solution.py:229
  13.1 33.0 %collective-permute-start.4 = (bf16[512,640]{1,0:T(8,128)(2,1)S(1)}, bf16[512,640]{1,0:T(8,128)(2,1)S(1)}, u32[]{:S(2)}, u32[]{:S(2)}) collective-permute-start(bf16[512,640]{1,0:T(8,128)(2,1)S(1)} %convolution_convert_fusion), channel_id=1, source_target_pairs={{0,0},{1,1},{2,2},{3,3},{4,7},{5,6},{6,5},{7,4},{8,8},{9,9},{10,10... | collective-permute-start | bytes 1966088 | tf_op jit(solution)/shard_map/ppermute | solution.py:229
  20.7 31.7 %copy-start.16 = (bf16[40,128]{1,0:T(8,128)(2,1)}, bf16[40,128]{1,0:T(8,128)(2,1)S(1)}, u32[]{:S(2)}) copy-start(bf16[40,128]{1,0:T(8,128)(2,1)S(1)} %fusion) | copy-start | bytes 30724
  40.5 43.3 %copy-start.5 = (bf16[640,512]{1,0:T(8,128)(2,1)}, bf16[640,512]{1,0:T(8,128)(2,1)S(1)}, u32[]{:S(2)}) copy-start(bf16[640,512]{1,0:T(8,128)(2,1)S(1)} %collective-permute-done.1.g10) | copy-start | bytes 1966084
  40.5 5.6 %collective-permute-start.3 = (bf16[640,512]{1,0:T(8,128)(2,1)S(1)}, bf16[640,512]{1,0:T(8,128)(2,1)S(1)}, u32[]{:S(2)}, u32[]{:S(2)}) collective-permute-start(bf16[640,512]{1,0:T(8,128)(2,1)S(1)} %collective-permute-done.1.g10), channel_id=1, source_target_pairs={{0,4},{1,5},{2,6},{3,7},{4,0},{5,1},{6,2},{7,3},{8,12},{9,13},{10,... | collective-permute-start | bytes 1966088 | tf_op jit(solution)/shard_map/ppermute | solution.py:229
  41.3 11.1 %collective-permute-start.6 = (bf16[128,640]{1,0:T(8,128)(2,1)S(1)}, bf16[128,640]{1,0:T(8,128)(2,1)S(1)}, u32[]{:S(2)}, u32[]{:S(2)}) collective-permute-start(bf16[128,640]{1,0:T(8,128)(2,1)S(1)} %convolution_convert_fusion.2), channel_id=1, source_target_pairs={{0,7},{1,6},{2,5},{3,4},{4,0},{5,1},{6,2},{7,3},{8,15},{9,14},{10,... | collective-permute-start | bytes 491528 | tf_op jit(solution)/shard_map/ppermute | solution.py:229
  41.3 11.1 %collective-permute-start.7 = (bf16[40,128]{1,0:T(8,128)(2,1)S(1)}, bf16[40,128]{1,0:T(8,128)(2,1)S(1)}, u32[]{:S(2)}, u32[]{:S(2)}) collective-permute-start(bf16[40,128]{1,0:T(8,128)(2,1)S(1)} %fusion), channel_id=1, source_target_pairs={{0,1},{1,0},{2,3},{3,2},{4,5},{5,4},{6,7},{7,6},{8,9},{9,8},{10,11... | collective-permute-start | bytes 30728 | tf_op jit(solution)/shard_map/ppermute | solution.py:229
  44.4 39.4 %copy-start.7 = (bf16[512,640]{1,0:T(8,128)(2,1)}, bf16[512,640]{1,0:T(8,128)(2,1)S(1)}, u32[]{:S(2)}) copy-start(bf16[512,640]{1,0:T(8,128)(2,1)S(1)} %collective-permute-done.5.a1_ref) | copy-start | bytes 1966084
  46.1 37.7 %copy-start.9 = (bf16[512,640]{1,0:T(8,128)(2,1)}, bf16[512,640]{1,0:T(8,128)(2,1)S(1)}, u32[]{:S(2)}) copy-start(bf16[512,640]{1,0:T(8,128)(2,1)S(1)} %collective-permute-done.4.a0_ref) | copy-start | bytes 1966084
  46.2 37.7 %copy-start.11 = (bf16[640,512]{1,0:T(8,128)(2,1)}, bf16[640,512]{1,0:T(8,128)(2,1)S(1)}, u32[]{:S(2)}) copy-start(bf16[640,512]{1,0:T(8,128)(2,1)S(1)} %collective-permute-done.3.g11) | copy-start | bytes 1966084
  52.4 33.8 %copy-start.17 = (bf16[40,128]{1,0:T(8,128)(2,1)}, bf16[40,128]{1,0:T(8,128)(2,1)S(1)}, u32[]{:S(2)}) copy-start(bf16[40,128]{1,0:T(8,128)(2,1)S(1)} %collective-permute-done.7) | copy-start | bytes 30724
  84.2 2.1 %collective-permute-start.8 = (f32[8,128]{1,0:T(8,128)S(1)}, f32[8,128]{1,0:T(8,128)S(1)}, u32[]{:S(2)}, u32[]{:S(2)}) collective-permute-start(f32[8,128]{1,0:T(8,128)S(1)} %get-tuple-element.34), channel_id=1, source_target_pairs={{0,4},{1,5},{2,6},{3,7},{4,0},{5,1},{6,2},{7,3},{8,12},{9,13},{10,... | collective-permute-start | bytes 12296 | tf_op jit(solution)/shard_map/ppermute | solution.py:229
  86.3 3.4 %collective-permute-start.9 = (f32[8,128]{1,0:T(8,128)S(1)}, f32[8,128]{1,0:T(8,128)S(1)}, u32[]{:S(2)}, u32[]{:S(2)}) collective-permute-start(f32[8,128]{1,0:T(8,128)S(1)} %add.18), channel_id=1, source_target_pairs={{0,1},{1,0},{2,3},{3,2},{4,5},{5,4},{6,7},{7,6},{8,9},{9,8},{10,11... | collective-permute-start | bytes 12296 | tf_op jit(solution)/shard_map/ppermute | solution.py:229
  87.0 31.7 %copy-start.2 = (bf16[640,512]{1,0:T(8,128)(2,1)S(1)}, bf16[640,512]{1,0:T(8,128)(2,1)}, u32[]{:S(2)}) copy-start(bf16[640,512]{1,0:T(8,128)(2,1)} %copy-done.1) | copy-start | bytes 1966084
  87.0 31.7 %copy-start.4 = (bf16[640,512]{1,0:T(8,128)(2,1)S(1)}, bf16[640,512]{1,0:T(8,128)(2,1)}, u32[]{:S(2)}) copy-start(bf16[640,512]{1,0:T(8,128)(2,1)} %copy-done.3) | copy-start | bytes 1966084
  87.0 31.7 %copy-start.6 = (bf16[640,512]{1,0:T(8,128)(2,1)S(1)}, bf16[640,512]{1,0:T(8,128)(2,1)}, u32[]{:S(2)}) copy-start(bf16[640,512]{1,0:T(8,128)(2,1)} %copy-done.5) | copy-start | bytes 1966084
  87.0 31.7 %copy-start.8 = (bf16[512,640]{1,0:T(8,128)(2,1)S(1)}, bf16[512,640]{1,0:T(8,128)(2,1)}, u32[]{:S(2)}) copy-start(bf16[512,640]{1,0:T(8,128)(2,1)} %copy-done.7) | copy-start | bytes 1966084
  87.0 31.7 %copy-start.10 = (bf16[512,640]{1,0:T(8,128)(2,1)S(1)}, bf16[512,640]{1,0:T(8,128)(2,1)}, u32[]{:S(2)}) copy-start(bf16[512,640]{1,0:T(8,128)(2,1)} %copy-done.9) | copy-start | bytes 1966084
  87.0 31.7 %copy-start.12 = (bf16[640,512]{1,0:T(8,128)(2,1)S(1)}, bf16[640,512]{1,0:T(8,128)(2,1)}, u32[]{:S(2)}) copy-start(bf16[640,512]{1,0:T(8,128)(2,1)} %copy-done.11) | copy-start | bytes 1966084
  89.6 4.6 %collective-permute-start.10 = (f32[8,128]{1,0:T(8,128)S(1)}, f32[8,128]{1,0:T(8,128)S(1)}, u32[]{:S(2)}, u32[]{:S(2)}) collective-permute-start(f32[8,128]{1,0:T(8,128)S(1)} %add.19.total_ref), channel_id=1, source_target_pairs={{0,3},{1,2},{2,1},{3,0},{4,7},{5,6},{6,5},{7,4},{8,11},{9,10},{10,... | collective-permute-start | bytes 12296 | tf_op jit(solution)/shard_map/ppermute | solution.py:229

commit v8 on v7

--- a/solution.py
+++ b/solution.py
@@ -183,35 +183,23 @@
     )(chunk, total, more, qg, qa)[0]
 
 
-def score_kernel(lengths_ref, p_ref, g00, g01, g10, g11, a0_ref, a1_ref, out_ref):
-    width, tokens = g00.shape
-    count = lengths_ref.shape[1]
+def score_kernel(which, lengths_ref, p_ref, near_ref, far_ref, acts_ref, out_ref):
+    width, tokens = near_ref.shape
     lane = lax.broadcasted_iota(jnp.int32, (1, tokens), 1)
-    line = lax.broadcasted_iota(jnp.int32, (count, 1), 0)
-    found = []
-    for b, (near, far, acts) in enumerate(((g00, g10, a0_ref), (g01, g11, a1_ref))):
-        sums = jnp.zeros((1, tokens), f32)
-        for member, grads in enumerate((near, far)):
-            product = dot(p_ref[member * width : (member + 1) * width, :], acts[...], ((1,), (1,)))
-            sums = sums + jnp.sum(grads[...].astype(f32) * product, axis=0, keepdims=True)
-        rows = jnp.zeros((count, 1), f32)
-        for j, (start, finish) in enumerate(bounds_of(lengths_ref, b)):
-            inside = (lane >= start) & (lane < finish)
-            value = jnp.sum(jnp.where(inside, sums, 0.0), axis=1, keepdims=True)
-            rows = jnp.where(line == j, value, rows)
-        found.append(jnp.broadcast_to(rows, (count, 128)))
-    first = lengths_ref[2, 0] == 0
-    half = out_ref.shape[0] // 2
-    for i in range(half):
-        out_ref[i] = jnp.where(first, found[0], found[1])
-        out_ref[half + i] = jnp.where(first, found[1], found[0])
-
-
-def scores_of(lengths, precond, g00, g01, g10, g11, a0, a1):
-    shape = (lax.axis_size("c") * lax.axis_size("m"), lengths.shape[1], 128)
-    return local_call(score_kernel, [jax.ShapeDtypeStruct(shape, f32)])(
-        lengths, precond, g00, g01, g10, g11, a0, a1
-    )[0]
+    sums = jnp.zeros((1, tokens), f32)
+    for member, grads in enumerate((near_ref, far_ref)):
+        product = dot(p_ref[member * width : (member + 1) * width, :], acts_ref[...], ((1,), (1,)))
+        sums = sums + jnp.sum(grads[...].astype(f32) * product, axis=0, keepdims=True)
+    for j, (start, finish) in enumerate(bounds_of(lengths_ref, which)):
+        inside = (lane >= start) & (lane < finish)
+        value = jnp.sum(jnp.where(inside, sums, 0.0), axis=1, keepdims=True)
+        out_ref[j : j + 1, :] = jnp.broadcast_to(value, (1, out_ref.shape[1]))
+
+
+def scores_of(which, lengths, precond, near, far, acts):
+    return local_call(
+        functools.partial(score_kernel, which), [jax.ShapeDtypeStruct((lengths.shape[1], LANES), f32)]
+    )(lengths, precond, near, far, acts)[0]
 
 
 def routes(f):
@@ -227,10 +215,6 @@
 
 def moved(array, pairs):
     return lax.ppermute(array, BLOCKS, pairs)
-
-
-def summed(parts, axes):
-    return jnp.sum(lax.all_to_all(parts, axes, 0, 0, tiled=True), axis=0)
 
 
 def shards(train_acts, train_grads, lengths, query_acts, query_grads, basis_in, basis_out):
@@ -248,8 +232,7 @@
     acts, g01, query_acts, query_grads = lax.optimization_barrier((acts, g01, query_acts, query_grads))
     a1 = moved(acts, ACTS_OTHER)
     a0 = moved(acts, ACTS_SAME)
-    core = lax.broadcast_in_dim(lax.axis_index("c"), lengths.shape, ())
-    both = jnp.stack([lengths, other, core])
+    both = jnp.stack([lengths, other])
 
     width, cols = g00.shape[0], a0.shape[1]
     chunk = 2 * width // ring_size
@@ -273,8 +256,11 @@
     damping_scale = DAMPING_RATIO * scale / (2 * width * cols * blocks)
     mine = precond_of(ring_size, scale, damping_scale, mine, total, more, qg, qa)
     precond = lax.all_to_all(mine, RING, 0, 0, tiled=True).reshape(2 * width, cols)
-    found = scores_of(both, precond, g00, g01, g10, g11, a0, a1)
-    return summed(found, BLOCKS)[:, 0].reshape(1, count)
+    found = moved(scores_of(1, both, precond, g01, g11, a1), OTHER_CORE)
+    found = found + scores_of(0, both, precond, g00, g10, a0)
+    found = found + moved(found, GRADS_PARTNER)
+    found = found + moved(found, ACTS_PARTNER)
+    return found[:, 0].reshape(1, count)
 
 
 def solution(mesh):

time: 137 us -> 136 us (level)
  blocking collectives: 70.1 us -> 55.7 us
  waiting for transfers between devices: 30.1 us -> 37.2 us
  starting transfers between devices: 16.9 us -> 22.1 us
    all_to_all x1 -> x0, blocking collectives: 14.4 us -> none  [summed(): return jnp.sum(lax.all_to_all(parts, axes, 0, 0, tiled=True), axis=0)]
    ppermute x11 -> x14, waiting for transfers between devices: 30.1 us -> 37.2 us  [moved(): return lax.ppermute(array, BLOCKS, pairs)]
    ppermute x11 -> x14, starting transfers between devices: 16.9 us -> 22.1 us  [moved(): return lax.ppermute(array, BLOCKS, pairs)]
    pallas_call x4 -> x5, Pallas kernels: 9.69 us -> 10.6 us  [call(): pl.pallas_call(kernel, in_specs=[there] * scalars + [here] * (len(operand...]
  transfers between devices with their start and end apart: 11 -> 14, of which waited for: 6 -> 8; matrix products, arithmetic and copies ran while one was open for 7% -> 7% of each run, Pallas kernels for 5% -> 6%
where the time goes in v8:
time: 136 us; the launch traced here: 135 us
  blocking collectives  55.7 us (41%)
  waiting for transfers between devices  37.2 us (27%)
  starting transfers between devices  22.1 us (16%)
  Pallas kernels  10.6 us (8%)
  matrix products  8.1 us (6%)
    ppermute x14, waiting for transfers between devices, moved(): return lax.ppermute(array, BLOCKS, pairs)  37.2 us
    all_to_all x1, blocking collectives, shards(): parts = lax.all_to_all(curvature, RING, 0, 0, tiled=True)  31.3 us
    all_to_all x1, blocking collectives, shards(): lax.all_to_all(mine, RING, 0, 0, tiled=True).reshape(2 * width, cols)  24.4 us
    ppermute x14, starting transfers between devices, moved(): return lax.ppermute(array, BLOCKS, pairs)  22.1 us
    pallas_call x5, Pallas kernels, call(): pl.pallas_call(kernel, in_specs=[there] * scalars + [here] * (len(operand...  10.6 us
    dot_general x4, matrix products, dot(): lax.dot_general(a, b, (contract, ((), ())), preferred_element_type=f32)  8.1 us
  transfers between devices with their start and end apart: 14, of which 8 were waited for; matrix products, arithmetic and copies ran while one was open for 7% of the time, Pallas kernels for 6%

profile of v8, /device:TPU:1, one launch (start us, length us, event | category | flops | bytes accessed | tf_op | source)
XLA Modules:
  0.0 135.5 jit_solution(8795914501692998329)
XLA Ops:
  0.0 0.0 copy-start
  0.0 3.2 %collective-permute-start = (s32[4]{0:T(128)}, s32[4]{0:T(128)S(1)}, u32[]{:S(2)}, u32[]{:S(2)}) collective-permute-start(s32[4]{0:T(128)} %param.9), channel_id=1, source_target_pairs={{0,4},{1,5},{2,6},{3,7},{4,0},{5,1},{6,2},{7,3},{8,12},{9,13},{10,... | collective-permute-start | bytes 56 | tf_op jit(solution)/shard_map/ppermute | solution.py:217
  3.2 0.0 copy-done
  3.3 3.8 %convolution_convert_fusion.1.g00.near_ref = bf16[640,512]{1,0:T(8,128)(2,1)S(1)} fusion(bf16[2560,640]{1,0:T(8,128)(2,1)S(1)} %copy-done, bf16[512,2560]{1,0:T(8,128)(2,1)} %param.8), kind=kOutput, calls=%fused_computation.1 | convolution fusion | flops 1678049280 | bytes 6553600 | tf_op jit(solution)/shard_map/dot_general | solution.py:29
  7.1 0.0 copy-start.1
  7.1 0.0 collective-permute-done
  7.1 2.0 %collective-permute-start.2 = (bf16[640,512]{1,0:T(8,128)(2,1)S(1)}, bf16[640,512]{1,0:T(8,128)(2,1)S(1)}, u32[]{:S(2)}, u32[]{:S(2)}) collective-permute-start(bf16[640,512]{1,0:T(8,128)(2,1)S(1)} %convolution_convert_fusion.1.g00.near_ref), channel_id=1, source_target_pairs={{0,4},{1,5},{2,6},{3,7},{4,0},{5,1},{6,2},{7,3},{8,12},{9,13},{10,... | collective-permute-start | bytes 1966088 | tf_op jit(solution)/shard_map/ppermute | solution.py:217
  9.1 1.3 collective-permute-start.1
  10.4 0.0 copy-done.18
  10.4 0.0 copy-done.13
  10.4 0.0 copy-done.19
  10.4 0.0 copy-start.14
  10.4 2.2 %convolution_convert_fusion = bf16[512,640]{1,0:T(8,128)(2,1)S(1)} fusion(bf16[512,2560]{1,0:T(8,128)(2,1)S(1)} %copy-done.19, bf16[2560,640]{1,0:T(8,128)(2,1)S(1)} %copy-done.13), kind=kOutput, calls=%fused_computation | convolution fusion | flops 1678049280 | bytes 6553600 | tf_op jit(solution)/shard_map/dot_general | solution.py:29
  12.6 0.0 copy-start.15
  12.6 0.0 collective-permute-done.2.g01.near_ref
  12.6 0.0 copy-start.5
  12.6 0.4 collective-permute-start.5
  13.1 6.1 %collective-permute-start.4 = (bf16[512,640]{1,0:T(8,128)(2,1)S(1)}, bf16[512,640]{1,0:T(8,128)(2,1)S(1)}, u32[]{:S(2)}, u32[]{:S(2)}) collective-permute-start(bf16[512,640]{1,0:T(8,128)(2,1)S(1)} %convolution_convert_fusion), channel_id=1, source_target_pairs={{0,0},{1,1},{2,2},{3,3},{4,7},{5,6},{6,5},{7,4},{8,8},{9,9},{10,10... | collective-permute-start | bytes 1966088 | tf_op jit(solution)/shard_map/ppermute | solution.py:217
  19.2 0.0 copy-done.14
  19.2 1.4 %fusion.1 = bf16[128,640]{0,1:T(8,128)(2,1)S(1)} fusion(bf16[128,2560]{1,0:T(8,128)(2,1)S(1)} %copy-done.14, bf16[2560,640]{1,0:T(8,128)(2,1)S(1)} %copy-done), kind=kOutput, calls=%fused_computation.8 | convolution fusion | flops 419430400 | bytes 4096000 | tf_op jit(solution)/shard_map/dot_general | solution.py:29
  20.6 0.0 copy-done.15
  20.7 0.0 copy-start.16
  20.7 0.7 convolution_convert_fusion.2
  21.4 19.2 %collective-permute-done.1.g10.far_ref = bf16[640,512]{1,0:T(8,128)(2,1)S(1)} collective-permute-done((bf16[640,512]{1,0:T(8,128)(2,1)S(1)}, bf16[640,512]{1,0:T(8,128)(2,1)S(1)}, u32[]{:S(2)}, u32[]{:S(2)}) %collective-permute-start.1) | collective-permute-done | bytes 655392 | tf_op jit(solution)/shard_map/ppermute | solution.py:217
  40.5 0.8 collective-permute-start.3
  41.3 0.0 collective-permute-start.6
  41.3 0.0 collective-permute-start.7
  41.3 3.1 %collective-permute-done.5.a1_ref.acts_ref = bf16[512,640]{1,0:T(8,128)(2,1)S(1)} collective-permute-done((bf16[512,640]{1,0:T(8,128)(2,1)S(1)}, bf16[512,640]{1,0:T(8,128)(2,1)S(1)}, u32[]{:S(2)}, u32[]{:S(2)}) %collective-permute-start.5) | collective-permute-done | bytes 655392 | tf_op jit(solution)/shard_map/ppermute | solution.py:217
  44.4 1.7 %collective-permute-done.4.a0_ref.acts_ref = bf16[512,640]{1,0:T(8,128)(2,1)S(1)} collective-permute-done((bf16[512,640]{1,0:T(8,128)(2,1)S(1)}, bf16[512,640]{1,0:T(8,128)(2,1)S(1)}, u32[]{:S(2)}, u32[]{:S(2)}) %collective-permute-start.4) | collective-permute-done | bytes 655392 | tf_op jit(solution)/shard_map/ppermute | solution.py:217
  46.1 0.0 collective-permute-done.3.g11.far_ref
  46.1 0.0 copy-done.1
  46.1 0.0 copy-done.5
  46.1 0.0 copy-start.11
  46.1 6.3 %shard_map.73 = bf16[32,208,128]{2,1,0:T(8,128)(2,1)S(1)} custom-call(s32[2,4]{1,0:T(2,128)S(1)} %pad_add_fusion.lengths_ref, bf16[640,512]{1,0:T(8,128)(2,1)S(1)} %convolution_convert_fusion.1.g00.near_ref, bf16[640,512]{1,0:T(8,128)(2,1)S(1)} %collective-permute-done.2.g01.near_ref, bf16[640,512]{1,0:T(8,128)(2,1)S(1)} %collective-permute-done.1.g10.far_ref, ...), custom_call_target="tpu_custom_call" | custom-call | tf_op jit(solution)/shard_map/pallas_call | solution.py:48
  52.4 0.0 copy-done.16
  52.5 0.0 collective-permute-done.7
  52.5 0.0 copy-start.17
  52.5 0.0 collective-permute-done.6.qa_ref
  52.5 31.3 %all_to_all.10.parts_ref = bf16[32,208,128]{2,1,0:T(8,128)(2,1)S(1)} all-to-all(bf16[32,208,128]{2,1,0:T(8,128)(2,1)S(1)} %shard_map.73), channel_id=1, replica_groups=mesh['x'=4,'zl'=2,'y'=4,'c'=2,'m'=4] {'x','zl','y'}, dimensions={0} | all-to-all | bytes 3407872 | tf_op jit(solution)/shard_map/all_to_all | solution.py:250
  83.8 0.0 copy-done.3
  83.8 0.0 copy-done.9
  83.8 0.0 copy-done.7
  83.8 0.0 copy-done.11
  83.8 0.3 shard_map.74
  84.1 1.3 collective-permute-start.8
  85.4 0.8 collective-permute-done.8
  86.2 0.0 copy-done.17
  86.2 0.7 collective-permute-start.9
  86.9 2.6 %collective-permute-done.9 = f32[8,128]{1,0:T(8,128)S(1)} collective-permute-done((f32[8,128]{1,0:T(8,128)S(1)}, f32[8,128]{1,0:T(8,128)S(1)}, u32[]{:S(2)}, u32[]{:S(2)}) %collective-permute-start.9) | collective-permute-done | bytes 4128 | tf_op jit(solution)/shard_map/ppermute | solution.py:217
  89.6 1.1 collective-permute-start.10
  90.7 0.7 broadcast_select_fusion.qg_ref
  91.4 2.7 %collective-permute-done.10.more_ref = f32[8,128]{1,0:T(8,128)S(1)} collective-permute-done((f32[8,128]{1,0:T(8,128)S(1)}, f32[8,128]{1,0:T(8,128)S(1)}, u32[]{:S(2)}, u32[]{:S(2)}) %collective-permute-start.10) | collective-permute-done | bytes 4128 | tf_op jit(solution)/shard_map/ppermute | solution.py:217
  94.2 0.3 shard_map.75
  94.5 24.4 %all_to_all.11 = bf16[32,40,640]{2,1,0:T(8,128)(2,1)S(1)} all-to-all(bf16[32,40,640]{2,1,0:T(8,128)(2,1)S(1)} %shard_map.75), channel_id=1, replica_groups=mesh['x'=4,'zl'=2,'y'=4,'c'=2,'m'=4] {'x','zl','y'}, dimensions={0} | all-to-all | bytes 3276800 | tf_op jit(solution)/shard_map/all_to_all | solution.py:258
  118.9 0.0 copy-done.10
  118.9 1.9 %shard_map.76 = f32[4,128]{1,0:T(4,128)S(1)} custom-call(s32[2,4]{1,0:T(2,128)S(1)} %pad_add_fusion.lengths_ref, bf16[1280,640]{1,0:T(8,128)(2,1)S(1)} %bitcast.14, bf16[640,512]{1,0:T(8,128)(2,1)S(1)} %copy-done.6, bf16[640,512]{1,0:T(8,128)(2,1)S(1)} %copy-done.12, bf16[512,640]{1,0:T(8,128)(2,1)S(1)} %copy-done.10), custom_call_target="tpu_custom_call" | custom-call | tf_op jit(solution)/shard_map/pallas_call | solution.py:48
  120.7 4.3 %collective-permute-start.11 = (f32[4,128]{1,0:T(4,128)S(1)}, f32[4,128]{1,0:T(4,128)S(1)}, u32[]{:S(2)}, u32[]{:S(2)}) collective-permute-start(f32[4,128]{1,0:T(4,128)S(1)} %shard_map.76), channel_id=1, source_target_pairs={{0,4},{1,5},{2,6},{3,7},{4,0},{5,1},{6,2},{7,3},{8,12},{9,13},{10,... | collective-permute-start | bytes 6152 | tf_op jit(solution)/shard_map/ppermute | solution.py:217
  125.0 1.8 %shard_map.77 = f32[4,128]{1,0:T(4,128)S(1)} custom-call(s32[2,4]{1,0:T(2,128)S(1)} %pad_add_fusion.lengths_ref, bf16[1280,640]{1,0:T(8,128)(2,1)S(1)} %bitcast.15, bf16[640,512]{1,0:T(8,128)(2,1)S(1)} %copy-done.2, bf16[640,512]{1,0:T(8,128)(2,1)S(1)} %copy-done.4, bf16[512,640]{1,0:T(8,128)(2,1)S(1)} %copy-done.8), custom_call_target="tpu_custom_call" | custom-call | tf_op jit(solution)/shard_map/pallas_call | solution.py:48
  126.9 0.0 collective-permute-done.11
  126.9 0.3 collective-permute-start.12
  127.2 3.1 %collective-permute-done.12 = f32[4,128]{1,0:T(4,128)S(1)} collective-permute-done((f32[4,128]{1,0:T(4,128)S(1)}, f32[4,128]{1,0:T(4,128)S(1)}, u32[]{:S(2)}, u32[]{:S(2)}) %collective-permute-start.12) | collective-permute-done | bytes 2080 | tf_op jit(solution)/shard_map/ppermute | solution.py:217
  130.3 0.6 collective-permute-start.13
  130.9 3.9 %collective-permute-done.13 = f32[4,128]{1,0:T(4,128)S(1)} collective-permute-done((f32[4,128]{1,0:T(4,128)S(1)}, f32[4,128]{1,0:T(4,128)S(1)}, u32[]{:S(2)}, u32[]{:S(2)}) %collective-permute-start.13) | collective-permute-done | bytes 2080 | tf_op jit(solution)/shard_map/ppermute | solution.py:217
  134.9 0.6 slice_reduce_fusion
  (24 shorter events, 0.1 us)
Async XLA Ops:
  0.0 3.2 %copy-start = (bf16[2560,640]{1,0:T(8,128)(2,1)S(1)}, bf16[2560,640]{1,0:T(8,128)(2,1)}, u32[]{:S(2)}) copy-start(bf16[2560,640]{1,0:T(8,128)(2,1)} %param.13) | copy-start | bytes 9830404
  0.0 7.1 %collective-permute-start = (s32[4]{0:T(128)}, s32[4]{0:T(128)S(1)}, u32[]{:S(2)}, u32[]{:S(2)}) collective-permute-start(s32[4]{0:T(128)} %param.9), channel_id=1, source_target_pairs={{0,4},{1,5},{2,6},{3,7},{4,0},{5,1},{6,2},{7,3},{8,12},{9,13},{10,... | collective-permute-start | bytes 56 | tf_op jit(solution)/shard_map/ppermute | solution.py:217
  3.2 7.1 %copy-start.18 = (s32[4]{0:T(128)S(1)}, s32[4]{0:T(128)}, u32[]{:S(2)}) copy-start(s32[4]{0:T(128)} %param.9) | copy-start | bytes 52
  3.2 7.1 %copy-start.13 = (bf16[2560,640]{1,0:T(8,128)(2,1)S(1)}, bf16[2560,640]{1,0:T(8,128)(2,1)}, u32[]{:S(2)}) copy-start(bf16[2560,640]{1,0:T(8,128)(2,1)} %param.12) | copy-start | bytes 9830404
  3.3 7.1 %copy-start.19 = (bf16[512,2560]{1,0:T(8,128)(2,1)S(1)}, bf16[512,2560]{1,0:T(8,128)(2,1)}, u32[]{:S(2)}) copy-start(bf16[512,2560]{1,0:T(8,128)(2,1)} %param.7) | copy-start | bytes 7864324
  7.1 39.0 %copy-start.1 = (bf16[640,512]{1,0:T(8,128)(2,1)}, bf16[640,512]{1,0:T(8,128)(2,1)S(1)}, u32[]{:S(2)}) copy-start(bf16[640,512]{1,0:T(8,128)(2,1)S(1)} %convolution_convert_fusion.1.g00.near_ref) | copy-start | bytes 1966084
  7.1 5.5 %collective-permute-start.2 = (bf16[640,512]{1,0:T(8,128)(2,1)S(1)}, bf16[640,512]{1,0:T(8,128)(2,1)S(1)}, u32[]{:S(2)}, u32[]{:S(2)}) collective-permute-start(bf16[640,512]{1,0:T(8,128)(2,1)S(1)} %convolution_convert_fusion.1.g00.near_ref), channel_id=1, source_target_pairs={{0,4},{1,5},{2,6},{3,7},{4,0},{5,1},{6,2},{7,3},{8,12},{9,13},{10,... | collective-permute-start | bytes 1966088 | tf_op jit(solution)/shard_map/ppermute | solution.py:217
  9.1 31.4 %collective-permute-start.1 = (bf16[640,512]{1,0:T(8,128)(2,1)S(1)}, bf16[640,512]{1,0:T(8,128)(2,1)S(1)}, u32[]{:S(2)}, u32[]{:S(2)}) collective-permute-start(bf16[640,512]{1,0:T(8,128)(2,1)S(1)} %convolution_convert_fusion.1.g00.near_ref), channel_id=1, source_target_pairs={{0,1},{1,0},{2,3},{3,2},{4,5},{5,4},{6,7},{7,6},{8,9},{9,8},{10,11... | collective-permute-start | bytes 1966088 | tf_op jit(solution)/shard_map/ppermute | solution.py:217
  10.4 8.8 %copy-start.14 = (bf16[128,2560]{1,0:T(8,128)(2,1)S(1)}, bf16[128,2560]{1,0:T(8,128)(2,1)}, u32[]{:S(2)}) copy-start(bf16[128,2560]{1,0:T(8,128)(2,1)} %param.11) | copy-start | bytes 1966084
  12.6 8.0 %copy-start.15 = (bf16[128,2560]{1,0:T(8,128)(2,1)S(1)}, bf16[128,2560]{1,0:T(8,128)(2,1)}, u32[]{:S(2)}) copy-start(bf16[128,2560]{1,0:T(8,128)(2,1)} %param.10) | copy-start | bytes 1966084
  12.6 33.5 %copy-start.5 = (bf16[640,512]{1,0:T(8,128)(2,1)}, bf16[640,512]{1,0:T(8,128)(2,1)S(1)}, u32[]{:S(2)}) copy-start(bf16[640,512]{1,0:T(8,128)(2,1)S(1)} %collective-permute-done.2.g01.near_ref) | copy-start | bytes 1966084
  12.6 31.7 %collective-permute-start.5 = (bf16[512,640]{1,0:T(8,128)(2,1)S(1)}, bf16[512,640]{1,0:T(8,128)(2,1)S(1)}, u32[]{:S(2)}, u32[]{:S(2)}) collective-permute-start(bf16[512,640]{1,0:T(8,128)(2,1)S(1)} %convolution_convert_fusion), channel_id=1, source_target_pairs={{0,7},{1,6},{2,5},{3,4},{4,0},{5,1},{6,2},{7,3},{8,15},{9,14},{10,... | collective-permute-start | bytes 1966088 | tf_op jit(solution)/shard_map/ppermute | solution.py:217
  13.1 33.0 %collective-permute-start.4 = (bf16[512,640]{1,0:T(8,128)(2,1)S(1)}, bf16[512,640]{1,0:T(8,128)(2,1)S(1)}, u32[]{:S(2)}, u32[]{:S(2)}) collective-permute-start(bf16[512,640]{1,0:T(8,128)(2,1)S(1)} %convolution_convert_fusion), channel_id=1, source_target_pairs={{0,0},{1,1},{2,2},{3,3},{4,7},{5,6},{6,5},{7,4},{8,8},{9,9},{10,10... | collective-permute-start | bytes 1966088 | tf_op jit(solution)/shard_map/ppermute | solution.py:217
  20.7 31.8 %copy-start.16 = (bf16[40,128]{1,0:T(8,128)(2,1)}, bf16[40,128]{1,0:T(8,128)(2,1)S(1)}, u32[]{:S(2)}) copy-start(bf16[40,128]{1,0:T(8,128)(2,1)S(1)} %fusion) | copy-start | bytes 30724
  40.5 43.3 %copy-start.3 = (bf16[640,512]{1,0:T(8,128)(2,1)}, bf16[640,512]{1,0:T(8,128)(2,1)S(1)}, u32[]{:S(2)}) copy-start(bf16[640,512]{1,0:T(8,128)(2,1)S(1)} %collective-permute-done.1.g10.far_ref) | copy-start | bytes 1966084
  40.5 5.6 %collective-permute-start.3 = (bf16[640,512]{1,0:T(8,128)(2,1)S(1)}, bf16[640,512]{1,0:T(8,128)(2,1)S(1)}, u32[]{:S(2)}, u32[]{:S(2)}) collective-permute-start(bf16[640,512]{1,0:T(8,128)(2,1)S(1)} %collective-permute-done.1.g10.far_ref), channel_id=1, source_target_pairs={{0,4},{1,5},{2,6},{3,7},{4,0},{5,1},{6,2},{7,3},{8,12},{9,13},{10,... | collective-permute-start | bytes 1966088 | tf_op jit(solution)/shard_map/ppermute | solution.py:217
  41.3 11.2 %collective-permute-start.6 = (bf16[128,640]{1,0:T(8,128)(2,1)S(1)}, bf16[128,640]{1,0:T(8,128)(2,1)S(1)}, u32[]{:S(2)}, u32[]{:S(2)}) collective-permute-start(bf16[128,640]{1,0:T(8,128)(2,1)S(1)} %convolution_convert_fusion.2), channel_id=1, source_target_pairs={{0,7},{1,6},{2,5},{3,4},{4,0},{5,1},{6,2},{7,3},{8,15},{9,14},{10,... | collective-permute-start | bytes 491528 | tf_op jit(solution)/shard_map/ppermute | solution.py:217
  41.3 11.2 %collective-permute-start.7 = (bf16[40,128]{1,0:T(8,128)(2,1)S(1)}, bf16[40,128]{1,0:T(8,128)(2,1)S(1)}, u32[]{:S(2)}, u32[]{:S(2)}) collective-permute-start(bf16[40,128]{1,0:T(8,128)(2,1)S(1)} %fusion), channel_id=1, source_target_pairs={{0,1},{1,0},{2,3},{3,2},{4,5},{5,4},{6,7},{7,6},{8,9},{9,8},{10,11... | collective-permute-start | bytes 30728 | tf_op jit(solution)/shard_map/ppermute | solution.py:217
  44.4 39.5 %copy-start.9 = (bf16[512,640]{1,0:T(8,128)(2,1)}, bf16[512,640]{1,0:T(8,128)(2,1)S(1)}, u32[]{:S(2)}) copy-start(bf16[512,640]{1,0:T(8,128)(2,1)S(1)} %collective-permute-done.5.a1_ref.acts_ref) | copy-start | bytes 1966084
  46.1 37.7 %copy-start.7 = (bf16[512,640]{1,0:T(8,128)(2,1)}, bf16[512,640]{1,0:T(8,128)(2,1)S(1)}, u32[]{:S(2)}) copy-start(bf16[512,640]{1,0:T(8,128)(2,1)S(1)} %collective-permute-done.4.a0_ref.acts_ref) | copy-start | bytes 1966084
  46.1 37.7 %copy-start.11 = (bf16[640,512]{1,0:T(8,128)(2,1)}, bf16[640,512]{1,0:T(8,128)(2,1)S(1)}, u32[]{:S(2)}) copy-start(bf16[640,512]{1,0:T(8,128)(2,1)S(1)} %collective-permute-done.3.g11.far_ref) | copy-start | bytes 1966084
  52.5 33.8 %copy-start.17 = (bf16[40,128]{1,0:T(8,128)(2,1)}, bf16[40,128]{1,0:T(8,128)(2,1)S(1)}, u32[]{:S(2)}) copy-start(bf16[40,128]{1,0:T(8,128)(2,1)S(1)} %collective-permute-done.7) | copy-start | bytes 30724
  84.1 2.1 %collective-permute-start.8 = (f32[8,128]{1,0:T(8,128)S(1)}, f32[8,128]{1,0:T(8,128)S(1)}, u32[]{:S(2)}, u32[]{:S(2)}) collective-permute-start(f32[8,128]{1,0:T(8,128)S(1)} %get-tuple-element.34), channel_id=1, source_target_pairs={{0,4},{1,5},{2,6},{3,7},{4,0},{5,1},{6,2},{7,3},{8,12},{9,13},{10,... | collective-permute-start | bytes 12296 | tf_op jit(solution)/shard_map/ppermute | solution.py:217
  86.2 3.4 %collective-permute-start.9 = (f32[8,128]{1,0:T(8,128)S(1)}, f32[8,128]{1,0:T(8,128)S(1)}, u32[]{:S(2)}, u32[]{:S(2)}) collective-permute-start(f32[8,128]{1,0:T(8,128)S(1)} %add.27), channel_id=1, source_target_pairs={{0,1},{1,0},{2,3},{3,2},{4,5},{5,4},{6,7},{7,6},{8,9},{9,8},{10,11... | collective-permute-start | bytes 12296 | tf_op jit(solution)/shard_map/ppermute | solution.py:217
  86.9 31.9 %copy-start.6 = (bf16[640,512]{1,0:T(8,128)(2,1)S(1)}, bf16[640,512]{1,0:T(8,128)(2,1)}, u32[]{:S(2)}) copy-start(bf16[640,512]{1,0:T(8,128)(2,1)} %copy-done.5) | copy-start | bytes 1966084
  86.9 31.9 %copy-start.10 = (bf16[512,640]{1,0:T(8,128)(2,1)S(1)}, bf16[512,640]{1,0:T(8,128)(2,1)}, u32[]{:S(2)}) copy-start(bf16[512,640]{1,0:T(8,128)(2,1)} %copy-done.9) | copy-start | bytes 1966084
  86.9 31.9 %copy-start.12 = (bf16[640,512]{1,0:T(8,128)(2,1)S(1)}, bf16[640,512]{1,0:T(8,128)(2,1)}, u32[]{:S(2)}) copy-start(bf16[640,512]{1,0:T(8,128)(2,1)} %copy-done.11) | copy-start | bytes 1966084
  89.6 4.6 %collective-permute-start.10 = (f32[8,128]{1,0:T(8,128)S(1)}, f32[8,128]{1,0:T(8,128)S(1)}, u32[]{:S(2)}, u32[]{:S(2)}) collective-permute-start(f32[8,128]{1,0:T(8,128)S(1)} %add.28.total_ref), channel_id=1, source_target_pairs={{0,3},{1,2},{2,1},{3,0},{4,7},{5,6},{6,5},{7,4},{8,11},{9,10},{10,... | collective-permute-start | bytes 12296 | tf_op jit(solution)/shard_map/ppermute | solution.py:217
  94.4 30.6 %copy-start.2 = (bf16[640,512]{1,0:T(8,128)(2,1)S(1)}, bf16[640,512]{1,0:T(8,128)(2,1)}, u32[]{:S(2)}) copy-start(bf16[640,512]{1,0:T(8,128)(2,1)} %copy-done.1) | copy-start | bytes 1966084
  94.4 30.6 %copy-start.4 = (bf16[640,512]{1,0:T(8,128)(2,1)S(1)}, bf16[640,512]{1,0:T(8,128)(2,1)}, u32[]{:S(2)}) copy-start(bf16[640,512]{1,0:T(8,128)(2,1)} %copy-done.3) | copy-start | bytes 1966084
  94.5 30.6 %copy-start.8 = (bf16[512,640]{1,0:T(8,128)(2,1)S(1)}, bf16[512,640]{1,0:T(8,128)(2,1)}, u32[]{:S(2)}) copy-start(bf16[512,640]{1,0:T(8,128)(2,1)} %copy-done.7) | copy-start | bytes 1966084
  120.7 6.1 %collective-permute-start.11 = (f32[4,128]{1,0:T(4,128)S(1)}, f32[4,128]{1,0:T(4,128)S(1)}, u32[]{:S(2)}, u32[]{:S(2)}) collective-permute-start(f32[4,128]{1,0:T(4,128)S(1)} %shard_map.76), channel_id=1, source_target_pairs={{0,4},{1,5},{2,6},{3,7},{4,0},{5,1},{6,2},{7,3},{8,12},{9,13},{10,... | collective-permute-start | bytes 6152 | tf_op jit(solution)/shard_map/ppermute | solution.py:217
  126.9 3.4 %collective-permute-start.12 = (f32[4,128]{1,0:T(4,128)S(1)}, f32[4,128]{1,0:T(4,128)S(1)}, u32[]{:S(2)}, u32[]{:S(2)}) collective-permute-start(f32[4,128]{1,0:T(4,128)S(1)} %add.29), channel_id=1, source_target_pairs={{0,1},{1,0},{2,3},{3,2},{4,5},{5,4},{6,7},{7,6},{8,9},{9,8},{10,11... | collective-permute-start | bytes 6152 | tf_op jit(solution)/shard_map/ppermute | solution.py:217
  130.3 4.5 %collective-permute-start.13 = (f32[4,128]{1,0:T(4,128)S(1)}, f32[4,128]{1,0:T(4,128)S(1)}, u32[]{:S(2)}, u32[]{:S(2)}) collective-permute-start(f32[4,128]{1,0:T(4,128)S(1)} %add.30), channel_id=1, source_target_pairs={{0,3},{1,2},{2,1},{3,0},{4,7},{5,6},{6,5},{7,4},{8,11},{9,10},{10,... | collective-permute-start | bytes 6152 | tf_op jit(solution)/shard_map/ppermute | solution.py:217

commit v9 on v8

--- a/solution.py
+++ b/solution.py
@@ -242,12 +242,12 @@
     qg_mine = lax.dynamic_slice_in_dim(qg_own, lax.rem(ring, inner) * chunk, chunk, 0)
     g10, qa, qg_mine, both = lax.optimization_barrier((g10, qa, qg_mine, both))
     g11 = moved(g10, OTHER_CORE)
+    curvature = curvature_of(ring_size, both, g00, g01, g10, g11, a0, a1)
+    parts = lax.all_to_all(curvature, RING, 0, 0, tiled=True)
+    parts, qa, qg_mine = lax.optimization_barrier((parts, qa, qg_mine))
     qa = moved(qa, ACTS_OTHER)
     qg_far = moved(qg_mine, GRADS_PARTNER)
-    curvature = curvature_of(ring_size, both, g00, g01, g10, g11, a0, a1)
-    curvature, qa, qg_far = lax.optimization_barrier((curvature, qa, qg_far))
     qg = jnp.where(ring < inner, qg_mine, qg_far)
-    parts = lax.all_to_all(curvature, RING, 0, 0, tiled=True)
     mine, total = reduced(parts, cols)
     total = total + moved(total, OTHER_CORE)
     total = total + moved(total, GRADS_PARTNER)

time: 136 us -> 137 us (level)
  waiting for transfers between devices: 37.2 us -> 30.4 us
  starting transfers between devices: 22.1 us -> 27.7 us
  blocking collectives: 55.7 us -> 57.1 us
    ppermute x14, waiting for transfers between devices: 37.2 us -> 30.4 us  [moved(): return lax.ppermute(array, BLOCKS, pairs)]
    ppermute x14, starting transfers between devices: 22.1 us -> 27.7 us  [moved(): return lax.ppermute(array, BLOCKS, pairs)]
    all_to_all x1, blocking collectives: 24.4 us -> 26.9 us  [shards(): lax.all_to_all(mine, RING, 0, 0, tiled=True).reshape(2 * width, cols)]
  transfers between devices with their start and end apart: 14 -> 14, of which waited for: 8 -> 8; matrix products, arithmetic and copies ran while one was open for 7% -> 7% of each run, Pallas kernels for 6% -> 2%
where the time goes in v9:
time: 137 us; the launch traced here: 136 us
  blocking collectives  57.1 us (42%)
  waiting for transfers between devices  30.4 us (22%)
  starting transfers between devices  27.7 us (20%)
  Pallas kernels  10.6 us (8%)
  matrix products  8.09 us (6%)
    ppermute x14, waiting for transfers between devices, moved(): return lax.ppermute(array, BLOCKS, pairs)  30.4 us
    all_to_all x1, blocking collectives, shards(): parts = lax.all_to_all(curvature, RING, 0, 0, tiled=True)  30.1 us
    ppermute x14, starting transfers between devices, moved(): return lax.ppermute(array, BLOCKS, pairs)  27.7 us
    all_to_all x1, blocking collectives, shards(): lax.all_to_all(mine, RING, 0, 0, tiled=True).reshape(2 * width, cols)  26.9 us
    pallas_call x5, Pallas kernels, call(): pl.pallas_call(kernel, in_specs=[there] * scalars + [here] * (len(operand...  10.6 us
    dot_general x4, matrix products, dot(): lax.dot_general(a, b, (contract, ((), ())), preferred_element_type=f32)  8.09 us
  transfers between devices with their start and end apart: 14, of which 8 were waited for; matrix products, arithmetic and copies ran while one was open for 7% of the time, Pallas kernels for 2%

profile of v9, /device:TPU:1, one launch (start us, length us, event | category | flops | bytes accessed | tf_op | source)
XLA Modules:
  0.0 136.1 jit_solution(783914732579836565)
XLA Ops:
  0.0 0.0 copy-start
  0.0 3.2 %collective-permute-start = (s32[4]{0:T(128)}, s32[4]{0:T(128)S(1)}, u32[]{:S(2)}, u32[]{:S(2)}) collective-permute-start(s32[4]{0:T(128)} %param.9), channel_id=1, source_target_pairs={{0,4},{1,5},{2,6},{3,7},{4,0},{5,1},{6,2},{7,3},{8,12},{9,13},{10,... | collective-permute-start | bytes 56 | tf_op jit(solution)/shard_map/ppermute | solution.py:217
  3.2 0.0 copy-done
  3.3 3.8 %convolution_convert_fusion.1.g00.near_ref = bf16[640,512]{1,0:T(8,128)(2,1)S(1)} fusion(bf16[2560,640]{1,0:T(8,128)(2,1)S(1)} %copy-done, bf16[512,2560]{1,0:T(8,128)(2,1)} %param.8), kind=kOutput, calls=%fused_computation.1 | convolution fusion | flops 1678049280 | bytes 6553600 | tf_op jit(solution)/shard_map/dot_general | solution.py:29
  7.1 0.0 copy-start.1
  7.1 0.0 collective-permute-done
  7.1 2.0 %collective-permute-start.2 = (bf16[640,512]{1,0:T(8,128)(2,1)S(1)}, bf16[640,512]{1,0:T(8,128)(2,1)S(1)}, u32[]{:S(2)}, u32[]{:S(2)}) collective-permute-start(bf16[640,512]{1,0:T(8,128)(2,1)S(1)} %convolution_convert_fusion.1.g00.near_ref), channel_id=1, source_target_pairs={{0,4},{1,5},{2,6},{3,7},{4,0},{5,1},{6,2},{7,3},{8,12},{9,13},{10,... | collective-permute-start | bytes 1966088 | tf_op jit(solution)/shard_map/ppermute | solution.py:217
  9.1 1.3 collective-permute-start.1
  10.4 0.0 copy-done.16
  10.4 0.0 copy-done.13
  10.4 0.0 copy-done.17
  10.4 0.0 copy-start.14
  10.4 2.2 %convolution_convert_fusion = bf16[512,640]{1,0:T(8,128)(2,1)S(1)} fusion(bf16[512,2560]{1,0:T(8,128)(2,1)S(1)} %copy-done.17, bf16[2560,640]{1,0:T(8,128)(2,1)S(1)} %copy-done.13), kind=kOutput, calls=%fused_computation | convolution fusion | flops 1678049280 | bytes 6553600 | tf_op jit(solution)/shard_map/dot_general | solution.py:29
  12.6 0.0 copy-start.15
  12.6 0.0 collective-permute-done.2.g01.near_ref
  12.6 0.0 copy-start.5
  12.6 0.4 collective-permute-start.5
  13.1 6.1 %collective-permute-start.4 = (bf16[512,640]{1,0:T(8,128)(2,1)S(1)}, bf16[512,640]{1,0:T(8,128)(2,1)S(1)}, u32[]{:S(2)}, u32[]{:S(2)}) collective-permute-start(bf16[512,640]{1,0:T(8,128)(2,1)S(1)} %convolution_convert_fusion), channel_id=1, source_target_pairs={{0,0},{1,1},{2,2},{3,3},{4,7},{5,6},{6,5},{7,4},{8,8},{9,9},{10,10... | collective-permute-start | bytes 1966088 | tf_op jit(solution)/shard_map/ppermute | solution.py:217
  19.2 0.0 copy-done.14
  19.2 1.4 %fusion.1 = bf16[128,640]{0,1:T(8,128)(2,1)S(1)} fusion(bf16[128,2560]{1,0:T(8,128)(2,1)S(1)} %copy-done.14, bf16[2560,640]{1,0:T(8,128)(2,1)S(1)} %copy-done), kind=kOutput, calls=%fused_computation.8 | convolution fusion | flops 419430400 | bytes 4096000 | tf_op jit(solution)/shard_map/dot_general | solution.py:29
  20.6 0.6 fusion
  21.2 0.0 copy-done.15
  21.2 0.7 convolution_convert_fusion.2
  21.9 18.6 %collective-permute-done.1.g10.far_ref = bf16[640,512]{1,0:T(8,128)(2,1)S(1)} collective-permute-done((bf16[640,512]{1,0:T(8,128)(2,1)S(1)}, bf16[640,512]{1,0:T(8,128)(2,1)S(1)}, u32[]{:S(2)}, u32[]{:S(2)}) %collective-permute-start.1) | collective-permute-done | bytes 655392 | tf_op jit(solution)/shard_map/ppermute | solution.py:217
  40.5 0.8 collective-permute-start.3
  41.3 3.1 %collective-permute-done.5.a1_ref.acts_ref = bf16[512,640]{1,0:T(8,128)(2,1)S(1)} collective-permute-done((bf16[512,640]{1,0:T(8,128)(2,1)S(1)}, bf16[512,640]{1,0:T(8,128)(2,1)S(1)}, u32[]{:S(2)}, u32[]{:S(2)}) %collective-permute-start.5) | collective-permute-done | bytes 655392 | tf_op jit(solution)/shard_map/ppermute | solution.py:217
  44.4 1.7 %collective-permute-done.4.a0_ref.acts_ref = bf16[512,640]{1,0:T(8,128)(2,1)S(1)} collective-permute-done((bf16[512,640]{1,0:T(8,128)(2,1)S(1)}, bf16[512,640]{1,0:T(8,128)(2,1)S(1)}, u32[]{:S(2)}, u32[]{:S(2)}) %collective-permute-start.4) | collective-permute-done | bytes 655392 | tf_op jit(solution)/shard_map/ppermute | solution.py:217
  46.1 0.0 collective-permute-done.3.g11.far_ref
  46.1 0.0 copy-done.1
  46.1 0.0 copy-done.5
  46.1 0.0 copy-start.11
  46.1 6.3 %shard_map.73 = bf16[32,208,128]{2,1,0:T(8,128)(2,1)S(1)} custom-call(s32[2,4]{1,0:T(2,128)S(1)} %pad_add_fusion.lengths_ref, bf16[640,512]{1,0:T(8,128)(2,1)S(1)} %convolution_convert_fusion.1.g00.near_ref, bf16[640,512]{1,0:T(8,128)(2,1)S(1)} %collective-permute-done.2.g01.near_ref, bf16[640,512]{1,0:T(8,128)(2,1)S(1)} %collective-permute-done.1.g10.far_ref, ...), custom_call_target="tpu_custom_call" | custom-call | tf_op jit(solution)/shard_map/pallas_call | solution.py:48
  52.5 30.1 %all_to_all.10.parts_ref = bf16[32,208,128]{2,1,0:T(8,128)(2,1)S(1)} all-to-all(bf16[32,208,128]{2,1,0:T(8,128)(2,1)S(1)} %shard_map.73), channel_id=1, replica_groups=mesh['x'=4,'zl'=2,'y'=4,'c'=2,'m'=4] {'x','zl','y'}, dimensions={0} | all-to-all | bytes 3407872 | tf_op jit(solution)/shard_map/all_to_all | solution.py:246
  82.6 0.0 copy-done.3
  82.6 0.0 copy-done.9
  82.6 0.0 copy-done.7
  82.6 0.0 copy-done.11
  82.6 1.3 collective-permute-start.9
  83.9 0.3 shard_map.74
  84.2 0.0 collective-permute-start.6
  84.3 1.2 collective-permute-done.6
  85.4 1.1 collective-permute-start.7
  86.5 0.4 collective-permute-start.10
  87.0 1.8 %collective-permute-done.7 = f32[8,128]{1,0:T(8,128)S(1)} collective-permute-done((f32[8,128]{1,0:T(8,128)S(1)}, f32[8,128]{1,0:T(8,128)S(1)}, u32[]{:S(2)}, u32[]{:S(2)}) %collective-permute-start.7) | collective-permute-done | bytes 4128 | tf_op jit(solution)/shard_map/ppermute | solution.py:217
  88.8 3.2 %collective-permute-start.8 = (f32[8,128]{1,0:T(8,128)S(1)}, f32[8,128]{1,0:T(8,128)S(1)}, u32[]{:S(2)}, u32[]{:S(2)}) collective-permute-start(f32[8,128]{1,0:T(8,128)S(1)} %add.28.total_ref), channel_id=1, source_target_pairs={{0,3},{1,2},{2,1},{3,0},{4,7},{5,6},{6,5},{7,4},{8,11},{9,10},{10,... | collective-permute-start | bytes 12296 | tf_op jit(solution)/shard_map/ppermute | solution.py:217
  92.0 0.0 collective-permute-done.9
  92.0 0.7 broadcast_select_fusion.qg_ref
  92.7 0.8 collective-permute-done.8.more_ref
  93.5 0.0 collective-permute-done.10.qa_ref
  93.5 0.3 shard_map.75
  93.8 0.0 copy-start.2
  93.8 0.0 copy-start.4
  93.8 0.0 copy-start.8
  93.8 26.9 %all_to_all.11 = bf16[32,40,640]{2,1,0:T(8,128)(2,1)S(1)} all-to-all(bf16[32,40,640]{2,1,0:T(8,128)(2,1)S(1)} %shard_map.75), channel_id=1, replica_groups=mesh['x'=4,'zl'=2,'y'=4,'c'=2,'m'=4] {'x','zl','y'}, dimensions={0} | all-to-all | bytes 3276800 | tf_op jit(solution)/shard_map/all_to_all | solution.py:258
  120.8 0.0 copy-done.6
  120.8 1.8 %shard_map.76 = f32[4,128]{1,0:T(4,128)S(1)} custom-call(s32[2,4]{1,0:T(2,128)S(1)} %pad_add_fusion.lengths_ref, bf16[1280,640]{1,0:T(8,128)(2,1)S(1)} %bitcast.14, bf16[640,512]{1,0:T(8,128)(2,1)S(1)} %copy-done.6, bf16[640,512]{1,0:T(8,128)(2,1)S(1)} %copy-done.12, bf16[512,640]{1,0:T(8,128)(2,1)S(1)} %copy-done.10), custom_call_target="tpu_custom_call" | custom-call | tf_op jit(solution)/shard_map/pallas_call | solution.py:48
  122.6 3.0 %collective-permute-start.11 = (f32[4,128]{1,0:T(4,128)S(1)}, f32[4,128]{1,0:T(4,128)S(1)}, u32[]{:S(2)}, u32[]{:S(2)}) collective-permute-start(f32[4,128]{1,0:T(4,128)S(1)} %shard_map.76), channel_id=1, source_target_pairs={{0,4},{1,5},{2,6},{3,7},{4,0},{5,1},{6,2},{7,3},{8,12},{9,13},{10,... | collective-permute-start | bytes 6152 | tf_op jit(solution)/shard_map/ppermute | solution.py:217
  125.6 1.9 %shard_map.77 = f32[4,128]{1,0:T(4,128)S(1)} custom-call(s32[2,4]{1,0:T(2,128)S(1)} %pad_add_fusion.lengths_ref, bf16[1280,640]{1,0:T(8,128)(2,1)S(1)} %bitcast.15, bf16[640,512]{1,0:T(8,128)(2,1)S(1)} %copy-done.2, bf16[640,512]{1,0:T(8,128)(2,1)S(1)} %copy-done.4, bf16[512,640]{1,0:T(8,128)(2,1)S(1)} %copy-done.8), custom_call_target="tpu_custom_call" | custom-call | tf_op jit(solution)/shard_map/pallas_call | solution.py:48
  127.5 0.0 collective-permute-done.11
  127.5 1.6 %collective-permute-start.12 = (f32[4,128]{1,0:T(4,128)S(1)}, f32[4,128]{1,0:T(4,128)S(1)}, u32[]{:S(2)}, u32[]{:S(2)}) collective-permute-start(f32[4,128]{1,0:T(4,128)S(1)} %add.29), channel_id=1, source_target_pairs={{0,1},{1,0},{2,3},{3,2},{4,5},{5,4},{6,7},{7,6},{8,9},{9,8},{10,11... | collective-permute-start | bytes 6152 | tf_op jit(solution)/shard_map/ppermute | solution.py:217
  129.1 1.9 %collective-permute-done.12 = f32[4,128]{1,0:T(4,128)S(1)} collective-permute-done((f32[4,128]{1,0:T(4,128)S(1)}, f32[4,128]{1,0:T(4,128)S(1)}, u32[]{:S(2)}, u32[]{:S(2)}) %collective-permute-start.12) | collective-permute-done | bytes 2080 | tf_op jit(solution)/shard_map/ppermute | solution.py:217
  130.9 3.1 %collective-permute-start.13 = (f32[4,128]{1,0:T(4,128)S(1)}, f32[4,128]{1,0:T(4,128)S(1)}, u32[]{:S(2)}, u32[]{:S(2)}) collective-permute-start(f32[4,128]{1,0:T(4,128)S(1)} %add.30), channel_id=1, source_target_pairs={{0,3},{1,2},{2,1},{3,0},{4,7},{5,6},{6,5},{7,4},{8,11},{9,10},{10,... | collective-permute-start | bytes 6152 | tf_op jit(solution)/shard_map/ppermute | solution.py:217
  134.1 1.4 %collective-permute-done.13 = f32[4,128]{1,0:T(4,128)S(1)} collective-permute-done((f32[4,128]{1,0:T(4,128)S(1)}, f32[4,128]{1,0:T(4,128)S(1)}, u32[]{:S(2)}, u32[]{:S(2)}) %collective-permute-start.13) | collective-permute-done | bytes 2080 | tf_op jit(solution)/shard_map/ppermute | solution.py:217
  135.5 0.6 slice_reduce_fusion
  (20 shorter events, 0.0 us)
Async XLA Ops:
  0.0 3.2 %copy-start = (bf16[2560,640]{1,0:T(8,128)(2,1)S(1)}, bf16[2560,640]{1,0:T(8,128)(2,1)}, u32[]{:S(2)}) copy-start(bf16[2560,640]{1,0:T(8,128)(2,1)} %param.13) | copy-start | bytes 9830404
  0.0 7.1 %collective-permute-start = (s32[4]{0:T(128)}, s32[4]{0:T(128)S(1)}, u32[]{:S(2)}, u32[]{:S(2)}) collective-permute-start(s32[4]{0:T(128)} %param.9), channel_id=1, source_target_pairs={{0,4},{1,5},{2,6},{3,7},{4,0},{5,1},{6,2},{7,3},{8,12},{9,13},{10,... | collective-permute-start | bytes 56 | tf_op jit(solution)/shard_map/ppermute | solution.py:217
  3.2 7.1 %copy-start.16 = (s32[4]{0:T(128)S(1)}, s32[4]{0:T(128)}, u32[]{:S(2)}) copy-start(s32[4]{0:T(128)} %param.9) | copy-start | bytes 52
  3.2 7.1 %copy-start.13 = (bf16[2560,640]{1,0:T(8,128)(2,1)S(1)}, bf16[2560,640]{1,0:T(8,128)(2,1)}, u32[]{:S(2)}) copy-start(bf16[2560,640]{1,0:T(8,128)(2,1)} %param.12) | copy-start | bytes 9830404
  3.3 7.1 %copy-start.17 = (bf16[512,2560]{1,0:T(8,128)(2,1)S(1)}, bf16[512,2560]{1,0:T(8,128)(2,1)}, u32[]{:S(2)}) copy-start(bf16[512,2560]{1,0:T(8,128)(2,1)} %param.7) | copy-start | bytes 7864324
  7.1 39.0 %copy-start.1 = (bf16[640,512]{1,0:T(8,128)(2,1)}, bf16[640,512]{1,0:T(8,128)(2,1)S(1)}, u32[]{:S(2)}) copy-start(bf16[640,512]{1,0:T(8,128)(2,1)S(1)} %convolution_convert_fusion.1.g00.near_ref) | copy-start | bytes 1966084
  7.1 5.5 %collective-permute-start.2 = (bf16[640,512]{1,0:T(8,128)(2,1)S(1)}, bf16[640,512]{1,0:T(8,128)(2,1)S(1)}, u32[]{:S(2)}, u32[]{:S(2)}) collective-permute-start(bf16[640,512]{1,0:T(8,128)(2,1)S(1)} %convolution_convert_fusion.1.g00.near_ref), channel_id=1, source_target_pairs={{0,4},{1,5},{2,6},{3,7},{4,0},{5,1},{6,2},{7,3},{8,12},{9,13},{10,... | collective-permute-start | bytes 1966088 | tf_op jit(solution)/shard_map/ppermute | solution.py:217
  9.1 31.4 %collective-permute-start.1 = (bf16[640,512]{1,0:T(8,128)(2,1)S(1)}, bf16[640,512]{1,0:T(8,128)(2,1)S(1)}, u32[]{:S(2)}, u32[]{:S(2)}) collective-permute-start(bf16[640,512]{1,0:T(8,128)(2,1)S(1)} %convolution_convert_fusion.1.g00.near_ref), channel_id=1, source_target_pairs={{0,1},{1,0},{2,3},{3,2},{4,5},{5,4},{6,7},{7,6},{8,9},{9,8},{10,11... | collective-permute-start | bytes 1966088 | tf_op jit(solution)/shard_map/ppermute | solution.py:217
  10.4 8.8 %copy-start.14 = (bf16[128,2560]{1,0:T(8,128)(2,1)S(1)}, bf16[128,2560]{1,0:T(8,128)(2,1)}, u32[]{:S(2)}) copy-start(bf16[128,2560]{1,0:T(8,128)(2,1)} %param.11) | copy-start | bytes 1966084
  12.6 8.6 %copy-start.15 = (bf16[128,2560]{1,0:T(8,128)(2,1)S(1)}, bf16[128,2560]{1,0:T(8,128)(2,1)}, u32[]{:S(2)}) copy-start(bf16[128,2560]{1,0:T(8,128)(2,1)} %param.10) | copy-start | bytes 1966084
  12.6 33.5 %copy-start.5 = (bf16[640,512]{1,0:T(8,128)(2,1)}, bf16[640,512]{1,0:T(8,128)(2,1)S(1)}, u32[]{:S(2)}) copy-start(bf16[640,512]{1,0:T(8,128)(2,1)S(1)} %collective-permute-done.2.g01.near_ref) | copy-start | bytes 1966084
  12.6 31.7 %collective-permute-start.5 = (bf16[512,640]{1,0:T(8,128)(2,1)S(1)}, bf16[512,640]{1,0:T(8,128)(2,1)S(1)}, u32[]{:S(2)}, u32[]{:S(2)}) collective-permute-start(bf16[512,640]{1,0:T(8,128)(2,1)S(1)} %convolution_convert_fusion), channel_id=1, source_target_pairs={{0,7},{1,6},{2,5},{3,4},{4,0},{5,1},{6,2},{7,3},{8,15},{9,14},{10,... | collective-permute-start | bytes 1966088 | tf_op jit(solution)/shard_map/ppermute | solution.py:217
  13.1 33.0 %collective-permute-start.4 = (bf16[512,640]{1,0:T(8,128)(2,1)S(1)}, bf16[512,640]{1,0:T(8,128)(2,1)S(1)}, u32[]{:S(2)}, u32[]{:S(2)}) collective-permute-start(bf16[512,640]{1,0:T(8,128)(2,1)S(1)} %convolution_convert_fusion), channel_id=1, source_target_pairs={{0,0},{1,1},{2,2},{3,3},{4,7},{5,6},{6,5},{7,4},{8,8},{9,9},{10,10... | collective-permute-start | bytes 1966088 | tf_op jit(solution)/shard_map/ppermute | solution.py:217
  40.5 42.1 %copy-start.3 = (bf16[640,512]{1,0:T(8,128)(2,1)}, bf16[640,512]{1,0:T(8,128)(2,1)S(1)}, u32[]{:S(2)}) copy-start(bf16[640,512]{1,0:T(8,128)(2,1)S(1)} %collective-permute-done.1.g10.far_ref) | copy-start | bytes 1966084
  40.5 5.6 %collective-permute-start.3 = (bf16[640,512]{1,0:T(8,128)(2,1)S(1)}, bf16[640,512]{1,0:T(8,128)(2,1)S(1)}, u32[]{:S(2)}, u32[]{:S(2)}) collective-permute-start(bf16[640,512]{1,0:T(8,128)(2,1)S(1)} %collective-permute-done.1.g10.far_ref), channel_id=1, source_target_pairs={{0,4},{1,5},{2,6},{3,7},{4,0},{5,1},{6,2},{7,3},{8,12},{9,13},{10,... | collective-permute-start | bytes 1966088 | tf_op jit(solution)/shard_map/ppermute | solution.py:217
  44.4 38.2 %copy-start.9 = (bf16[512,640]{1,0:T(8,128)(2,1)}, bf16[512,640]{1,0:T(8,128)(2,1)S(1)}, u32[]{:S(2)}) copy-start(bf16[512,640]{1,0:T(8,128)(2,1)S(1)} %collective-permute-done.5.a1_ref.acts_ref) | copy-start | bytes 1966084
  46.1 36.5 %copy-start.7 = (bf16[512,640]{1,0:T(8,128)(2,1)}, bf16[512,640]{1,0:T(8,128)(2,1)S(1)}, u32[]{:S(2)}) copy-start(bf16[512,640]{1,0:T(8,128)(2,1)S(1)} %collective-permute-done.4.a0_ref.acts_ref) | copy-start | bytes 1966084
  46.1 36.5 %copy-start.11 = (bf16[640,512]{1,0:T(8,128)(2,1)}, bf16[640,512]{1,0:T(8,128)(2,1)S(1)}, u32[]{:S(2)}) copy-start(bf16[640,512]{1,0:T(8,128)(2,1)S(1)} %collective-permute-done.3.g11.far_ref) | copy-start | bytes 1966084
  82.6 9.4 %collective-permute-start.9 = (bf16[40,128]{1,0:T(8,128)(2,1)}, bf16[40,128]{1,0:T(8,128)(2,1)}, u32[]{:S(2)}, u32[]{:S(2)}) collective-permute-start(bf16[40,128]{1,0:T(8,128)(2,1)} %fusion), channel_id=1, source_target_pairs={{0,1},{1,0},{2,3},{3,2},{4,5},{5,4},{6,7},{7,6},{8,9},{9,8},{10,11... | collective-permute-start | bytes 30728 | tf_op jit(solution)/shard_map/ppermute | solution.py:217
  84.2 1.2 collective-permute-start.6
  85.4 3.4 %collective-permute-start.7 = (f32[8,128]{1,0:T(8,128)S(1)}, f32[8,128]{1,0:T(8,128)S(1)}, u32[]{:S(2)}, u32[]{:S(2)}) collective-permute-start(f32[8,128]{1,0:T(8,128)S(1)} %add.27), channel_id=1, source_target_pairs={{0,1},{1,0},{2,3},{3,2},{4,5},{5,4},{6,7},{7,6},{8,9},{9,8},{10,11... | collective-permute-start | bytes 12296 | tf_op jit(solution)/shard_map/ppermute | solution.py:217
  86.5 34.2 %copy-start.6 = (bf16[640,512]{1,0:T(8,128)(2,1)S(1)}, bf16[640,512]{1,0:T(8,128)(2,1)}, u32[]{:S(2)}) copy-start(bf16[640,512]{1,0:T(8,128)(2,1)} %copy-done.5) | copy-start | bytes 1966084
  86.5 34.2 %copy-start.10 = (bf16[512,640]{1,0:T(8,128)(2,1)S(1)}, bf16[512,640]{1,0:T(8,128)(2,1)}, u32[]{:S(2)}) copy-start(bf16[512,640]{1,0:T(8,128)(2,1)} %copy-done.9) | copy-start | bytes 1966084
  86.5 34.2 %copy-start.12 = (bf16[640,512]{1,0:T(8,128)(2,1)S(1)}, bf16[640,512]{1,0:T(8,128)(2,1)}, u32[]{:S(2)}) copy-start(bf16[640,512]{1,0:T(8,128)(2,1)} %copy-done.11) | copy-start | bytes 1966084
  86.5 7.0 %collective-permute-start.10 = (bf16[128,640]{1,0:T(8,128)(2,1)S(1)}, bf16[128,640]{1,0:T(8,128)(2,1)S(1)}, u32[]{:S(2)}, u32[]{:S(2)}) collective-permute-start(bf16[128,640]{1,0:T(8,128)(2,1)S(1)} %convolution_convert_fusion.2), channel_id=1, source_target_pairs={{0,7},{1,6},{2,5},{3,4},{4,0},{5,1},{6,2},{7,3},{8,15},{9,14},{10,... | collective-permute-start | bytes 491528 | tf_op jit(solution)/shard_map/ppermute | solution.py:217
  88.8 4.7 %collective-permute-start.8 = (f32[8,128]{1,0:T(8,128)S(1)}, f32[8,128]{1,0:T(8,128)S(1)}, u32[]{:S(2)}, u32[]{:S(2)}) collective-permute-start(f32[8,128]{1,0:T(8,128)S(1)} %add.28.total_ref), channel_id=1, source_target_pairs={{0,3},{1,2},{2,1},{3,0},{4,7},{5,6},{6,5},{7,4},{8,11},{9,10},{10,... | collective-permute-start | bytes 12296 | tf_op jit(solution)/shard_map/ppermute | solution.py:217
  93.8 31.8 %copy-start.2 = (bf16[640,512]{1,0:T(8,128)(2,1)S(1)}, bf16[640,512]{1,0:T(8,128)(2,1)}, u32[]{:S(2)}) copy-start(bf16[640,512]{1,0:T(8,128)(2,1)} %copy-done.1) | copy-start | bytes 1966084
  93.8 31.8 %copy-start.4 = (bf16[640,512]{1,0:T(8,128)(2,1)S(1)}, bf16[640,512]{1,0:T(8,128)(2,1)}, u32[]{:S(2)}) copy-start(bf16[640,512]{1,0:T(8,128)(2,1)} %copy-done.3) | copy-start | bytes 1966084
  93.8 31.8 %copy-start.8 = (bf16[512,640]{1,0:T(8,128)(2,1)S(1)}, bf16[512,640]{1,0:T(8,128)(2,1)}, u32[]{:S(2)}) copy-start(bf16[512,640]{1,0:T(8,128)(2,1)} %copy-done.7) | copy-start | bytes 1966084
  122.6 4.8 %collective-permute-start.11 = (f32[4,128]{1,0:T(4,128)S(1)}, f32[4,128]{1,0:T(4,128)S(1)}, u32[]{:S(2)}, u32[]{:S(2)}) collective-permute-start(f32[4,128]{1,0:T(4,128)S(1)} %shard_map.76), channel_id=1, source_target_pairs={{0,4},{1,5},{2,6},{3,7},{4,0},{5,1},{6,2},{7,3},{8,12},{9,13},{10,... | collective-permute-start | bytes 6152 | tf_op jit(solution)/shard_map/ppermute | solution.py:217
  127.5 3.4 %collective-permute-start.12 = (f32[4,128]{1,0:T(4,128)S(1)}, f32[4,128]{1,0:T(4,128)S(1)}, u32[]{:S(2)}, u32[]{:S(2)}) collective-permute-start(f32[4,128]{1,0:T(4,128)S(1)} %add.29), channel_id=1, source_target_pairs={{0,1},{1,0},{2,3},{3,2},{4,5},{5,4},{6,7},{7,6},{8,9},{9,8},{10,11... | collective-permute-start | bytes 6152 | tf_op jit(solution)/shard_map/ppermute | solution.py:217
  130.9 4.5 %collective-permute-start.13 = (f32[4,128]{1,0:T(4,128)S(1)}, f32[4,128]{1,0:T(4,128)S(1)}, u32[]{:S(2)}, u32[]{:S(2)}) collective-permute-start(f32[4,128]{1,0:T(4,128)S(1)} %add.30), channel_id=1, source_target_pairs={{0,3},{1,2},{2,1},{3,0},{4,7},{5,6},{6,5},{7,4},{8,11},{9,10},{10,... | collective-permute-start | bytes 6152 | tf_op jit(solution)/shard_map/ppermute | solution.py:217

commit v10 on v8

--- a/solution.py
+++ b/solution.py
@@ -190,15 +190,18 @@
     for member, grads in enumerate((near_ref, far_ref)):
         product = dot(p_ref[member * width : (member + 1) * width, :], acts_ref[...], ((1,), (1,)))
         sums = sums + jnp.sum(grads[...].astype(f32) * product, axis=0, keepdims=True)
+    place = lax.broadcasted_iota(jnp.int32, out_ref.shape, 1)
+    found = jnp.zeros(out_ref.shape, f32)
     for j, (start, finish) in enumerate(bounds_of(lengths_ref, which)):
         inside = (lane >= start) & (lane < finish)
         value = jnp.sum(jnp.where(inside, sums, 0.0), axis=1, keepdims=True)
-        out_ref[j : j + 1, :] = jnp.broadcast_to(value, (1, out_ref.shape[1]))
+        found = jnp.where(place == j, value, found)
+    out_ref[...] = found
 
 
 def scores_of(which, lengths, precond, near, far, acts):
     return local_call(
-        functools.partial(score_kernel, which), [jax.ShapeDtypeStruct((lengths.shape[1], LANES), f32)]
+        functools.partial(score_kernel, which), [jax.ShapeDtypeStruct((1, LANES), f32)]
     )(lengths, precond, near, far, acts)[0]
 
 
@@ -260,7 +263,7 @@
     found = found + scores_of(0, both, precond, g00, g10, a0)
     found = found + moved(found, GRADS_PARTNER)
     found = found + moved(found, ACTS_PARTNER)
-    return found[:, 0].reshape(1, count)
+    return found[:, 0:count]
 
 
 def solution(mesh):

time: 136 us -> 136 us (level)
  no operation moved by 1% of the time
where the time goes in v10:
time: 136 us; the launch traced here: 135 us
  blocking collectives  55.8 us (41%)
  waiting for transfers between devices  37.1 us (27%)
  starting transfers between devices  22.1 us (16%)
  Pallas kernels  10.5 us (8%)
  matrix products  8.1 us (6%)
    ppermute x14, waiting for transfers between devices, moved(): return lax.ppermute(array, BLOCKS, pairs)  37.1 us
    all_to_all x1, blocking collectives, shards(): parts = lax.all_to_all(curvature, RING, 0, 0, tiled=True)  31.4 us
    all_to_all x1, blocking collectives, shards(): lax.all_to_all(mine, RING, 0, 0, tiled=True).reshape(2 * width, cols)  24.4 us
    ppermute x14, starting transfers between devices, moved(): return lax.ppermute(array, BLOCKS, pairs)  22.1 us
    pallas_call x5, Pallas kernels, call(): pl.pallas_call(kernel, in_specs=[there] * scalars + [here] * (len(operand...  10.5 us
    dot_general x4, matrix products, dot(): lax.dot_general(a, b, (contract, ((), ())), preferred_element_type=f32)  8.1 us
  transfers between devices with their start and end apart: 14, of which 8 were waited for; matrix products, arithmetic and copies ran while one was open for 7% of the time, Pallas kernels for 6%

profile of v10, /device:TPU:1, one launch (start us, length us, event | category | flops | bytes accessed | tf_op | source)
XLA Modules:
  0.0 135.3 jit_solution(6956180229585379807)
XLA Ops:
  0.0 0.0 copy-start
  0.0 3.2 %collective-permute-start = (s32[4]{0:T(128)}, s32[4]{0:T(128)S(1)}, u32[]{:S(2)}, u32[]{:S(2)}) collective-permute-start(s32[4]{0:T(128)} %param.9), channel_id=1, source_target_pairs={{0,4},{1,5},{2,6},{3,7},{4,0},{5,1},{6,2},{7,3},{8,12},{9,13},{10,... | collective-permute-start | bytes 56 | tf_op jit(solution)/shard_map/ppermute | solution.py:220
  3.2 0.0 copy-done
  3.3 3.8 %convolution_convert_fusion.1.g00.near_ref = bf16[640,512]{1,0:T(8,128)(2,1)S(1)} fusion(bf16[2560,640]{1,0:T(8,128)(2,1)S(1)} %copy-done, bf16[512,2560]{1,0:T(8,128)(2,1)} %param.8), kind=kOutput, calls=%fused_computation.1 | convolution fusion | flops 1678049280 | bytes 6553600 | tf_op jit(solution)/shard_map/dot_general | solution.py:29
  7.1 0.0 copy-start.1
  7.1 0.0 collective-permute-done
  7.1 2.0 %collective-permute-start.2 = (bf16[640,512]{1,0:T(8,128)(2,1)S(1)}, bf16[640,512]{1,0:T(8,128)(2,1)S(1)}, u32[]{:S(2)}, u32[]{:S(2)}) collective-permute-start(bf16[640,512]{1,0:T(8,128)(2,1)S(1)} %convolution_convert_fusion.1.g00.near_ref), channel_id=1, source_target_pairs={{0,4},{1,5},{2,6},{3,7},{4,0},{5,1},{6,2},{7,3},{8,12},{9,13},{10,... | collective-permute-start | bytes 1966088 | tf_op jit(solution)/shard_map/ppermute | solution.py:220
  9.1 1.3 collective-permute-start.1
  10.4 0.0 copy-done.18
  10.4 0.0 copy-done.13
  10.4 0.0 copy-done.19
  10.4 0.0 copy-start.14
  10.4 2.2 %convolution_convert_fusion = bf16[512,640]{1,0:T(8,128)(2,1)S(1)} fusion(bf16[512,2560]{1,0:T(8,128)(2,1)S(1)} %copy-done.19, bf16[2560,640]{1,0:T(8,128)(2,1)S(1)} %copy-done.13), kind=kOutput, calls=%fused_computation | convolution fusion | flops 1678049280 | bytes 6553600 | tf_op jit(solution)/shard_map/dot_general | solution.py:29
  12.6 0.0 copy-start.15
  12.6 0.0 collective-permute-done.2.g01.near_ref
  12.6 0.0 copy-start.5
  12.6 0.4 collective-permute-start.5
  13.1 6.1 %collective-permute-start.4 = (bf16[512,640]{1,0:T(8,128)(2,1)S(1)}, bf16[512,640]{1,0:T(8,128)(2,1)S(1)}, u32[]{:S(2)}, u32[]{:S(2)}) collective-permute-start(bf16[512,640]{1,0:T(8,128)(2,1)S(1)} %convolution_convert_fusion), channel_id=1, source_target_pairs={{0,0},{1,1},{2,2},{3,3},{4,7},{5,6},{6,5},{7,4},{8,8},{9,9},{10,10... | collective-permute-start | bytes 1966088 | tf_op jit(solution)/shard_map/ppermute | solution.py:220
  19.2 0.0 copy-done.14
  19.2 1.4 %fusion.1 = bf16[128,640]{0,1:T(8,128)(2,1)S(1)} fusion(bf16[128,2560]{1,0:T(8,128)(2,1)S(1)} %copy-done.14, bf16[2560,640]{1,0:T(8,128)(2,1)S(1)} %copy-done), kind=kOutput, calls=%fused_computation.7 | convolution fusion | flops 419430400 | bytes 4096000 | tf_op jit(solution)/shard_map/dot_general | solution.py:29
  20.6 0.0 copy-done.15
  20.7 0.0 copy-start.16
  20.7 0.7 convolution_convert_fusion.2
  21.4 19.2 %collective-permute-done.1.g10.far_ref = bf16[640,512]{1,0:T(8,128)(2,1)S(1)} collective-permute-done((bf16[640,512]{1,0:T(8,128)(2,1)S(1)}, bf16[640,512]{1,0:T(8,128)(2,1)S(1)}, u32[]{:S(2)}, u32[]{:S(2)}) %collective-permute-start.1) | collective-permute-done | bytes 655392 | tf_op jit(solution)/shard_map/ppermute | solution.py:220
  40.5 0.8 collective-permute-start.3
  41.3 0.0 collective-permute-start.6
  41.3 0.0 collective-permute-start.7
  41.3 3.1 %collective-permute-done.5.a1_ref.acts_ref = bf16[512,640]{1,0:T(8,128)(2,1)S(1)} collective-permute-done((bf16[512,640]{1,0:T(8,128)(2,1)S(1)}, bf16[512,640]{1,0:T(8,128)(2,1)S(1)}, u32[]{:S(2)}, u32[]{:S(2)}) %collective-permute-start.5) | collective-permute-done | bytes 655392 | tf_op jit(solution)/shard_map/ppermute | solution.py:220
  44.4 1.7 %collective-permute-done.4.a0_ref.acts_ref = bf16[512,640]{1,0:T(8,128)(2,1)S(1)} collective-permute-done((bf16[512,640]{1,0:T(8,128)(2,1)S(1)}, bf16[512,640]{1,0:T(8,128)(2,1)S(1)}, u32[]{:S(2)}, u32[]{:S(2)}) %collective-permute-start.4) | collective-permute-done | bytes 655392 | tf_op jit(solution)/shard_map/ppermute | solution.py:220
  46.1 0.0 collective-permute-done.3.g11.far_ref
  46.1 0.0 copy-done.1
  46.1 0.0 copy-done.5
  46.1 0.0 copy-start.11
  46.1 6.2 %shard_map.73 = bf16[32,208,128]{2,1,0:T(8,128)(2,1)S(1)} custom-call(s32[2,4]{1,0:T(2,128)S(1)} %pad_add_fusion.lengths_ref, bf16[640,512]{1,0:T(8,128)(2,1)S(1)} %convolution_convert_fusion.1.g00.near_ref, bf16[640,512]{1,0:T(8,128)(2,1)S(1)} %collective-permute-done.2.g01.near_ref, bf16[640,512]{1,0:T(8,128)(2,1)S(1)} %collective-permute-done.1.g10.far_ref, ...), custom_call_target="tpu_custom_call" | custom-call | tf_op jit(solution)/shard_map/pallas_call | solution.py:48
  52.4 0.0 copy-done.16
  52.4 0.0 collective-permute-done.7
  52.4 0.0 copy-start.17
  52.4 0.0 collective-permute-done.6.qa_ref
  52.4 31.4 %all_to_all.10.parts_ref = bf16[32,208,128]{2,1,0:T(8,128)(2,1)S(1)} all-to-all(bf16[32,208,128]{2,1,0:T(8,128)(2,1)S(1)} %shard_map.73), channel_id=1, replica_groups=mesh['x'=4,'zl'=2,'y'=4,'c'=2,'m'=4] {'x','zl','y'}, dimensions={0} | all-to-all | bytes 3407872 | tf_op jit(solution)/shard_map/all_to_all | solution.py:253
  83.8 0.0 copy-done.3
  83.8 0.0 copy-done.9
  83.8 0.0 copy-done.7
  83.8 0.0 copy-done.11
  83.8 0.3 shard_map.74
  84.1 1.3 collective-permute-start.8
  85.4 0.8 collective-permute-done.8
  86.2 0.0 copy-done.17
  86.2 0.7 collective-permute-start.9
  86.9 2.6 %collective-permute-done.9 = f32[8,128]{1,0:T(8,128)S(1)} collective-permute-done((f32[8,128]{1,0:T(8,128)S(1)}, f32[8,128]{1,0:T(8,128)S(1)}, u32[]{:S(2)}, u32[]{:S(2)}) %collective-permute-start.9) | collective-permute-done | bytes 4128 | tf_op jit(solution)/shard_map/ppermute | solution.py:220
  89.6 1.1 collective-permute-start.10
  90.7 0.7 broadcast_select_fusion.qg_ref
  91.4 2.7 %collective-permute-done.10.more_ref = f32[8,128]{1,0:T(8,128)S(1)} collective-permute-done((f32[8,128]{1,0:T(8,128)S(1)}, f32[8,128]{1,0:T(8,128)S(1)}, u32[]{:S(2)}, u32[]{:S(2)}) %collective-permute-start.10) | collective-permute-done | bytes 4128 | tf_op jit(solution)/shard_map/ppermute | solution.py:220
  94.2 0.3 shard_map.75
  94.4 0.0 copy-start.2
  94.5 24.4 %all_to_all.11 = bf16[32,40,640]{2,1,0:T(8,128)(2,1)S(1)} all-to-all(bf16[32,40,640]{2,1,0:T(8,128)(2,1)S(1)} %shard_map.75), channel_id=1, replica_groups=mesh['x'=4,'zl'=2,'y'=4,'c'=2,'m'=4] {'x','zl','y'}, dimensions={0} | all-to-all | bytes 3276800 | tf_op jit(solution)/shard_map/all_to_all | solution.py:261
  118.9 1.9 %shard_map.76 = f32[1,128]{1,0:T(1,128)S(1)} custom-call(s32[2,4]{1,0:T(2,128)S(1)} %pad_add_fusion.lengths_ref, bf16[1280,640]{1,0:T(8,128)(2,1)S(1)} %bitcast.14, bf16[640,512]{1,0:T(8,128)(2,1)S(1)} %copy-done.6, bf16[640,512]{1,0:T(8,128)(2,1)S(1)} %copy-done.12, bf16[512,640]{1,0:T(8,128)(2,1)S(1)} %copy-done.10), custom_call_target="tpu_custom_call" | custom-call | tf_op jit(solution)/shard_map/pallas_call | solution.py:48
  120.7 4.3 %collective-permute-start.11 = (f32[1,128]{1,0:T(1,128)S(1)}, f32[1,128]{1,0:T(1,128)S(1)}, u32[]{:S(2)}, u32[]{:S(2)}) collective-permute-start(f32[1,128]{1,0:T(1,128)S(1)} %shard_map.76), channel_id=1, source_target_pairs={{0,4},{1,5},{2,6},{3,7},{4,0},{5,1},{6,2},{7,3},{8,12},{9,13},{10,... | collective-permute-start | bytes 1544 | tf_op jit(solution)/shard_map/ppermute | solution.py:220
  125.0 1.9 %shard_map.77 = f32[1,128]{1,0:T(1,128)S(1)} custom-call(s32[2,4]{1,0:T(2,128)S(1)} %pad_add_fusion.lengths_ref, bf16[1280,640]{1,0:T(8,128)(2,1)S(1)} %bitcast.15, bf16[640,512]{1,0:T(8,128)(2,1)S(1)} %copy-done.2, bf16[640,512]{1,0:T(8,128)(2,1)S(1)} %copy-done.4, bf16[512,640]{1,0:T(8,128)(2,1)S(1)} %copy-done.8), custom_call_target="tpu_custom_call" | custom-call | tf_op jit(solution)/shard_map/pallas_call | solution.py:48
  126.9 0.0 collective-permute-done.11
  126.9 0.3 collective-permute-start.12
  127.2 3.1 %collective-permute-done.12 = f32[1,128]{1,0:T(1,128)S(1)} collective-permute-done((f32[1,128]{1,0:T(1,128)S(1)}, f32[1,128]{1,0:T(1,128)S(1)}, u32[]{:S(2)}, u32[]{:S(2)}) %collective-permute-start.12) | collective-permute-done | bytes 544 | tf_op jit(solution)/shard_map/ppermute | solution.py:220
  130.3 0.6 collective-permute-start.13
  130.9 3.9 %collective-permute-done.13 = f32[1,128]{1,0:T(1,128)S(1)} collective-permute-done((f32[1,128]{1,0:T(1,128)S(1)}, f32[1,128]{1,0:T(1,128)S(1)}, u32[]{:S(2)}, u32[]{:S(2)}) %collective-permute-start.13) | collective-permute-done | bytes 544 | tf_op jit(solution)/shard_map/ppermute | solution.py:220
  134.8 0.5 add.31
  (23 shorter events, 0.1 us)
Async XLA Ops:
  0.0 3.2 %copy-start = (bf16[2560,640]{1,0:T(8,128)(2,1)S(1)}, bf16[2560,640]{1,0:T(8,128)(2,1)}, u32[]{:S(2)}) copy-start(bf16[2560,640]{1,0:T(8,128)(2,1)} %param.13) | copy-start | bytes 9830404
  0.0 7.1 %collective-permute-start = (s32[4]{0:T(128)}, s32[4]{0:T(128)S(1)}, u32[]{:S(2)}, u32[]{:S(2)}) collective-permute-start(s32[4]{0:T(128)} %param.9), channel_id=1, source_target_pairs={{0,4},{1,5},{2,6},{3,7},{4,0},{5,1},{6,2},{7,3},{8,12},{9,13},{10,... | collective-permute-start | bytes 56 | tf_op jit(solution)/shard_map/ppermute | solution.py:220
  3.2 7.1 %copy-start.18 = (s32[4]{0:T(128)S(1)}, s32[4]{0:T(128)}, u32[]{:S(2)}) copy-start(s32[4]{0:T(128)} %param.9) | copy-start | bytes 52
  3.2 7.1 %copy-start.13 = (bf16[2560,640]{1,0:T(8,128)(2,1)S(1)}, bf16[2560,640]{1,0:T(8,128)(2,1)}, u32[]{:S(2)}) copy-start(bf16[2560,640]{1,0:T(8,128)(2,1)} %param.12) | copy-start | bytes 9830404
  3.3 7.1 %copy-start.19 = (bf16[512,2560]{1,0:T(8,128)(2,1)S(1)}, bf16[512,2560]{1,0:T(8,128)(2,1)}, u32[]{:S(2)}) copy-start(bf16[512,2560]{1,0:T(8,128)(2,1)} %param.7) | copy-start | bytes 7864324
  7.1 39.0 %copy-start.1 = (bf16[640,512]{1,0:T(8,128)(2,1)}, bf16[640,512]{1,0:T(8,128)(2,1)S(1)}, u32[]{:S(2)}) copy-start(bf16[640,512]{1,0:T(8,128)(2,1)S(1)} %convolution_convert_fusion.1.g00.near_ref) | copy-start | bytes 1966084
  7.1 5.5 %collective-permute-start.2 = (bf16[640,512]{1,0:T(8,128)(2,1)S(1)}, bf16[640,512]{1,0:T(8,128)(2,1)S(1)}, u32[]{:S(2)}, u32[]{:S(2)}) collective-permute-start(bf16[640,512]{1,0:T(8,128)(2,1)S(1)} %convolution_convert_fusion.1.g00.near_ref), channel_id=1, source_target_pairs={{0,4},{1,5},{2,6},{3,7},{4,0},{5,1},{6,2},{7,3},{8,12},{9,13},{10,... | collective-permute-start | bytes 1966088 | tf_op jit(solution)/shard_map/ppermute | solution.py:220
  9.1 31.4 %collective-permute-start.1 = (bf16[640,512]{1,0:T(8,128)(2,1)S(1)}, bf16[640,512]{1,0:T(8,128)(2,1)S(1)}, u32[]{:S(2)}, u32[]{:S(2)}) collective-permute-start(bf16[640,512]{1,0:T(8,128)(2,1)S(1)} %convolution_convert_fusion.1.g00.near_ref), channel_id=1, source_target_pairs={{0,1},{1,0},{2,3},{3,2},{4,5},{5,4},{6,7},{7,6},{8,9},{9,8},{10,11... | collective-permute-start | bytes 1966088 | tf_op jit(solution)/shard_map/ppermute | solution.py:220
  10.4 8.8 %copy-start.14 = (bf16[128,2560]{1,0:T(8,128)(2,1)S(1)}, bf16[128,2560]{1,0:T(8,128)(2,1)}, u32[]{:S(2)}) copy-start(bf16[128,2560]{1,0:T(8,128)(2,1)} %param.11) | copy-start | bytes 1966084
  12.6 8.0 %copy-start.15 = (bf16[128,2560]{1,0:T(8,128)(2,1)S(1)}, bf16[128,2560]{1,0:T(8,128)(2,1)}, u32[]{:S(2)}) copy-start(bf16[128,2560]{1,0:T(8,128)(2,1)} %param.10) | copy-start | bytes 1966084
  12.6 33.5 %copy-start.5 = (bf16[640,512]{1,0:T(8,128)(2,1)}, bf16[640,512]{1,0:T(8,128)(2,1)S(1)}, u32[]{:S(2)}) copy-start(bf16[640,512]{1,0:T(8,128)(2,1)S(1)} %collective-permute-done.2.g01.near_ref) | copy-start | bytes 1966084
  12.6 31.7 %collective-permute-start.5 = (bf16[512,640]{1,0:T(8,128)(2,1)S(1)}, bf16[512,640]{1,0:T(8,128)(2,1)S(1)}, u32[]{:S(2)}, u32[]{:S(2)}) collective-permute-start(bf16[512,640]{1,0:T(8,128)(2,1)S(1)} %convolution_convert_fusion), channel_id=1, source_target_pairs={{0,7},{1,6},{2,5},{3,4},{4,0},{5,1},{6,2},{7,3},{8,15},{9,14},{10,... | collective-permute-start | bytes 1966088 | tf_op jit(solution)/shard_map/ppermute | solution.py:220
  13.1 33.0 %collective-permute-start.4 = (bf16[512,640]{1,0:T(8,128)(2,1)S(1)}, bf16[512,640]{1,0:T(8,128)(2,1)S(1)}, u32[]{:S(2)}, u32[]{:S(2)}) collective-permute-start(bf16[512,640]{1,0:T(8,128)(2,1)S(1)} %convolution_convert_fusion), channel_id=1, source_target_pairs={{0,0},{1,1},{2,2},{3,3},{4,7},{5,6},{6,5},{7,4},{8,8},{9,9},{10,10... | collective-permute-start | bytes 1966088 | tf_op jit(solution)/shard_map/ppermute | solution.py:220
  20.7 31.7 %copy-start.16 = (bf16[40,128]{1,0:T(8,128)(2,1)}, bf16[40,128]{1,0:T(8,128)(2,1)S(1)}, u32[]{:S(2)}) copy-start(bf16[40,128]{1,0:T(8,128)(2,1)S(1)} %fusion) | copy-start | bytes 30724
  40.5 43.3 %copy-start.3 = (bf16[640,512]{1,0:T(8,128)(2,1)}, bf16[640,512]{1,0:T(8,128)(2,1)S(1)}, u32[]{:S(2)}) copy-start(bf16[640,512]{1,0:T(8,128)(2,1)S(1)} %collective-permute-done.1.g10.far_ref) | copy-start | bytes 1966084
  40.5 5.6 %collective-permute-start.3 = (bf16[640,512]{1,0:T(8,128)(2,1)S(1)}, bf16[640,512]{1,0:T(8,128)(2,1)S(1)}, u32[]{:S(2)}, u32[]{:S(2)}) collective-permute-start(bf16[640,512]{1,0:T(8,128)(2,1)S(1)} %collective-permute-done.1.g10.far_ref), channel_id=1, source_target_pairs={{0,4},{1,5},{2,6},{3,7},{4,0},{5,1},{6,2},{7,3},{8,12},{9,13},{10,... | collective-permute-start | bytes 1966088 | tf_op jit(solution)/shard_map/ppermute | solution.py:220
  41.3 11.1 %collective-permute-start.6 = (bf16[128,640]{1,0:T(8,128)(2,1)S(1)}, bf16[128,640]{1,0:T(8,128)(2,1)S(1)}, u32[]{:S(2)}, u32[]{:S(2)}) collective-permute-start(bf16[128,640]{1,0:T(8,128)(2,1)S(1)} %convolution_convert_fusion.2), channel_id=1, source_target_pairs={{0,7},{1,6},{2,5},{3,4},{4,0},{5,1},{6,2},{7,3},{8,15},{9,14},{10,... | collective-permute-start | bytes 491528 | tf_op jit(solution)/shard_map/ppermute | solution.py:220
  41.3 11.1 %collective-permute-start.7 = (bf16[40,128]{1,0:T(8,128)(2,1)S(1)}, bf16[40,128]{1,0:T(8,128)(2,1)S(1)}, u32[]{:S(2)}, u32[]{:S(2)}) collective-permute-start(bf16[40,128]{1,0:T(8,128)(2,1)S(1)} %fusion), channel_id=1, source_target_pairs={{0,1},{1,0},{2,3},{3,2},{4,5},{5,4},{6,7},{7,6},{8,9},{9,8},{10,11... | collective-permute-start | bytes 30728 | tf_op jit(solution)/shard_map/ppermute | solution.py:220
  44.4 39.5 %copy-start.9 = (bf16[512,640]{1,0:T(8,128)(2,1)}, bf16[512,640]{1,0:T(8,128)(2,1)S(1)}, u32[]{:S(2)}) copy-start(bf16[512,640]{1,0:T(8,128)(2,1)S(1)} %collective-permute-done.5.a1_ref.acts_ref) | copy-start | bytes 1966084
  46.1 37.7 %copy-start.7 = (bf16[512,640]{1,0:T(8,128)(2,1)}, bf16[512,640]{1,0:T(8,128)(2,1)S(1)}, u32[]{:S(2)}) copy-start(bf16[512,640]{1,0:T(8,128)(2,1)S(1)} %collective-permute-done.4.a0_ref.acts_ref) | copy-start | bytes 1966084
  46.1 37.7 %copy-start.11 = (bf16[640,512]{1,0:T(8,128)(2,1)}, bf16[640,512]{1,0:T(8,128)(2,1)S(1)}, u32[]{:S(2)}) copy-start(bf16[640,512]{1,0:T(8,128)(2,1)S(1)} %collective-permute-done.3.g11.far_ref) | copy-start | bytes 1966084
  52.4 33.9 %copy-start.17 = (bf16[40,128]{1,0:T(8,128)(2,1)}, bf16[40,128]{1,0:T(8,128)(2,1)S(1)}, u32[]{:S(2)}) copy-start(bf16[40,128]{1,0:T(8,128)(2,1)S(1)} %collective-permute-done.7) | copy-start | bytes 30724
  84.1 2.1 %collective-permute-start.8 = (f32[8,128]{1,0:T(8,128)S(1)}, f32[8,128]{1,0:T(8,128)S(1)}, u32[]{:S(2)}, u32[]{:S(2)}) collective-permute-start(f32[8,128]{1,0:T(8,128)S(1)} %get-tuple-element.34), channel_id=1, source_target_pairs={{0,4},{1,5},{2,6},{3,7},{4,0},{5,1},{6,2},{7,3},{8,12},{9,13},{10,... | collective-permute-start | bytes 12296 | tf_op jit(solution)/shard_map/ppermute | solution.py:220
  86.2 3.4 %collective-permute-start.9 = (f32[8,128]{1,0:T(8,128)S(1)}, f32[8,128]{1,0:T(8,128)S(1)}, u32[]{:S(2)}, u32[]{:S(2)}) collective-permute-start(f32[8,128]{1,0:T(8,128)S(1)} %add.27), channel_id=1, source_target_pairs={{0,1},{1,0},{2,3},{3,2},{4,5},{5,4},{6,7},{7,6},{8,9},{9,8},{10,11... | collective-permute-start | bytes 12296 | tf_op jit(solution)/shard_map/ppermute | solution.py:220
  86.9 31.9 %copy-start.6 = (bf16[640,512]{1,0:T(8,128)(2,1)S(1)}, bf16[640,512]{1,0:T(8,128)(2,1)}, u32[]{:S(2)}) copy-start(bf16[640,512]{1,0:T(8,128)(2,1)} %copy-done.5) | copy-start | bytes 1966084
  86.9 31.9 %copy-start.10 = (bf16[512,640]{1,0:T(8,128)(2,1)S(1)}, bf16[512,640]{1,0:T(8,128)(2,1)}, u32[]{:S(2)}) copy-start(bf16[512,640]{1,0:T(8,128)(2,1)} %copy-done.9) | copy-start | bytes 1966084
  86.9 31.9 %copy-start.12 = (bf16[640,512]{1,0:T(8,128)(2,1)S(1)}, bf16[640,512]{1,0:T(8,128)(2,1)}, u32[]{:S(2)}) copy-start(bf16[640,512]{1,0:T(8,128)(2,1)} %copy-done.11) | copy-start | bytes 1966084
  89.6 4.6 %collective-permute-start.10 = (f32[8,128]{1,0:T(8,128)S(1)}, f32[8,128]{1,0:T(8,128)S(1)}, u32[]{:S(2)}, u32[]{:S(2)}) collective-permute-start(f32[8,128]{1,0:T(8,128)S(1)} %add.28.total_ref), channel_id=1, source_target_pairs={{0,3},{1,2},{2,1},{3,0},{4,7},{5,6},{6,5},{7,4},{8,11},{9,10},{10,... | collective-permute-start | bytes 12296 | tf_op jit(solution)/shard_map/ppermute | solution.py:220
  94.4 30.6 %copy-start.2 = (bf16[640,512]{1,0:T(8,128)(2,1)S(1)}, bf16[640,512]{1,0:T(8,128)(2,1)}, u32[]{:S(2)}) copy-start(bf16[640,512]{1,0:T(8,128)(2,1)} %copy-done.1) | copy-start | bytes 1966084
  94.4 30.6 %copy-start.4 = (bf16[640,512]{1,0:T(8,128)(2,1)S(1)}, bf16[640,512]{1,0:T(8,128)(2,1)}, u32[]{:S(2)}) copy-start(bf16[640,512]{1,0:T(8,128)(2,1)} %copy-done.3) | copy-start | bytes 1966084
  94.5 30.6 %copy-start.8 = (bf16[512,640]{1,0:T(8,128)(2,1)S(1)}, bf16[512,640]{1,0:T(8,128)(2,1)}, u32[]{:S(2)}) copy-start(bf16[512,640]{1,0:T(8,128)(2,1)} %copy-done.7) | copy-start | bytes 1966084
  120.7 6.1 %collective-permute-start.11 = (f32[1,128]{1,0:T(1,128)S(1)}, f32[1,128]{1,0:T(1,128)S(1)}, u32[]{:S(2)}, u32[]{:S(2)}) collective-permute-start(f32[1,128]{1,0:T(1,128)S(1)} %shard_map.76), channel_id=1, source_target_pairs={{0,4},{1,5},{2,6},{3,7},{4,0},{5,1},{6,2},{7,3},{8,12},{9,13},{10,... | collective-permute-start | bytes 1544 | tf_op jit(solution)/shard_map/ppermute | solution.py:220
  126.9 3.4 %collective-permute-start.12 = (f32[1,128]{1,0:T(1,128)S(1)}, f32[1,128]{1,0:T(1,128)S(1)}, u32[]{:S(2)}, u32[]{:S(2)}) collective-permute-start(f32[1,128]{1,0:T(1,128)S(1)} %add.29), channel_id=1, source_target_pairs={{0,1},{1,0},{2,3},{3,2},{4,5},{5,4},{6,7},{7,6},{8,9},{9,8},{10,11... | collective-permute-start | bytes 1544 | tf_op jit(solution)/shard_map/ppermute | solution.py:220
  130.3 4.5 %collective-permute-start.13 = (f32[1,128]{1,0:T(1,128)S(1)}, f32[1,128]{1,0:T(1,128)S(1)}, u32[]{:S(2)}, u32[]{:S(2)}) collective-permute-start(f32[1,128]{1,0:T(1,128)S(1)} %add.30), channel_id=1, source_target_pairs={{0,3},{1,2},{2,1},{3,0},{4,7},{5,6},{6,5},{7,4},{8,11},{9,10},{10,... | collective-permute-start | bytes 1544 | tf_op jit(solution)/shard_map/ppermute | solution.py:220
